TPU v7x, 32 devices: a whole 2x2x4 slice. The times are simulated.
32 devices in a mesh: seq: 8 (over z, y), head: 4 (over x, core).
Axes of the slice: x: 2, y: 2, z: 4, core: 2. Of those that a mesh axis runs over, the one named last changes fastest.
Arguments:
- queries: bfloat16 [4096, 4096], P(('seq', 'head')), may hold values from -100 to 100
- keys_in: bfloat16 [4096, 4096], P(('seq', 'head')), may hold values from -16 to 16
- values_in: bfloat16 [4096, 4096], P(('seq', 'head')), may hold values from -16 to 16
- grad_out: bfloat16 [4096, 4096], P(('seq', 'head')), may hold values from -6 to 6
Outputs:
- attended: bfloat16 [4096, 4096], P(('seq', 'head'))
- grad_queries: bfloat16 [4096, 4096], P(('seq', 'head'))
- grad_keys: bfloat16 [4096, 4096], P(('seq', 'head'))
- grad_values: bfloat16 [4096, 4096], P(('seq', 'head'))
All inputs are finite; a program needn't handle non-finite values.
Results may differ from a plain program's by a relative error of at most 0.0052.
Values may be sent and summed in bfloat16 or wider, within the bound.
No kernel may reach another device: no remote copies, remote signals or barrier semaphores. Data moves between devices by JAX's collectives and lax.ppermute only.
A program may use at most 64 MiB of HBM per device.

v0:
```python
import jax
import jax.numpy as jnp
from jax import lax
from jax.sharding import PartitionSpec as P

HD = 128
CROWS = 16


def swapped(block, axis, apart):
    count = lax.axis_size(axis)
    route = []
    for low in range(count):
        high = low | 1 << apart
        if high != low and high < count:
            route += [(low, high), (high, low)]
    return lax.ppermute(block, axis, route)


def on_device(queries, keys_in, values_in, grad_out):
    seq_count = lax.axis_size("seq")
    depth = seq_count.bit_length() - 1
    scale_q = HD ** (-0.5)
    query_here, key_here, value_here, grad_here = (
        lax.all_to_all(queries, "head", split_axis=1, concat_axis=0, tiled=True),
        lax.all_to_all(keys_in, "head", split_axis=1, concat_axis=0, tiled=True),
        lax.all_to_all(values_in, "head", split_axis=1, concat_axis=0, tiled=True),
        lax.all_to_all(grad_out, "head", split_axis=1, concat_axis=0, tiled=True),
    )
    rows_here = query_here.shape[0]
    head_count = query_here.shape[1] // HD
    pool_size = rows_here // CROWS
    query_three = query_here.reshape(rows_here, head_count, HD)
    key_three = key_here.reshape(rows_here, head_count, HD)
    value_three = value_here.reshape(rows_here, head_count, HD)
    grad_three = grad_here.reshape(rows_here, head_count, HD)
    pooled_k = jnp.mean(
        key_three.astype(jnp.float32).reshape(CROWS, pool_size, head_count, HD), axis=1
    ).transpose(1, 0, 2)
    pooled_v = jnp.mean(
        value_three.astype(jnp.float32).reshape(CROWS, pool_size, head_count, HD), axis=1
    ).transpose(1, 0, 2)
    own_pooled = jnp.stack([pooled_k, pooled_v], axis=0)
    siblings = []
    mean_now = own_pooled
    for level in range(depth):
        received = swapped(mean_now, "seq", level)
        siblings.append(received)
        mean_now = 0.5 * (mean_now + received)
    coarse = (
        jnp.stack(siblings, axis=2).reshape(2, head_count, depth * CROWS, HD).astype(jnp.bfloat16)
    )
    log_counts = jnp.repeat(
        jnp.log(float(pool_size) * 2.0 ** jnp.arange(depth, dtype=jnp.float32)), CROWS
    )
    offsets = jnp.concatenate([jnp.zeros((rows_here,), jnp.float32), log_counts])
    keys_full = jnp.concatenate([key_three.transpose(1, 0, 2), coarse[0]], axis=1)
    values_full = jnp.concatenate([value_three.transpose(1, 0, 2), coarse[1]], axis=1)
    scores = (
        jnp.einsum("shd,htd->hst", query_three, keys_full, preferred_element_type=jnp.float32)
        * scale_q
        + offsets
    )
    probs = jax.nn.softmax(scores, axis=-1)
    probs_low = probs.astype(jnp.bfloat16)
    attended = jnp.einsum(
        "hst,htd->shd", probs_low, values_full, preferred_element_type=jnp.float32
    ).astype(jnp.bfloat16)
    dprob = jnp.einsum("shd,htd->hst", grad_three, values_full, preferred_element_type=jnp.float32)
    dscore = (scale_q * probs * (dprob - jnp.sum(probs * dprob, axis=-1, keepdims=True))).astype(
        jnp.bfloat16
    )
    grad_query = jnp.einsum(
        "hst,htd->shd", dscore, keys_full, preferred_element_type=jnp.float32
    ).astype(jnp.bfloat16)
    dkeys = jnp.einsum("hst,shd->htd", dscore, query_three, preferred_element_type=jnp.float32)
    dvalues = jnp.einsum("hst,shd->htd", probs_low, grad_three, preferred_element_type=jnp.float32)
    coarse_grad = jnp.stack([dkeys[:, rows_here:], dvalues[:, rows_here:]], axis=0).reshape(
        2, head_count, depth, CROWS, HD
    )
    grad_above = jnp.zeros((2, head_count, CROWS, HD), jnp.float32)
    for level in reversed(range(depth)):
        outgoing = coarse_grad[:, :, level] + 0.5 * grad_above
        grad_above = 0.5 * grad_above + swapped(outgoing, "seq", level)
    spread = jnp.broadcast_to(
        (grad_above / float(pool_size))[:, :, :, None, :], (2, head_count, CROWS, pool_size, HD)
    )
    spread = spread.reshape(2, head_count, rows_here, HD)
    grad_key = (dkeys[:, :rows_here] + spread[0]).transpose(1, 0, 2).astype(jnp.bfloat16)
    grad_value = (dvalues[:, :rows_here] + spread[1]).transpose(1, 0, 2).astype(jnp.bfloat16)
    width_here = head_count * HD
    return (
        lax.all_to_all(
            attended.reshape(rows_here, width_here), "head", split_axis=0, concat_axis=1, tiled=True
        ),
        lax.all_to_all(
            grad_query.reshape(rows_here, width_here),
            "head",
            split_axis=0,
            concat_axis=1,
            tiled=True,
        ),
        lax.all_to_all(
            grad_key.reshape(rows_here, width_here), "head", split_axis=0, concat_axis=1, tiled=True
        ),
        lax.all_to_all(
            grad_value.reshape(rows_here, width_here),
            "head",
            split_axis=0,
            concat_axis=1,
            tiled=True,
        ),
    )


def solution(mesh):
    placed = (
        P(("seq", "head"), None),
        P(("seq", "head"), None),
        P(("seq", "head"), None),
        P(("seq", "head"), None),
    )
    return jax.shard_map(
        on_device,
        mesh=mesh,
        in_specs=placed,
        out_specs=(
            P(("seq", "head"), None),
            P(("seq", "head"), None),
            P(("seq", "head"), None),
            P(("seq", "head"), None),
        ),
        check_vma=False,
    )
```

profile of v0, /device:TPU:1, one launch (start us, length us, event | category | flops | bytes accessed | tf_op | source)
XLA Modules:
  0.0 195.5 jit_solution(10389261349473130361)
XLA Ops:
  3.0 4.3 %all-to-all-start = ((bf16[128,4,1024]{2,0,1:T(8,128)(2,1)}), bf16[128,4,1024]{2,0,1:T(8,128)(2,1)S(1)}, u32[]{:S(2)}, u32[]{:S(2)}) async-start(bf16[128,4,1024]{2,0,1:T(8,128)(2,1)} %bitcast.126), calls=%async_computation | async-start | bytes 2097152 | tf_op jit(solution)/shard_map/all_to_all | solution.py:27
  8.3 12.3 %all-to-all-done = bf16[128,4,1024]{2,0,1:T(8,128)(2,1)S(1)} async-done(((bf16[128,4,1024]{2,0,1:T(8,128)(2,1)}), bf16[128,4,1024]{2,0,1:T(8,128)(2,1)S(1)}, u32[]{:S(2)}, u32[]{:S(2)}) %all-to-all-start) | async-done | bytes 1048608 | tf_op jit(solution)/shard_map/all_to_all | solution.py:27
  20.6 4.6 %all-to-all-start.1 = ((bf16[128,4,1024]{2,0,1:T(8,128)(2,1)}), bf16[128,4,1024]{2,0,1:T(8,128)(2,1)S(1)}, u32[]{:S(2)}, u32[]{:S(2)}) async-start(bf16[128,4,1024]{2,0,1:T(8,128)(2,1)} %bitcast.125), calls=%async_computation.1 | async-start | bytes 2097152 | tf_op jit(solution)/shard_map/all_to_all | solution.py:26
  27.9 10.9 %all-to-all-done.1 = bf16[128,4,1024]{2,0,1:T(8,128)(2,1)S(1)} async-done(((bf16[128,4,1024]{2,0,1:T(8,128)(2,1)}), bf16[128,4,1024]{2,0,1:T(8,128)(2,1)S(1)}, u32[]{:S(2)}, u32[]{:S(2)}) %all-to-all-start.1) | async-done | bytes 1048608 | tf_op jit(solution)/shard_map/all_to_all | solution.py:26
  38.8 4.4 %all-to-all-start.2 = ((bf16[128,4,1024]{2,0,1:T(8,128)(2,1)}), bf16[128,4,1024]{2,0,1:T(8,128)(2,1)S(1)}, u32[]{:S(2)}, u32[]{:S(2)}) async-start(bf16[128,4,1024]{2,0,1:T(8,128)(2,1)} %bitcast.146), calls=%async_computation.2 | async-start | bytes 2097152 | tf_op jit(solution)/shard_map/all_to_all | solution.py:25
  44.9 11.9 %all-to-all-done.2 = bf16[128,4,1024]{2,0,1:T(8,128)(2,1)S(1)} async-done(((bf16[128,4,1024]{2,0,1:T(8,128)(2,1)}), bf16[128,4,1024]{2,0,1:T(8,128)(2,1)S(1)}, u32[]{:S(2)}, u32[]{:S(2)}) %all-to-all-start.2) | async-done | bytes 1048608 | tf_op jit(solution)/shard_map/all_to_all | solution.py:25
  56.8 5.1 %all-to-all-start.4 = ((bf16[128,4,1024]{2,0,1:T(8,128)(2,1)}), bf16[128,4,1024]{2,0,1:T(8,128)(2,1)}, u32[]{:S(2)}, u32[]{:S(2)}) async-start(bf16[128,4,1024]{2,0,1:T(8,128)(2,1)} %bitcast.123), calls=%async_computation.4 | async-start | bytes 2097152 | tf_op jit(solution)/shard_map/all_to_all | solution.py:28
  63.9 3.9 %collective-permute-done = f32[2,8,16,128]{3,1,2,0:T(8,128)S(1)} collective-permute-done((f32[2,8,16,128]{3,1,2,0:T(8,128)S(1)}, f32[2,8,16,128]{3,1,2,0:T(8,128)S(1)}, u32[]{:S(2)}, u32[]{:S(2)}) %collective-permute-start) | collective-permute-done | bytes 131104 | tf_op jit(solution)/shard_map/ppermute | solution.py:17
  72.0 3.6 %all-to-all-done.4 = bf16[128,4,1024]{2,0,1:T(8,128)(2,1)} async-done(((bf16[128,4,1024]{2,0,1:T(8,128)(2,1)}), bf16[128,4,1024]{2,0,1:T(8,128)(2,1)}, u32[]{:S(2)}, u32[]{:S(2)}) %all-to-all-start.4) | async-done | bytes 1048608 | tf_op jit(solution)/shard_map/all_to_all | solution.py:28
  78.1 3.1 %collective-permute-start.2 = (bf16[2,8,16,128]{3,1,2,0:T(8,128)(2,1)S(1)}, bf16[2,8,16,128]{3,1,2,0:T(8,128)(2,1)S(1)}, u32[]{:S(2)}, u32[]{:S(2)}) collective-permute-start(bf16[2,8,16,128]{3,1,2,0:T(8,128)(2,1)S(1)} %add_multiply_fusion.2), channel_id=1, source_target_pairs={{0,16},{16,0},{4,20},{20,4},{8,24},{24,8},{12,28},{28,12},{1,17},{... | collective-permute-start | bytes 196616 | tf_op jit(solution)/shard_map/ppermute | solution.py:17
  83.0 5.4 %fusion.48 = (f32[8,512]{1,0:T(8,128)S(1)}, f32[8,512,560]{1,2,0:T(8,128)}) fusion(f32[560]{0:T(1024)S(1)} %concatenate.12, bf16[512,8,128]{2,1,0:T(8,128)(2,1)S(1)} %bitcast.139, bf16[8,48,128]{2,1,0:T(8,128)(2,1)S(1)} %bitcast.162, bf16[8,512,128]{2,1,0:T(8,128)(2,1)S(1)} %bitcast.137), kind=kOutput, calls=%fused_computation.75 | convolution fusion | flops 598671936 | bytes 11389120 | tf_op jit(solution)/shard_map/sub | solution.py:64
  88.4 4.8 %fusion.19 = bf16[512,8,128]{0,2,1:T(8,128)(2,1)S(1)} fusion(bf16[8,48,128]{2,1,0:T(8,128)(2,1)S(1)} %bitcast.164, bf16[8,512,128]{2,1,0:T(8,128)(2,1)S(1)} %bitcast.157, f32[8,512,560]{1,2,0:T(8,128)} %get-tuple-element.19, f32[8,512]{1,0:T(8,128)S(1)} %get-tuple-element.18), kind=kOutput, calls=%fused_computation.26 | convolution fusion | flops 594608128 | bytes 11386880 | tf_op jit(solution)/shard_map/hst,htd->shd/dot_general | solution.py:66
  94.8 4.4 %fusion.1 = (f32[8,512]{1,0:T(8,128)S(1)}, f32[8,560,512]{2,1,0:T(8,128)}) fusion(f32[8,512,560]{1,2,0:T(8,128)S(1)} %copy-done.1, f32[8,512]{1,0:T(8,128)S(1)} %get-tuple-element.18, bf16[512,8,128]{2,1,0:T(8,128)(2,1)S(1)} %bitcast.159, bf16[8,48,128]{2,1,0:T(8,128)(2,1)S(1)} %bitcast.165, bf16[8,512,128]{2,1,0:T(8,128)(2,1)S(1)} %bitcast.158), kind=kOutput, calls=%fused_computation.3 | convolution fusion | flops 596373504 | bytes 20578304 | tf_op jit(solution)/shard_map/shd,htd->hst/dot_general | solution.py:69
  103.4 6.7 %all-to-all-start.3 = ((bf16[4,128,1024]{1,2,0:T(8,128)(2,1)}), bf16[4,128,1024]{1,2,0:T(8,128)(2,1)}, u32[]{:S(2)}, u32[]{:S(2)}) async-start(bf16[4,128,1024]{1,2,0:T(8,128)(2,1)} %copy.62), calls=%async_computation.3 | async-start | bytes 2097152 | tf_op jit(solution)/shard_map/all_to_all | solution.py:93
  110.1 10.9 %fusion.3 = bf16[8,512,560]{1,2,0:T(8,128)(2,1)} fusion(f32[8,560,512]{2,1,0:T(8,128)} %get-tuple-element.21, f32[8,512]{1,0:T(8,128)S(1)} %get-tuple-element.20, f32[8,512,560]{1,2,0:T(8,128)} %get-tuple-element.19, f32[8,512]{1,0:T(8,128)S(1)} %get-tuple-element.18), kind=kLoop, calls=%fused_computation.5 | loop fusion | flops 11468800 | bytes 22970368 | tf_op jit(solution)/shard_map/convert_element_type | solution.py:70
  121.0 4.1 %fusion.31 = f32[8,560,128]{2,1,0:T(8,128)S(1)} fusion(bf16[8,512,560]{1,2,0:T(8,128)(2,1)} %fusion.3, bf16[512,8,128]{2,1,0:T(8,128)(2,1)} %bitcast.140), kind=kOutput, calls=%fused_computation.43 | convolution fusion | flops 587202560 | bytes 7929856 | tf_op jit(solution)/shard_map/hst,shd->htd/dot_general | solution.py:76
  127.4 6.5 %collective-permute-done.3 = f32[2,8,16,128]{3,1,2,0:T(8,128)S(1)} collective-permute-done((f32[2,8,16,128]{3,1,2,0:T(8,128)S(1)}, f32[2,8,16,128]{3,1,2,0:T(8,128)S(1)}, u32[]{:S(2)}, u32[]{:S(2)}) %collective-permute-start.3) | collective-permute-done | bytes 131104 | tf_op jit(solution)/shard_map/ppermute | solution.py:17
  139.8 4.2 %all-to-all-start.5 = ((bf16[4,128,1024]{1,2,0:T(8,128)(2,1)}), bf16[4,128,1024]{1,2,0:T(8,128)(2,1)S(1)}, u32[]{:S(2)}, u32[]{:S(2)}) async-start(bf16[4,128,1024]{1,2,0:T(8,128)(2,1)} %copy.65), calls=%async_computation.5 | async-start | bytes 2097152 | tf_op jit(solution)/shard_map/all_to_all | solution.py:96
  146.4 3.8 %collective-permute-done.5 = f32[2,8,16,128]{3,1,2,0:T(8,128)S(1)} collective-permute-done((f32[2,8,16,128]{3,1,2,0:T(8,128)S(1)}, f32[2,8,16,128]{3,1,2,0:T(8,128)S(1)}, u32[]{:S(2)}, u32[]{:S(2)}) %collective-permute-start.5) | collective-permute-done | bytes 131104 | tf_op jit(solution)/shard_map/ppermute | solution.py:17
  153.3 4.3 %all-to-all-done.5 = bf16[4,128,1024]{1,2,0:T(8,128)(2,1)S(1)} async-done(((bf16[4,128,1024]{1,2,0:T(8,128)(2,1)}), bf16[4,128,1024]{1,2,0:T(8,128)(2,1)S(1)}, u32[]{:S(2)}, u32[]{:S(2)}) %all-to-all-start.5) | async-done | bytes 1048608 | tf_op jit(solution)/shard_map/all_to_all | solution.py:96
  157.7 4.4 %all-to-all-start.6 = ((bf16[4,128,1024]{2,1,0:T(8,128)(2,1)}), bf16[4,128,1024]{2,1,0:T(8,128)(2,1)S(1)}, u32[]{:S(2)}, u32[]{:S(2)}) async-start(bf16[4,128,1024]{2,1,0:T(8,128)(2,1)} %all_to_all.124), calls=%async_computation.6 | async-start | bytes 2097152 | tf_op jit(solution)/shard_map/all_to_all | solution.py:103
  165.8 9.8 %all-to-all-done.6 = bf16[4,128,1024]{2,1,0:T(8,128)(2,1)S(1)} async-done(((bf16[4,128,1024]{2,1,0:T(8,128)(2,1)}), bf16[4,128,1024]{2,1,0:T(8,128)(2,1)S(1)}, u32[]{:S(2)}, u32[]{:S(2)}) %all-to-all-start.6) | async-done | bytes 1048608 | tf_op jit(solution)/shard_map/all_to_all | solution.py:103
  175.6 4.4 %all-to-all-start.7 = ((bf16[4,128,1024]{2,1,0:T(8,128)(2,1)}), bf16[4,128,1024]{2,1,0:T(8,128)(2,1)S(1)}, u32[]{:S(2)}, u32[]{:S(2)}) async-start(bf16[4,128,1024]{2,1,0:T(8,128)(2,1)} %all_to_all.128), calls=%async_computation.7 | async-start | bytes 2097152 | tf_op jit(solution)/shard_map/all_to_all | solution.py:106
  185.5 8.1 %all-to-all-done.7 = bf16[4,128,1024]{2,1,0:T(8,128)(2,1)S(1)} async-done(((bf16[4,128,1024]{2,1,0:T(8,128)(2,1)}), bf16[4,128,1024]{2,1,0:T(8,128)(2,1)S(1)}, u32[]{:S(2)}, u32[]{:S(2)}) %all-to-all-start.7) | async-done | bytes 1048608 | tf_op jit(solution)/shard_map/all_to_all | solution.py:106
  (94 shorter events, 48.7 us)
Async XLA Ops:
  0.6 6.6 %copy-start.5 = (bf16[128,4096]{1,0:T(8,128)(2,1)S(1)}, bf16[128,4096]{1,0:T(8,128)(2,1)}, u32[]{:S(2)}) copy-start(bf16[128,4096]{1,0:T(8,128)(2,1)} %param.5) | copy-start | bytes 3145732
  3.0 17.6 %all-to-all-start = ((bf16[128,4,1024]{2,0,1:T(8,128)(2,1)}), bf16[128,4,1024]{2,0,1:T(8,128)(2,1)S(1)}, u32[]{:S(2)}, u32[]{:S(2)}) async-start(bf16[128,4,1024]{2,0,1:T(8,128)(2,1)} %bitcast.126), calls=%async_computation | async-start | bytes 2097152 | tf_op jit(solution)/shard_map/all_to_all | solution.py:27
  7.3 18.0 %copy-start.6 = (bf16[128,4096]{1,0:T(8,128)(2,1)S(1)}, bf16[128,4096]{1,0:T(8,128)(2,1)}, u32[]{:S(2)}) copy-start(bf16[128,4096]{1,0:T(8,128)(2,1)} %param.4) | copy-start | bytes 3145732
  20.6 18.2 %all-to-all-start.1 = ((bf16[128,4,1024]{2,0,1:T(8,128)(2,1)}), bf16[128,4,1024]{2,0,1:T(8,128)(2,1)S(1)}, u32[]{:S(2)}, u32[]{:S(2)}) async-start(bf16[128,4,1024]{2,0,1:T(8,128)(2,1)} %bitcast.125), calls=%async_computation.1 | async-start | bytes 2097152 | tf_op jit(solution)/shard_map/all_to_all | solution.py:26
  38.8 18.0 %all-to-all-start.2 = ((bf16[128,4,1024]{2,0,1:T(8,128)(2,1)}), bf16[128,4,1024]{2,0,1:T(8,128)(2,1)S(1)}, u32[]{:S(2)}, u32[]{:S(2)}) async-start(bf16[128,4,1024]{2,0,1:T(8,128)(2,1)} %bitcast.146), calls=%async_computation.2 | async-start | bytes 2097152 | tf_op jit(solution)/shard_map/all_to_all | solution.py:25
  56.8 12.9 %copy-start.3 = (bf16[128,4,1024]{2,0,1:T(8,128)(2,1)}, bf16[128,4,1024]{2,0,1:T(8,128)(2,1)S(1)}, u32[]{:S(2)}) copy-start(bf16[128,4,1024]{2,0,1:T(8,128)(2,1)S(1)} %all-to-all-done.2) | copy-start | bytes 3145732
  56.8 18.8 %all-to-all-start.4 = ((bf16[128,4,1024]{2,0,1:T(8,128)(2,1)}), bf16[128,4,1024]{2,0,1:T(8,128)(2,1)}, u32[]{:S(2)}, u32[]{:S(2)}) async-start(bf16[128,4,1024]{2,0,1:T(8,128)(2,1)} %bitcast.123), calls=%async_computation.4 | async-start | bytes 2097152 | tf_op jit(solution)/shard_map/all_to_all | solution.py:28
  61.9 6.0 %collective-permute-start = (f32[2,8,16,128]{3,1,2,0:T(8,128)S(1)}, f32[2,8,16,128]{3,1,2,0:T(8,128)S(1)}, u32[]{:S(2)}, u32[]{:S(2)}) collective-permute-start(f32[2,8,16,128]{3,1,2,0:T(8,128)S(1)} %pad_maximum_fusion.10), channel_id=1, source_target_pairs={{0,4},{4,0},{8,12},{12,8},{16,20},{20,16},{24,28},{28,24},{1,5},{5... | collective-permute-start | bytes 393224 | tf_op jit(solution)/shard_map/ppermute | solution.py:17
  67.9 10.2 %collective-permute-start.1 = (f32[2,8,16,128]{3,1,2,0:T(8,128)S(1)}, f32[2,8,16,128]{3,1,2,0:T(8,128)S(1)}, u32[]{:S(2)}, u32[]{:S(2)}) collective-permute-start(f32[2,8,16,128]{3,1,2,0:T(8,128)S(1)} %get-tuple-element.17), channel_id=1, source_target_pairs={{0,8},{8,0},{4,12},{12,4},{16,24},{24,16},{20,28},{28,20},{1,9},{9... | collective-permute-start | bytes 393224 | tf_op jit(solution)/shard_map/ppermute | solution.py:17
  71.5 11.4 %copy-start.2 = (bf16[64,8,8,128]{3,2,1,0:T(8,128)(2,1)}, bf16[64,8,8,128]{3,2,1,0:T(8,128)(2,1)S(1)}, u32[]{:S(2)}) copy-start(bf16[64,8,8,128]{3,2,1,0:T(8,128)(2,1)S(1)} %copy.88) | copy-start | bytes 3145732
  78.1 4.8 %collective-permute-start.2 = (bf16[2,8,16,128]{3,1,2,0:T(8,128)(2,1)S(1)}, bf16[2,8,16,128]{3,1,2,0:T(8,128)(2,1)S(1)}, u32[]{:S(2)}, u32[]{:S(2)}) collective-permute-start(bf16[2,8,16,128]{3,1,2,0:T(8,128)(2,1)S(1)} %add_multiply_fusion.2), channel_id=1, source_target_pairs={{0,16},{16,0},{4,20},{20,4},{8,24},{24,8},{12,28},{28,12},{1,17},{... | collective-permute-start | bytes 196616 | tf_op jit(solution)/shard_map/ppermute | solution.py:17
  82.9 5.4 %copy-start.11 = (bf16[1,8,3,16,128]{4,3,2,1,0:T(8,128)(2,1)}, bf16[1,8,3,16,128]{4,3,2,1,0:T(8,128)(2,1)S(1)}, u32[]{:S(2)}) copy-start(bf16[1,8,3,16,128]{4,3,2,1,0:T(8,128)(2,1)S(1)} %copy.59) | copy-start | bytes 294916
  88.4 6.2 %copy-start.1 = (f32[8,512,560]{1,2,0:T(8,128)S(1)}, f32[8,512,560]{1,2,0:T(8,128)}, u32[]{:S(2)}) copy-start(f32[8,512,560]{1,2,0:T(8,128)} %get-tuple-element.19) | copy-start | bytes 27525124
  88.4 6.4 %copy-start.9 = (bf16[64,8,8,128]{3,2,1,0:T(8,128)(2,1)S(1)}, bf16[64,8,8,128]{3,2,1,0:T(8,128)(2,1)}, u32[]{:S(2)}) copy-start(bf16[64,8,8,128]{3,2,1,0:T(8,128)(2,1)} %copy.89) | copy-start | bytes 3145732
  103.4 36.5 %all-to-all-start.3 = ((bf16[4,128,1024]{1,2,0:T(8,128)(2,1)}), bf16[4,128,1024]{1,2,0:T(8,128)(2,1)}, u32[]{:S(2)}, u32[]{:S(2)}) async-start(bf16[4,128,1024]{1,2,0:T(8,128)(2,1)} %copy.62), calls=%async_computation.3 | async-start | bytes 2097152 | tf_op jit(solution)/shard_map/all_to_all | solution.py:93
  121.0 14.3 %copy-start = (bf16[8,512,560]{1,2,0:T(8,128)(2,1)S(1)}, bf16[8,512,560]{1,2,0:T(8,128)(2,1)}, u32[]{:S(2)}) copy-start(bf16[8,512,560]{1,2,0:T(8,128)(2,1)} %fusion.3) | copy-start | bytes 13762564
  125.1 10.2 %copy-start.12 = (bf16[1,8,3,16,128]{4,3,2,1,0:T(8,128)(2,1)S(1)}, bf16[1,8,3,16,128]{4,3,2,1,0:T(8,128)(2,1)}, u32[]{:S(2)}) copy-start(bf16[1,8,3,16,128]{4,3,2,1,0:T(8,128)(2,1)} %copy-done.11) | copy-start | bytes 294916
  125.3 8.7 %copy-start.10 = (f32[2,8,3,16,128]{4,1,3,0,2:T(8,128)}, f32[2,8,3,16,128]{4,1,3,0,2:T(8,128)S(1)}, u32[]{:S(2)}) copy-start(f32[2,8,3,16,128]{4,1,3,0,2:T(8,128)S(1)} %copy_dynamic-update-slice_fusion) | copy-start | bytes 1179652
  125.3 8.6 %collective-permute-start.3 = (f32[2,8,16,128]{3,1,2,0:T(8,128)S(1)}, f32[2,8,16,128]{3,1,2,0:T(8,128)S(1)}, u32[]{:S(2)}, u32[]{:S(2)}) collective-permute-start(f32[2,8,16,128]{3,1,2,0:T(8,128)S(1)} %slice_bitcast_fusion.2), channel_id=1, source_target_pairs={{0,16},{16,0},{4,20},{20,4},{8,24},{24,8},{12,28},{28,12},{1,17},{... | collective-permute-start | bytes 393224 | tf_op jit(solution)/shard_map/ppermute | solution.py:17
  134.6 9.4 %collective-permute-start.4 = (f32[2,8,16,128]{3,1,2,0:T(8,128)}, f32[2,8,16,128]{3,1,2,0:T(8,128)}, u32[]{:S(2)}, u32[]{:S(2)}) collective-permute-start(f32[2,8,16,128]{3,1,2,0:T(8,128)} %fusion.38), channel_id=1, source_target_pairs={{0,8},{8,0},{4,12},{12,4},{16,24},{24,16},{20,28},{28,20},{1,9},{9... | collective-permute-start | bytes 393224 | tf_op jit(solution)/shard_map/ppermute | solution.py:17
  139.8 17.8 %all-to-all-start.5 = ((bf16[4,128,1024]{1,2,0:T(8,128)(2,1)}), bf16[4,128,1024]{1,2,0:T(8,128)(2,1)S(1)}, u32[]{:S(2)}, u32[]{:S(2)}) async-start(bf16[4,128,1024]{1,2,0:T(8,128)(2,1)} %copy.65), calls=%async_computation.5 | async-start | bytes 2097152 | tf_op jit(solution)/shard_map/all_to_all | solution.py:96
  145.1 5.1 %collective-permute-start.5 = (f32[2,8,16,128]{3,1,2,0:T(8,128)S(1)}, f32[2,8,16,128]{3,1,2,0:T(8,128)S(1)}, u32[]{:S(2)}, u32[]{:S(2)}) collective-permute-start(f32[2,8,16,128]{3,1,2,0:T(8,128)S(1)} %fusion.37), channel_id=1, source_target_pairs={{0,4},{4,0},{8,12},{12,8},{16,20},{20,16},{24,28},{28,24},{1,5},{5... | collective-permute-start | bytes 393224 | tf_op jit(solution)/shard_map/ppermute | solution.py:17
  157.7 18.0 %all-to-all-start.6 = ((bf16[4,128,1024]{2,1,0:T(8,128)(2,1)}), bf16[4,128,1024]{2,1,0:T(8,128)(2,1)S(1)}, u32[]{:S(2)}, u32[]{:S(2)}) async-start(bf16[4,128,1024]{2,1,0:T(8,128)(2,1)} %all_to_all.124), calls=%async_computation.6 | async-start | bytes 2097152 | tf_op jit(solution)/shard_map/all_to_all | solution.py:103
  175.6 18.0 %all-to-all-start.7 = ((bf16[4,128,1024]{2,1,0:T(8,128)(2,1)}), bf16[4,128,1024]{2,1,0:T(8,128)(2,1)S(1)}, u32[]{:S(2)}, u32[]{:S(2)}) async-start(bf16[4,128,1024]{2,1,0:T(8,128)(2,1)} %all_to_all.128), calls=%async_computation.7 | async-start | bytes 2097152 | tf_op jit(solution)/shard_map/all_to_all | solution.py:106
  (4 other events, 12.8 us)
where the time goes:
time: 197 us; the launch traced here: 196 us
  waiting for transfers between devices  76.9 us (39%)
  starting transfers between devices  48.5 us (25%)
  local copies, waits for them, and re-layouts  29.3 us (15%)
  matrix products  23.5 us (12%)
  other arithmetic  16.3 us (8%)
    ppermute x6, waiting for transfers between devices, swapped(): return lax.ppermute(block, axis, route)  15.9 us
    unnamed x37, local copies, waits for them, and re-layouts  13.1 us
    all_to_all x1, waiting for transfers between devices, on_device(): lax.all_to_all(values_in, 'head', split_axis=1, concat_axis=0, tiled=True)  12.3 us
    all_to_all x1, waiting for transfers between devices, on_device(): lax.all_to_all(queries, 'head', split_axis=1, concat_axis=0, tiled=True)  11.9 us
    all_to_all x1, waiting for transfers between devices, on_device(): lax.all_to_all(keys_in, 'head', split_axis=1, concat_axis=0, tiled=True)  10.9 us
    convert_element_type x1, other arithmetic, on_device(): (scale_q * probs * (dprob - jnp.sum(probs * dprob, axis=-1, keepdims=True...  10.9 us
    ppermute x6, starting transfers between devices, swapped(): return lax.ppermute(block, axis, route)  10.6 us
    all_to_all x1, waiting for transfers between devices, on_device(): lax.all_to_all(grad_key.reshape(rows_here, width_here), 'head', split_axi...  9.8 us
  transfers between devices with their start and end apart: 14, of which 11 were waited for; matrix products, arithmetic and copies ran while one was open for 20% of the time, Pallas kernels for 0%

commit v1 on v0

v1 whole, which is shorter than its diff:
```python
import functools
import math

import jax
import jax.numpy as jnp
from jax import lax
from jax.experimental import pallas as pl
from jax.experimental.pallas import tpu as pltpu
from jax.sharding import PartitionSpec as P

HD = 128
CROWS = 16
SCALE = HD**-0.5


def swapped(block, axis, mask):
    count = lax.axis_size(axis)
    return lax.ppermute(block, axis, [(i, i ^ mask) for i in range(count)])


def attention_kernel(parts, depth, pool_size, *refs):
    blocks = refs[:parts]
    coarse_ref = refs[parts]
    out_refs = refs[parts + 1 : 2 * parts + 1]
    local_ref, coarse_grad_ref = refs[2 * parts + 1 :]
    rows = blocks[0].shape[1]
    own = parts * rows

    def whole(which):
        return jnp.concatenate([b[which] for b in blocks], axis=0)

    keys = jnp.concatenate([whole(0), coarse_ref[0]], axis=0)
    values = jnp.concatenate([whole(1), coarse_ref[1]], axis=0)
    queries, grads = whole(2), whole(3)
    seen = keys.shape[0]

    def dot(a, b, over):
        return lax.dot_general(
            a, b, (((over[0],), (over[1],)), ((), ())), preferred_element_type=jnp.float32
        )

    scores = dot(keys, queries, (1, 1)) * (SCALE * math.log2(math.e))
    row = lax.broadcasted_iota(jnp.int32, (seen - own, 1), 0)
    offset = (row // CROWS).astype(jnp.float32) + math.log2(pool_size)
    scores = jnp.concatenate([scores[:own], scores[own:] + offset], axis=0)
    powers = jnp.exp2(scores - jnp.max(scores, axis=0, keepdims=True))
    probs = powers * (1.0 / jnp.sum(powers, axis=0, keepdims=True))
    probs_low = probs.astype(jnp.bfloat16)
    dprob = dot(values, grads, (1, 1))
    mean = jnp.sum(probs * dprob, axis=0, keepdims=True)
    dscore = (probs * SCALE * (dprob - mean)).astype(jnp.bfloat16)
    attended = dot(values, probs_low, (0, 0)).T.astype(jnp.bfloat16)
    grad_query = dot(keys, dscore, (0, 0)).T.astype(jnp.bfloat16)
    dkeys = dot(dscore, queries, (1, 0))
    dvalues = dot(probs_low, grads, (1, 0))
    for part in range(parts):
        here = slice(part * rows, (part + 1) * rows)
        out_refs[part][0] = attended[here]
        out_refs[part][1] = grad_query[here]
    local_ref[0] = dkeys[:own]
    local_ref[1] = dvalues[:own]
    coarse_grad_ref[0] = dkeys[own:]
    coarse_grad_ref[1] = dvalues[own:]


def attention(blocks, coarse, first_head, depth, pool_size):
    parts = len(blocks)
    _, rows, width = blocks[0].shape
    heads = width // HD
    own = parts * rows
    extra = coarse.shape[1]
    seen = own + extra
    by_head = lambda h: (0, 0, h)
    outs = pl.pallas_call(
        functools.partial(attention_kernel, parts, depth, pool_size),
        grid=(heads,),
        in_specs=[pl.BlockSpec((4, rows, HD), by_head)] * parts
        + [pl.BlockSpec((2, extra, HD), lambda h: (0, 0, first_head + h))],
        out_specs=[pl.BlockSpec((2, rows, HD), by_head)] * parts
        + [pl.BlockSpec((2, own, HD), by_head), pl.BlockSpec((2, extra, HD), by_head)],
        out_shape=[jax.ShapeDtypeStruct((2, rows, width), jnp.bfloat16)] * parts
        + [
            jax.ShapeDtypeStruct((2, own, width), jnp.float32),
            jax.ShapeDtypeStruct((2, extra, width), jnp.float32),
        ],
        compiler_params=pltpu.CompilerParams(vmem_limit_bytes=40 * 1024 * 1024),
        cost_estimate=pl.CostEstimate(
            flops=12 * heads * own * seen * HD,
            bytes_accessed=24 * own * width,
            transcendentals=heads * own * seen,
        ),
        name="attention",
    )(*blocks, coarse)
    return outs[:parts], outs[parts], outs[parts + 1]


def on_device(queries, keys_in, values_in, grad_out):
    seq_count = lax.axis_size("seq")
    parts = lax.axis_size("head")
    me = lax.axis_index("head")
    depth = seq_count.bit_length() - 1
    rows, columns = queries.shape
    own = rows * parts
    pool_size = own // CROWS
    width = columns // parts
    heads = width // HD
    groups = 2 if heads % 2 == 0 else 1
    span = width // groups
    arrays = (keys_in, values_in, queries, grad_out)

    def pooled(x):
        return jnp.mean(x.astype(jnp.float32).reshape(rows // pool_size, pool_size, columns), axis=1)

    pooled_here = jnp.stack([pooled(keys_in), pooled(values_in)], axis=0)

    def column(part, group=0):
        return (me ^ part) * width + group * span

    pooled_parts = []
    for part in range(parts):
        block = lax.dynamic_slice_in_dim(pooled_here, column(part), width, axis=2)
        pooled_parts.append(swapped(block, "head", part) if part else block)
    mean_now = jnp.concatenate(pooled_parts, axis=1)

    blocks = []
    for group in range(groups):
        here = []
        for part in range(parts):
            block = jnp.stack(
                [lax.dynamic_slice_in_dim(x, column(part, group), span, axis=1) for x in arrays]
            )
            here.append(swapped(block, "head", part) if part else block)
        blocks.append(here)

    siblings = []
    for level in range(depth):
        received = swapped(mean_now, "seq", 1 << level)
        siblings.append(received)
        mean_now = 0.5 * (mean_now + received)
    coarse = jnp.concatenate(siblings, axis=1).astype(jnp.bfloat16)

    outs = [jnp.zeros((rows, columns), jnp.bfloat16) for _ in range(4)]
    for group in range(groups):
        sent, local, coarse_grad = attention(
            blocks[group], coarse, group * (heads // groups), depth, pool_size
        )
        coarse_grad = coarse_grad.reshape(2, depth, CROWS, span)
        for part in range(parts):
            back = swapped(sent[part], "head", part) if part else sent[part]
            for which in range(2):
                outs[which] = lax.dynamic_update_slice(
                    outs[which], back[which], (0, column(part, group))
                )
        above = jnp.zeros((2, CROWS, span), jnp.float32)
        for level in reversed(range(depth)):
            outgoing = coarse_grad[:, level] + 0.5 * above
            above = 0.5 * above + swapped(outgoing, "seq", 1 << level)
        above = above / float(pool_size)
        per = rows // pool_size
        for part in range(parts):
            spread = jnp.repeat(above[:, part * per : (part + 1) * per], pool_size, axis=1)
            total = (local[:, part * rows : (part + 1) * rows] + spread).astype(jnp.bfloat16)
            back = swapped(total, "head", part) if part else total
            for which in range(2):
                outs[2 + which] = lax.dynamic_update_slice(
                    outs[2 + which], back[which], (0, column(part, group))
                )
    return tuple(outs)


def solution(mesh):
    placed = (P(("seq", "head"), None),) * 4
    return jax.shard_map(
        on_device, mesh=mesh, in_specs=placed, out_specs=placed, check_vma=False
    )
```

time: 197 us -> 122 us (0.62)
  local copies, waits for them, and re-layouts: 29.3 us -> 3.95 us
  matrix products: 23.5 us -> 0 us
  waiting for transfers between devices: 76.9 us -> 55.9 us
  Pallas kernels: 0 us -> 13.5 us
  other arithmetic: 16.3 us -> 4.56 us
  starting transfers between devices: 48.5 us -> 43 us
    all_to_all x8 -> x0, waiting for transfers between devices: 60.9 us -> none  [the longest x1 12.3 us: on_device(): lax.all_to_all(values_in, 'head', split_axis=1, concat_axis=0, tiled=True)]
    ppermute x6 -> x30, waiting for transfers between devices: 15.9 us -> 55.9 us  [swapped(): return lax.ppermute(block, axis, [(i, i ^ mask) for i in range(count)])]
    all_to_all x8 -> x0, starting transfers between devices: 37.9 us -> none  [the longest x1 6.69 us: on_device(): lax.all_to_all(attended.reshape(rows_here, width_here), 'head', split_axi...]
    ppermute x6 -> x30, starting transfers between devices: 10.6 us -> 43 us  [swapped(): return lax.ppermute(block, axis, [(i, i ^ mask) for i in range(count)])]
    dot_general x5 -> x0, matrix products: 18.1 us -> none  [the longest x1 4.82 us: on_device(): jnp.einsum('hst,htd->shd', probs_low, values_full, preferred_element_type...]
    pallas_call x0 -> x2, Pallas kernels: none -> 13.5 us  [attention(): pl.pallas_call(functools.partial(attention_kernel, parts, depth, pool_siz...]
    all_to_all x12 -> x0, local copies, waits for them, and re-layouts: 13.2 us -> none  [the longest x2 2.45 us: on_device(): lax.all_to_all(grad_query.reshape(rows_here, width_here), 'head', split_a...]
    convert_element_type x5 -> x2, other arithmetic: 13.4 us -> 0.59 us  [on_device(): (local[:, part * rows:(part + 1) * rows] + spread).astype(jnp.bfloat16)]
  transfers between devices with their start and end apart: 14 -> 30, of which waited for: 11 -> 15; matrix products, arithmetic and copies ran while one was open for 20% -> 2% of each run, Pallas kernels for 0% -> 11%
where the time goes in v1:
time: 122 us
  waiting for transfers between devices  55.9 us (46%)
  starting transfers between devices  43 us (35%)
  Pallas kernels  13.5 us (11%)
  other arithmetic  4.56 us (4%)
  local copies, waits for them, and re-layouts  3.95 us (3%)
    ppermute x30, waiting for transfers between devices, swapped(): return lax.ppermute(block, axis, [(i, i ^ mask) for i in range(count)])  55.9 us
    ppermute x30, starting transfers between devices, swapped(): return lax.ppermute(block, axis, [(i, i ^ mask) for i in range(count)])  43 us
    pallas_call x2, Pallas kernels, attention(): pl.pallas_call(functools.partial(attention_kernel, parts, depth, pool_siz...  13.5 us
    reduce_sum x2, other arithmetic, pooled(): jnp.mean(x.astype(jnp.float32).reshape(rows // pool_size, pool_size, colu...  3.14 us
    unnamed x16, local copies, waits for them, and re-layouts  2.52 us
  transfers between devices with their start and end apart: 30, of which 15 were waited for; matrix products, arithmetic and copies ran while one was open for 2% of the time, Pallas kernels for 11%

profile of v1, /device:TPU:1, one launch (start us, length us, event | category | flops | bytes accessed | tf_op | source)
XLA Modules:
  0.0 122.1 jit_solution(9675514841521279104)
XLA Ops:
  0.7 1.6 %convert_reduce_fusion = f32[4,4096]{1,0:T(4,128)S(1)} fusion(bf16[128,4096]{1,0:T(8,128)(2,1)} %param.6), kind=kLoop, calls=%fused_computation | loop fusion | flops 1032192 | bytes 1114112 | tf_op jit(solution)/shard_map/reduce_sum | solution.py:112
  4.0 2.7 %collective-permute-start.4 = (f32[2,4,1024]{2,1,0:T(4,128)S(1)}, f32[2,4,1024]{2,1,0:T(4,128)S(1)}, u32[]{:S(2)}, u32[]{:S(2)}) collective-permute-start(f32[2,4,1024]{2,1,0:T(4,128)S(1)} %get-tuple-element.100), channel_id=1, source_target_pairs={{0,2},{1,3},{2,0},{3,1},{4,6},{5,7},{6,4},{7,5},{8,10},{9,11},{10,... | collective-permute-start | bytes 98312 | tf_op jit(solution)/shard_map/ppermute | solution.py:18
  16.8 2.7 %collective-permute-done.7 = f32[2,16,1024]{2,1,0:T(8,128)S(1)} collective-permute-done((f32[2,16,1024]{2,1,0:T(8,128)S(1)}, f32[2,16,1024]{2,1,0:T(8,128)S(1)}, u32[]{:S(2)}, u32[]{:S(2)}) %collective-permute-start.7) | collective-permute-done | bytes 131104 | tf_op jit(solution)/shard_map/ppermute | solution.py:18
  19.5 2.4 %collective-permute-start.8 = (bf16[2,16,1024]{2,1,0:T(8,128)(2,1)S(1)}, bf16[2,16,1024]{2,1,0:T(8,128)(2,1)S(1)}, u32[]{:S(2)}, u32[]{:S(2)}) collective-permute-start(bf16[2,16,1024]{2,1,0:T(8,128)(2,1)S(1)} %add_multiply_fusion), channel_id=1, source_target_pairs={{0,16},{4,20},{8,24},{12,28},{16,0},{20,4},{24,8},{28,12},{1,17},{... | collective-permute-start | bytes 196616 | tf_op jit(solution)/shard_map/ppermute | solution.py:18
  21.9 1.6 %collective-permute-done.8 = bf16[2,16,1024]{2,1,0:T(8,128)(2,1)S(1)} collective-permute-done((bf16[2,16,1024]{2,1,0:T(8,128)(2,1)S(1)}, bf16[2,16,1024]{2,1,0:T(8,128)(2,1)S(1)}, u32[]{:S(2)}, u32[]{:S(2)}) %collective-permute-start.8) | collective-permute-done | bytes 65568 | tf_op jit(solution)/shard_map/ppermute | solution.py:18
  23.9 3.5 %collective-permute-start = (bf16[4,128,512]{2,1,0:T(8,128)(2,1)S(1)}, bf16[4,128,512]{2,1,0:T(8,128)(2,1)S(1)}, u32[]{:S(2)}, u32[]{:S(2)}) collective-permute-start(bf16[4,128,512]{2,1,0:T(8,128)(2,1)S(1)} %pad_maximum_fusion.1), channel_id=1, source_target_pairs={{0,1},{1,0},{2,3},{3,2},{4,5},{5,4},{6,7},{7,6},{8,9},{9,8},{10,11... | collective-permute-start | bytes 1572872 | tf_op jit(solution)/shard_map/ppermute | solution.py:18
  27.5 7.5 %collective-permute-done.14.refs_3_ = bf16[4,128,512]{2,1,0:T(8,128)(2,1)S(1)} collective-permute-done((bf16[4,128,512]{2,1,0:T(8,128)(2,1)S(1)}, bf16[4,128,512]{2,1,0:T(8,128)(2,1)S(1)}, u32[]{:S(2)}, u32[]{:S(2)}) %collective-permute-start.14) | collective-permute-done | bytes 524320 | tf_op jit(solution)/shard_map/ppermute | solution.py:18
  35.0 6.7 %attention.3 = (bf16[2,128,512]{2,1,0:T(8,128)(2,1)S(1)}, bf16[2,128,512]{2,1,0:T(8,128)(2,1)S(1)}, bf16[2,128,512]{2,1,0:T(8,128)(2,1)S(1)}, bf16[2,128,512]{2,...) custom-call(bf16[4,128,512]{2,1,0:T(8,128)(2,1)S(1)} %pad_maximum_fusion.4.refs_0_, ...), custom_call_target="tpu_custom_call" | custom-call | flops 1761607680 | bytes 6291456 | tf_op jit(solution)/shard_map/attention/pallas_call | solution.py:74
  41.8 2.8 %collective-permute-start.24 = (f32[2,16,512]{2,1,0:T(8,128)S(1)}, f32[2,16,512]{2,1,0:T(8,128)S(1)}, u32[]{:S(2)}, u32[]{:S(2)}) collective-permute-start(f32[2,16,512]{2,1,0:T(8,128)S(1)} %slice_bitcast_fusion.30), channel_id=1, source_target_pairs={{0,16},{4,20},{8,24},{12,28},{16,0},{20,4},{24,8},{28,12},{1,17},{... | collective-permute-start | bytes 196616 | tf_op jit(solution)/shard_map/ppermute | solution.py:18
  44.6 1.6 %collective-permute-done.2.refs_3_ = bf16[4,128,512]{2,1,0:T(8,128)(2,1)S(1)} collective-permute-done((bf16[4,128,512]{2,1,0:T(8,128)(2,1)S(1)}, bf16[4,128,512]{2,1,0:T(8,128)(2,1)S(1)}, u32[]{:S(2)}, u32[]{:S(2)}) %collective-permute-start.2) | collective-permute-done | bytes 524320 | tf_op jit(solution)/shard_map/ppermute | solution.py:18
  46.2 10.1 %collective-permute-done.1.refs_2_ = bf16[4,128,512]{2,1,0:T(8,128)(2,1)S(1)} collective-permute-done((bf16[4,128,512]{2,1,0:T(8,128)(2,1)S(1)}, bf16[4,128,512]{2,1,0:T(8,128)(2,1)S(1)}, u32[]{:S(2)}, u32[]{:S(2)}) %collective-permute-start.1) | collective-permute-done | bytes 524320 | tf_op jit(solution)/shard_map/ppermute | solution.py:18
  56.4 6.7 %attention.2 = (bf16[2,128,512]{2,1,0:T(8,128)(2,1)S(1)}, bf16[2,128,512]{2,1,0:T(8,128)(2,1)S(1)}, bf16[2,128,512]{2,1,0:T(8,128)(2,1)S(1)}, bf16[2,128,512]{2,...) custom-call(bf16[4,128,512]{2,1,0:T(8,128)(2,1)S(1)} %pad_maximum_fusion.refs_0_, ...), custom_call_target="tpu_custom_call" | custom-call | flops 1761607680 | bytes 6291456 | tf_op jit(solution)/shard_map/attention/pallas_call | solution.py:74
  63.1 2.4 %collective-permute-start.18 = (f32[2,16,512]{2,1,0:T(8,128)S(1)}, f32[2,16,512]{2,1,0:T(8,128)S(1)}, u32[]{:S(2)}, u32[]{:S(2)}) collective-permute-start(f32[2,16,512]{2,1,0:T(8,128)S(1)} %slice_bitcast_fusion.33), channel_id=1, source_target_pairs={{0,16},{4,20},{8,24},{12,28},{16,0},{20,4},{24,8},{28,12},{1,17},{... | collective-permute-start | bytes 196616 | tf_op jit(solution)/shard_map/ppermute | solution.py:18
  65.7 1.5 %collective-permute-start.9 = (bf16[2,128,512]{2,1,0:T(8,128)(2,1)S(1)}, bf16[2,128,512]{2,1,0:T(8,128)(2,1)S(1)}, u32[]{:S(2)}, u32[]{:S(2)}) collective-permute-start(bf16[2,128,512]{2,1,0:T(8,128)(2,1)S(1)} %get-tuple-element.17), channel_id=1, source_target_pairs={{0,1},{1,0},{2,3},{3,2},{4,5},{5,4},{6,7},{7,6},{8,9},{9,8},{10,11... | collective-permute-start | bytes 786440 | tf_op jit(solution)/shard_map/ppermute | solution.py:18
  70.9 2.5 %collective-permute-done.19 = f32[2,16,512]{2,1,0:T(8,128)S(1)} collective-permute-done((f32[2,16,512]{2,1,0:T(8,128)S(1)}, f32[2,16,512]{2,1,0:T(8,128)S(1)}, u32[]{:S(2)}, u32[]{:S(2)}) %collective-permute-start.19) | collective-permute-done | bytes 65568 | tf_op jit(solution)/shard_map/ppermute | solution.py:18
  74.6 2.2 %collective-permute-done.25 = f32[2,16,512]{2,1,0:T(8,128)S(1)} collective-permute-done((f32[2,16,512]{2,1,0:T(8,128)S(1)}, f32[2,16,512]{2,1,0:T(8,128)S(1)}, u32[]{:S(2)}, u32[]{:S(2)}) %collective-permute-start.25) | collective-permute-done | bytes 65568 | tf_op jit(solution)/shard_map/ppermute | solution.py:18
  78.1 2.2 %collective-permute-done.20 = f32[2,16,512]{2,1,0:T(8,128)S(1)} collective-permute-done((f32[2,16,512]{2,1,0:T(8,128)S(1)}, f32[2,16,512]{2,1,0:T(8,128)S(1)}, u32[]{:S(2)}, u32[]{:S(2)}) %collective-permute-start.20) | collective-permute-done | bytes 65568 | tf_op jit(solution)/shard_map/ppermute | solution.py:18
  84.9 4.1 %collective-permute-start.17 = (bf16[2,128,512]{2,1,0:T(8,128)(2,1)S(1)}, bf16[2,128,512]{2,1,0:T(8,128)(2,1)S(1)}, u32[]{:S(2)}, u32[]{:S(2)}) collective-permute-start(bf16[2,128,512]{2,1,0:T(8,128)(2,1)S(1)} %get-tuple-element.23), channel_id=1, source_target_pairs={{0,3},{1,2},{2,1},{3,0},{4,7},{5,6},{6,5},{7,4},{8,11},{9,10},{10,... | collective-permute-start | bytes 786440 | tf_op jit(solution)/shard_map/ppermute | solution.py:18
  91.6 3.3 %collective-permute-start.27 = (bf16[2,128,512]{2,1,0:T(8,128)(2,1)S(1)}, bf16[2,128,512]{2,1,0:T(8,128)(2,1)S(1)}, u32[]{:S(2)}, u32[]{:S(2)}) collective-permute-start(bf16[2,128,512]{2,1,0:T(8,128)(2,1)S(1)} %get-tuple-element.30), channel_id=1, source_target_pairs={{0,1},{1,0},{2,3},{3,2},{4,5},{5,4},{6,7},{7,6},{8,9},{9,8},{10,11... | collective-permute-start | bytes 786440 | tf_op jit(solution)/shard_map/ppermute | solution.py:18
  94.9 4.8 %collective-permute-done.17 = bf16[2,128,512]{2,1,0:T(8,128)(2,1)S(1)} collective-permute-done((bf16[2,128,512]{2,1,0:T(8,128)(2,1)S(1)}, bf16[2,128,512]{2,1,0:T(8,128)(2,1)S(1)}, u32[]{:S(2)}, u32[]{:S(2)}) %collective-permute-start.17) | collective-permute-done | bytes 262176 | tf_op jit(solution)/shard_map/ppermute | solution.py:18
  99.7 2.3 %collective-permute-start.28 = (bf16[2,128,512]{2,1,0:T(8,128)(2,1)S(1)}, bf16[2,128,512]{2,1,0:T(8,128)(2,1)S(1)}, u32[]{:S(2)}, u32[]{:S(2)}) collective-permute-start(bf16[2,128,512]{2,1,0:T(8,128)(2,1)S(1)} %get-tuple-element.29), channel_id=1, source_target_pairs={{0,2},{1,3},{2,0},{3,1},{4,6},{5,7},{6,4},{7,5},{8,10},{9,11},{10,... | collective-permute-start | bytes 786440 | tf_op jit(solution)/shard_map/ppermute | solution.py:18
  102.8 8.1 %collective-permute-done.23 = bf16[2,128,512]{2,1,0:T(8,128)(2,1)S(1)} collective-permute-done((bf16[2,128,512]{2,1,0:T(8,128)(2,1)S(1)}, bf16[2,128,512]{2,1,0:T(8,128)(2,1)S(1)}, u32[]{:S(2)}, u32[]{:S(2)}) %collective-permute-start.23) | collective-permute-done | bytes 262176 | tf_op jit(solution)/shard_map/ppermute | solution.py:18
  111.1 2.9 %collective-permute-done.28 = bf16[2,128,512]{2,1,0:T(8,128)(2,1)S(1)} collective-permute-done((bf16[2,128,512]{2,1,0:T(8,128)(2,1)S(1)}, bf16[2,128,512]{2,1,0:T(8,128)(2,1)S(1)}, u32[]{:S(2)}, u32[]{:S(2)}) %collective-permute-start.28) | collective-permute-done | bytes 262176 | tf_op jit(solution)/shard_map/ppermute | solution.py:18
  114.0 6.7 %collective-permute-done.29 = bf16[2,128,512]{2,1,0:T(8,128)(2,1)S(1)} collective-permute-done((bf16[2,128,512]{2,1,0:T(8,128)(2,1)S(1)}, bf16[2,128,512]{2,1,0:T(8,128)(2,1)S(1)}, u32[]{:S(2)}, u32[]{:S(2)}) %collective-permute-start.29) | collective-permute-done | bytes 262176 | tf_op jit(solution)/shard_map/ppermute | solution.py:18
  (107 shorter events, 27.8 us)
Async XLA Ops:
  3.9 6.8 %collective-permute-start.3 = (f32[2,4,1024]{2,1,0:T(4,128)S(1)}, f32[2,4,1024]{2,1,0:T(4,128)S(1)}, u32[]{:S(2)}, u32[]{:S(2)}) collective-permute-start(f32[2,4,1024]{2,1,0:T(4,128)S(1)} %get-tuple-element.99), channel_id=1, source_target_pairs={{0,1},{1,0},{2,3},{3,2},{4,5},{5,4},{6,7},{7,6},{8,9},{9,8},{10,11... | collective-permute-start | bytes 98312 | tf_op jit(solution)/shard_map/ppermute | solution.py:18
  4.0 6.7 %collective-permute-start.4 = (f32[2,4,1024]{2,1,0:T(4,128)S(1)}, f32[2,4,1024]{2,1,0:T(4,128)S(1)}, u32[]{:S(2)}, u32[]{:S(2)}) collective-permute-start(f32[2,4,1024]{2,1,0:T(4,128)S(1)} %get-tuple-element.100), channel_id=1, source_target_pairs={{0,2},{1,3},{2,0},{3,1},{4,6},{5,7},{6,4},{7,5},{8,10},{9,11},{10,... | collective-permute-start | bytes 98312 | tf_op jit(solution)/shard_map/ppermute | solution.py:18
  8.7 15.2 %collective-permute-start.12 = (bf16[4,128,512]{2,1,0:T(8,128)(2,1)S(1)}, bf16[4,128,512]{2,1,0:T(8,128)(2,1)S(1)}, u32[]{:S(2)}, u32[]{:S(2)}) collective-permute-start(bf16[4,128,512]{2,1,0:T(8,128)(2,1)S(1)} %pad_maximum_fusion.5), channel_id=1, source_target_pairs={{0,1},{1,0},{2,3},{3,2},{4,5},{5,4},{6,7},{7,6},{8,9},{9,8},{10,11... | collective-permute-start | bytes 1572872 | tf_op jit(solution)/shard_map/ppermute | solution.py:18
  9.2 18.3 %collective-permute-start.13 = (bf16[4,128,512]{2,1,0:T(8,128)(2,1)S(1)}, bf16[4,128,512]{2,1,0:T(8,128)(2,1)S(1)}, u32[]{:S(2)}, u32[]{:S(2)}) collective-permute-start(bf16[4,128,512]{2,1,0:T(8,128)(2,1)S(1)} %pad_maximum_fusion.6), channel_id=1, source_target_pairs={{0,2},{1,3},{2,0},{3,1},{4,6},{5,7},{6,4},{7,5},{8,10},{9,11},{10,... | collective-permute-start | bytes 1572872 | tf_op jit(solution)/shard_map/ppermute | solution.py:18
  10.8 4.5 %collective-permute-start.6 = (f32[2,16,1024]{2,1,0:T(8,128)S(1)}, f32[2,16,1024]{2,1,0:T(8,128)S(1)}, u32[]{:S(2)}, u32[]{:S(2)}) collective-permute-start(f32[2,16,1024]{2,1,0:T(8,128)S(1)} %pad_maximum_fusion.9), channel_id=1, source_target_pairs={{0,4},{4,0},{8,12},{12,8},{16,20},{20,16},{24,28},{28,24},{1,5},{5... | collective-permute-start | bytes 393224 | tf_op jit(solution)/shard_map/ppermute | solution.py:18
  12.1 22.9 %collective-permute-start.14 = (bf16[4,128,512]{2,1,0:T(8,128)(2,1)S(1)}, bf16[4,128,512]{2,1,0:T(8,128)(2,1)S(1)}, u32[]{:S(2)}, u32[]{:S(2)}) collective-permute-start(bf16[4,128,512]{2,1,0:T(8,128)(2,1)S(1)} %pad_maximum_fusion.7), channel_id=1, source_target_pairs={{0,3},{1,2},{2,1},{3,0},{4,7},{5,6},{6,5},{7,4},{8,11},{9,10},{10,... | collective-permute-start | bytes 1572872 | tf_op jit(solution)/shard_map/ppermute | solution.py:18
  13.3 32.9 %collective-permute-start.2 = (bf16[4,128,512]{2,1,0:T(8,128)(2,1)S(1)}, bf16[4,128,512]{2,1,0:T(8,128)(2,1)S(1)}, u32[]{:S(2)}, u32[]{:S(2)}) collective-permute-start(bf16[4,128,512]{2,1,0:T(8,128)(2,1)S(1)} %pad_maximum_fusion.3), channel_id=1, source_target_pairs={{0,3},{1,2},{2,1},{3,0},{4,7},{5,6},{6,5},{7,4},{8,11},{9,10},{10,... | collective-permute-start | bytes 1572872 | tf_op jit(solution)/shard_map/ppermute | solution.py:18
  15.3 4.2 %collective-permute-start.7 = (f32[2,16,1024]{2,1,0:T(8,128)S(1)}, f32[2,16,1024]{2,1,0:T(8,128)S(1)}, u32[]{:S(2)}, u32[]{:S(2)}) collective-permute-start(f32[2,16,1024]{2,1,0:T(8,128)S(1)} %get-tuple-element.97), channel_id=1, source_target_pairs={{0,8},{4,12},{8,0},{12,4},{16,24},{20,28},{24,16},{28,20},{1,9},{5... | collective-permute-start | bytes 393224 | tf_op jit(solution)/shard_map/ppermute | solution.py:18
  23.6 32.8 %collective-permute-start.1 = (bf16[4,128,512]{2,1,0:T(8,128)(2,1)S(1)}, bf16[4,128,512]{2,1,0:T(8,128)(2,1)S(1)}, u32[]{:S(2)}, u32[]{:S(2)}) collective-permute-start(bf16[4,128,512]{2,1,0:T(8,128)(2,1)S(1)} %pad_maximum_fusion.2), channel_id=1, source_target_pairs={{0,2},{1,3},{2,0},{3,1},{4,6},{5,7},{6,4},{7,5},{8,10},{9,11},{10,... | collective-permute-start | bytes 1572872 | tf_op jit(solution)/shard_map/ppermute | solution.py:18
  23.9 32.5 %collective-permute-start = (bf16[4,128,512]{2,1,0:T(8,128)(2,1)S(1)}, bf16[4,128,512]{2,1,0:T(8,128)(2,1)S(1)}, u32[]{:S(2)}, u32[]{:S(2)}) collective-permute-start(bf16[4,128,512]{2,1,0:T(8,128)(2,1)S(1)} %pad_maximum_fusion.1), channel_id=1, source_target_pairs={{0,1},{1,0},{2,3},{3,2},{4,5},{5,4},{6,7},{7,6},{8,9},{9,8},{10,11... | collective-permute-start | bytes 1572872 | tf_op jit(solution)/shard_map/ppermute | solution.py:18
  41.8 27.9 %collective-permute-start.24 = (f32[2,16,512]{2,1,0:T(8,128)S(1)}, f32[2,16,512]{2,1,0:T(8,128)S(1)}, u32[]{:S(2)}, u32[]{:S(2)}) collective-permute-start(f32[2,16,512]{2,1,0:T(8,128)S(1)} %slice_bitcast_fusion.30), channel_id=1, source_target_pairs={{0,16},{4,20},{8,24},{12,28},{16,0},{20,4},{24,8},{28,12},{1,17},{... | collective-permute-start | bytes 196616 | tf_op jit(solution)/shard_map/ppermute | solution.py:18
  63.1 5.9 %collective-permute-start.18 = (f32[2,16,512]{2,1,0:T(8,128)S(1)}, f32[2,16,512]{2,1,0:T(8,128)S(1)}, u32[]{:S(2)}, u32[]{:S(2)}) collective-permute-start(f32[2,16,512]{2,1,0:T(8,128)S(1)} %slice_bitcast_fusion.33), channel_id=1, source_target_pairs={{0,16},{4,20},{8,24},{12,28},{16,0},{20,4},{24,8},{28,12},{1,17},{... | collective-permute-start | bytes 196616 | tf_op jit(solution)/shard_map/ppermute | solution.py:18
  65.7 19.2 %collective-permute-start.9 = (bf16[2,128,512]{2,1,0:T(8,128)(2,1)S(1)}, bf16[2,128,512]{2,1,0:T(8,128)(2,1)S(1)}, u32[]{:S(2)}, u32[]{:S(2)}) collective-permute-start(bf16[2,128,512]{2,1,0:T(8,128)(2,1)S(1)} %get-tuple-element.17), channel_id=1, source_target_pairs={{0,1},{1,0},{2,3},{3,2},{4,5},{5,4},{6,7},{7,6},{8,9},{9,8},{10,11... | collective-permute-start | bytes 786440 | tf_op jit(solution)/shard_map/ppermute | solution.py:18
  67.3 21.8 %collective-permute-start.10 = (bf16[2,128,512]{2,1,0:T(8,128)(2,1)S(1)}, bf16[2,128,512]{2,1,0:T(8,128)(2,1)S(1)}, u32[]{:S(2)}, u32[]{:S(2)}) collective-permute-start(bf16[2,128,512]{2,1,0:T(8,128)(2,1)S(1)} %get-tuple-element.18), channel_id=1, source_target_pairs={{0,2},{1,3},{2,0},{3,1},{4,6},{5,7},{6,4},{7,5},{8,10},{9,11},{10,... | collective-permute-start | bytes 786440 | tf_op jit(solution)/shard_map/ppermute | solution.py:18
  68.5 20.7 %collective-permute-start.11 = (bf16[2,128,512]{2,1,0:T(8,128)(2,1)S(1)}, bf16[2,128,512]{2,1,0:T(8,128)(2,1)S(1)}, u32[]{:S(2)}, u32[]{:S(2)}) collective-permute-start(bf16[2,128,512]{2,1,0:T(8,128)(2,1)S(1)} %get-tuple-element.19), channel_id=1, source_target_pairs={{0,3},{1,2},{2,1},{3,0},{4,7},{5,6},{6,5},{7,4},{8,11},{9,10},{10,... | collective-permute-start | bytes 786440 | tf_op jit(solution)/shard_map/ppermute | solution.py:18
  69.0 21.6 %collective-permute-start.15 = (bf16[2,128,512]{2,1,0:T(8,128)(2,1)S(1)}, bf16[2,128,512]{2,1,0:T(8,128)(2,1)S(1)}, u32[]{:S(2)}, u32[]{:S(2)}) collective-permute-start(bf16[2,128,512]{2,1,0:T(8,128)(2,1)S(1)} %get-tuple-element.21), channel_id=1, source_target_pairs={{0,1},{1,0},{2,3},{3,2},{4,5},{5,4},{6,7},{7,6},{8,9},{9,8},{10,11... | collective-permute-start | bytes 786440 | tf_op jit(solution)/shard_map/ppermute | solution.py:18
  83.4 8.2 %collective-permute-start.16 = (bf16[2,128,512]{2,1,0:T(8,128)(2,1)S(1)}, bf16[2,128,512]{2,1,0:T(8,128)(2,1)S(1)}, u32[]{:S(2)}, u32[]{:S(2)}) collective-permute-start(bf16[2,128,512]{2,1,0:T(8,128)(2,1)S(1)} %get-tuple-element.22), channel_id=1, source_target_pairs={{0,2},{1,3},{2,0},{3,1},{4,6},{5,7},{6,4},{7,5},{8,10},{9,11},{10,... | collective-permute-start | bytes 786440 | tf_op jit(solution)/shard_map/ppermute | solution.py:18
  84.9 14.8 %collective-permute-start.17 = (bf16[2,128,512]{2,1,0:T(8,128)(2,1)S(1)}, bf16[2,128,512]{2,1,0:T(8,128)(2,1)S(1)}, u32[]{:S(2)}, u32[]{:S(2)}) collective-permute-start(bf16[2,128,512]{2,1,0:T(8,128)(2,1)S(1)} %get-tuple-element.23), channel_id=1, source_target_pairs={{0,3},{1,2},{2,1},{3,0},{4,7},{5,6},{6,5},{7,4},{8,11},{9,10},{10,... | collective-permute-start | bytes 786440 | tf_op jit(solution)/shard_map/ppermute | solution.py:18
  89.1 13.0 %collective-permute-start.21 = (bf16[2,128,512]{2,1,0:T(8,128)(2,1)S(1)}, bf16[2,128,512]{2,1,0:T(8,128)(2,1)S(1)}, u32[]{:S(2)}, u32[]{:S(2)}) collective-permute-start(bf16[2,128,512]{2,1,0:T(8,128)(2,1)S(1)} %get-tuple-element.34), channel_id=1, source_target_pairs={{0,1},{1,0},{2,3},{3,2},{4,5},{5,4},{6,7},{7,6},{8,9},{9,8},{10,11... | collective-permute-start | bytes 786440 | tf_op jit(solution)/shard_map/ppermute | solution.py:18
  89.2 13.6 %collective-permute-start.22 = (bf16[2,128,512]{2,1,0:T(8,128)(2,1)S(1)}, bf16[2,128,512]{2,1,0:T(8,128)(2,1)S(1)}, u32[]{:S(2)}, u32[]{:S(2)}) collective-permute-start(bf16[2,128,512]{2,1,0:T(8,128)(2,1)S(1)} %get-tuple-element.33), channel_id=1, source_target_pairs={{0,2},{1,3},{2,0},{3,1},{4,6},{5,7},{6,4},{7,5},{8,10},{9,11},{10,... | collective-permute-start | bytes 786440 | tf_op jit(solution)/shard_map/ppermute | solution.py:18
  90.6 20.4 %collective-permute-start.23 = (bf16[2,128,512]{2,1,0:T(8,128)(2,1)S(1)}, bf16[2,128,512]{2,1,0:T(8,128)(2,1)S(1)}, u32[]{:S(2)}, u32[]{:S(2)}) collective-permute-start(bf16[2,128,512]{2,1,0:T(8,128)(2,1)S(1)} %get-tuple-element.32), channel_id=1, source_target_pairs={{0,3},{1,2},{2,1},{3,0},{4,7},{5,6},{6,5},{7,4},{8,11},{9,10},{10,... | collective-permute-start | bytes 786440 | tf_op jit(solution)/shard_map/ppermute | solution.py:18
  91.6 19.4 %collective-permute-start.27 = (bf16[2,128,512]{2,1,0:T(8,128)(2,1)S(1)}, bf16[2,128,512]{2,1,0:T(8,128)(2,1)S(1)}, u32[]{:S(2)}, u32[]{:S(2)}) collective-permute-start(bf16[2,128,512]{2,1,0:T(8,128)(2,1)S(1)} %get-tuple-element.30), channel_id=1, source_target_pairs={{0,1},{1,0},{2,3},{3,2},{4,5},{5,4},{6,7},{7,6},{8,9},{9,8},{10,11... | collective-permute-start | bytes 786440 | tf_op jit(solution)/shard_map/ppermute | solution.py:18
  99.7 14.3 %collective-permute-start.28 = (bf16[2,128,512]{2,1,0:T(8,128)(2,1)S(1)}, bf16[2,128,512]{2,1,0:T(8,128)(2,1)S(1)}, u32[]{:S(2)}, u32[]{:S(2)}) collective-permute-start(bf16[2,128,512]{2,1,0:T(8,128)(2,1)S(1)} %get-tuple-element.29), channel_id=1, source_target_pairs={{0,2},{1,3},{2,0},{3,1},{4,6},{5,7},{6,4},{7,5},{8,10},{9,11},{10,... | collective-permute-start | bytes 786440 | tf_op jit(solution)/shard_map/ppermute | solution.py:18
  102.1 18.7 %collective-permute-start.29 = (bf16[2,128,512]{2,1,0:T(8,128)(2,1)S(1)}, bf16[2,128,512]{2,1,0:T(8,128)(2,1)S(1)}, u32[]{:S(2)}, u32[]{:S(2)}) collective-permute-start(bf16[2,128,512]{2,1,0:T(8,128)(2,1)S(1)} %get-tuple-element.28), channel_id=1, source_target_pairs={{0,3},{1,2},{2,1},{3,0},{4,7},{5,6},{6,5},{7,4},{8,11},{9,10},{10,... | collective-permute-start | bytes 786440 | tf_op jit(solution)/shard_map/ppermute | solution.py:18
  (14 other events, 76.7 us)

commit v2 on v1

--- a/solution.py
+++ b/solution.py
@@ -63,21 +63,25 @@
     coarse_grad_ref[1] = dvalues[own:]
 
 
-def attention(blocks, coarse, first_head, depth, pool_size):
+def attention(blocks, coarse, first, heads, depth, pool_size):
     parts = len(blocks)
-    _, rows, width = blocks[0].shape
-    heads = width // HD
+    rows = blocks[0].shape[1]
+    width = heads * HD
     own = parts * rows
     extra = coarse.shape[1]
     seen = own + extra
-    by_head = lambda h: (0, 0, h)
+
+    def block_spec(lead, height, total):
+        skip = first if total > width else 0
+        return pl.BlockSpec((lead, height, HD), lambda h: (0, 0, skip + h))
+
     outs = pl.pallas_call(
         functools.partial(attention_kernel, parts, depth, pool_size),
         grid=(heads,),
-        in_specs=[pl.BlockSpec((4, rows, HD), by_head)] * parts
-        + [pl.BlockSpec((2, extra, HD), lambda h: (0, 0, first_head + h))],
-        out_specs=[pl.BlockSpec((2, rows, HD), by_head)] * parts
-        + [pl.BlockSpec((2, own, HD), by_head), pl.BlockSpec((2, extra, HD), by_head)],
+        in_specs=[block_spec(4, rows, b.shape[2]) for b in blocks]
+        + [block_spec(2, extra, coarse.shape[2])],
+        out_specs=[block_spec(2, rows, width)] * parts
+        + [block_spec(2, own, width), block_spec(2, extra, width)],
         out_shape=[jax.ShapeDtypeStruct((2, rows, width), jnp.bfloat16)] * parts
         + [
             jax.ShapeDtypeStruct((2, own, width), jnp.float32),
@@ -102,69 +106,114 @@
     rows, columns = queries.shape
     own = rows * parts
     pool_size = own // CROWS
+    per = rows // pool_size
     width = columns // parts
     heads = width // HD
-    groups = 2 if heads % 2 == 0 else 1
-    span = width // groups
+    split = [heads - heads // 2, heads // 2][: min(heads, 2)]
+    groups = len(split)
+    starts = [sum(split[:g]) for g in range(groups)]
+    far = range(2, parts)
     arrays = (keys_in, values_in, queries, grad_out)
 
-    def pooled(x):
-        return jnp.mean(x.astype(jnp.float32).reshape(rows // pool_size, pool_size, columns), axis=1)
-
-    pooled_here = jnp.stack([pooled(keys_in), pooled(values_in)], axis=0)
-
-    def column(part, group=0):
-        return (me ^ part) * width + group * span
-
+    def column(part, head=0):
+        return (me ^ part) * width + head * HD
+
+    def slab(part, head, size):
+        return jnp.stack(
+            [lax.dynamic_slice_in_dim(x, column(part, head), size, axis=1) for x in arrays]
+        )
+
+    landed = {}
+
+    def send(block, part, name):
+        landed[name] = swapped(block, "head", part)
+
+    def after(block, names):
+        for name in names:
+            if name in landed:
+                block, landed[name] = lax.optimization_barrier((block, landed[name]))
+        return block
+
+    slabs = [[slab(part, starts[g], split[g] * HD) for part in far] for g in range(groups)]
+    *slabs[0], keys_now, values_now = lax.optimization_barrier((*slabs[0], keys_in, values_in))
+    pooled_here = jnp.stack(
+        [
+            jnp.mean(x.astype(jnp.float32).reshape(per, pool_size, columns), axis=1)
+            for x in (keys_now, values_now)
+        ]
+    )
     pooled_parts = []
     for part in range(parts):
         block = lax.dynamic_slice_in_dim(pooled_here, column(part), width, axis=2)
         pooled_parts.append(swapped(block, "head", part) if part else block)
     mean_now = jnp.concatenate(pooled_parts, axis=1)
-
-    blocks = []
-    for group in range(groups):
-        here = []
-        for part in range(parts):
-            block = jnp.stack(
-                [lax.dynamic_slice_in_dim(x, column(part, group), span, axis=1) for x in arrays]
-            )
-            here.append(swapped(block, "head", part) if part else block)
-        blocks.append(here)
-
     siblings = []
     for level in range(depth):
         received = swapped(mean_now, "seq", 1 << level)
         siblings.append(received)
         mean_now = 0.5 * (mean_now + received)
+
+    blocks = []
+    for g in range(groups):
+        if g:
+            at = min(1, depth - 1)
+            *slabs[g], siblings[at] = lax.optimization_barrier((*slabs[g], siblings[at]))
+        for part in far:
+            send(slabs[g][part - 2], part, ("in", g, part))
+        size = split[g] * HD
+        blocks.append([slab(0, starts[g], size), swapped(slab(1, starts[g], size), "head", 1)])
     coarse = jnp.concatenate(siblings, axis=1).astype(jnp.bfloat16)
 
+    kept, grads, sums = [], [], []
+    for g in range(groups):
+        here = blocks[g] + [landed["in", g, part] for part in far]
+        sent, local, coarse_grad = attention(here, coarse, starts[g], split[g], depth, pool_size)
+        kept.append(sent)
+        grads.append(local)
+        sums.append(coarse_grad)
+    for g in range(groups):
+        for part in far:
+            send(kept[g][part], part, ("mid", g, part))
+    coarse_grad = jnp.concatenate(sums, axis=2).reshape(2, depth, CROWS, width)
+    order = [("mid", g, part) for g in range(groups) for part in (2, 3)]
+    pace = [[name] for name in order] + [[]] * depth
+    coarse_grad = after(coarse_grad, pace[0])
+    above = jnp.zeros((2, CROWS, width), jnp.float32)
+    for level in reversed(range(depth)):
+        outgoing = coarse_grad[:, level] + 0.5 * above
+        received = swapped(outgoing.astype(jnp.bfloat16), "seq", 1 << level)
+        received = after(received, pace[depth - level])
+        above = 0.5 * above + received.astype(jnp.float32)
+    above = above / float(pool_size)
+
+    def total(part):
+        spread = jnp.repeat(above[:, part * per : (part + 1) * per], pool_size, axis=1)
+        local = jnp.concatenate([g[:, part * rows : (part + 1) * rows] for g in grads], axis=2)
+        return (local + spread).astype(jnp.bfloat16)
+
+    near = [swapped(kept[g][1], "head", 1) for g in range(groups)]
+    last = [total(part) for part in far]
+    near_last = swapped(total(1), "head", 1)
+    for part in far:
+        send(last[part - 2], part, ("last", 0, part))
+
     outs = [jnp.zeros((rows, columns), jnp.bfloat16) for _ in range(4)]
-    for group in range(groups):
-        sent, local, coarse_grad = attention(
-            blocks[group], coarse, group * (heads // groups), depth, pool_size
-        )
-        coarse_grad = coarse_grad.reshape(2, depth, CROWS, span)
-        for part in range(parts):
-            back = swapped(sent[part], "head", part) if part else sent[part]
-            for which in range(2):
-                outs[which] = lax.dynamic_update_slice(
-                    outs[which], back[which], (0, column(part, group))
-                )
-        above = jnp.zeros((2, CROWS, span), jnp.float32)
-        for level in reversed(range(depth)):
-            outgoing = coarse_grad[:, level] + 0.5 * above
-            above = 0.5 * above + swapped(outgoing, "seq", 1 << level)
-        above = above / float(pool_size)
-        per = rows // pool_size
-        for part in range(parts):
-            spread = jnp.repeat(above[:, part * per : (part + 1) * per], pool_size, axis=1)
-            total = (local[:, part * rows : (part + 1) * rows] + spread).astype(jnp.bfloat16)
-            back = swapped(total, "head", part) if part else total
-            for which in range(2):
-                outs[2 + which] = lax.dynamic_update_slice(
-                    outs[2 + which], back[which], (0, column(part, group))
-                )
+
+    def place(first, back, part, head=0):
+        for which in range(back.shape[0]):
+            outs[first + which] = lax.dynamic_update_slice(
+                outs[first + which], back[which], (0, column(part, head))
+            )
+
+    for g in range(groups):
+        place(0, kept[g][0], 0, starts[g])
+        place(0, near[g], 1, starts[g])
+        for part in far:
+            place(0, landed["mid", g, part], part, starts[g])
+    place(2, total(0), 0)
+    place(2, near_last, 1)
+    for part in far:
+        place(2, landed["last", 0, part], part)
     return tuple(outs)
 
 

time: 122 us -> 106 us (0.87)
  starting transfers between devices: 43 us -> 24 us
  waiting for transfers between devices: 55.9 us -> 60 us
  other arithmetic: 4.56 us -> 1.76 us
    ppermute x30 -> x24, starting transfers between devices: 43 us -> 24 us  [swapped(): return lax.ppermute(block, axis, [(i, i ^ mask) for i in range(count)])]
    ppermute x30 -> x24, waiting for transfers between devices: 55.9 us -> 60 us  [swapped(): return lax.ppermute(block, axis, [(i, i ^ mask) for i in range(count)])]
    reduce_sum x2, other arithmetic: 3.14 us -> 0.53 us  [on_device(): jnp.mean(x.astype(jnp.float32).reshape(per, pool_size, columns), axis=1)]
    another operation x6, local copies, waits for them, and re-layouts: 0.98 us -> 2.62 us  [the longest x2 2.23 us: slab(): jnp.stack([lax.dynamic_slice_in_dim(x, column(part, head), size, axis=1)...]
    unnamed x16 -> x12, local copies, waits for them, and re-layouts: 2.52 us -> 1.59 us
  transfers between devices with their start and end apart: 30 -> 24, of which waited for: 15 -> 14; matrix products, arithmetic and copies ran while one was open for 2% -> 2% of each run, Pallas kernels for 11% -> 13%
where the time goes in v2:
time: 106 us; the launch traced here: 105 us
  waiting for transfers between devices  60 us (57%)
  starting transfers between devices  24 us (23%)
  Pallas kernels  13.5 us (13%)
  local copies, waits for them, and re-layouts  4.98 us (5%)
  other arithmetic  1.76 us (2%)
  between operations  1.15 us (1%)
    ppermute x24, waiting for transfers between devices, swapped(): return lax.ppermute(block, axis, [(i, i ^ mask) for i in range(count)])  60 us
    ppermute x24, starting transfers between devices, swapped(): return lax.ppermute(block, axis, [(i, i ^ mask) for i in range(count)])  24 us
    pallas_call x2, Pallas kernels, attention(): pl.pallas_call(functools.partial(attention_kernel, parts, depth, pool_siz...  13.5 us
    another operation x2, local copies, waits for them, and re-layouts, slab(): jnp.stack([lax.dynamic_slice_in_dim(x, column(part, head), size, axis=1)...  2.23 us
  transfers between devices with their start and end apart: 24, of which 14 were waited for; matrix products, arithmetic and copies ran while one was open for 2% of the time, Pallas kernels for 13%

profile of v2, /device:TPU:1, one launch (start us, length us, event | category | flops | bytes accessed | tf_op | source)
XLA Modules:
  0.0 105.4 jit_solution(4735375602232013313)
XLA Ops:
  0.7 1.9 %dynamic-slice_bitcast_fusion = (bf16[1,128,512]{2,1,0:T(8,128)(2,1)S(1)}, bf16[1,128,512]{2,1,0:T(8,128)(2,1)S(1)}, bf16[1,128,512]{2,1,0:T(8,128)(2,1)S(1)}, b...) fusion(bf16[128,4096]{1,0:T(8,128)(2,1)} %param.7, ...), kind=kLoop, calls=%fused_computation.75 | loop fusion | bytes 4194336 | tf_op jit(solution)/shard_map/stack | solution.py:122
  4.2 2.7 %collective-permute-start.4 = (f32[2,4,1024]{2,1,0:T(4,128)S(1)}, f32[2,4,1024]{2,1,0:T(4,128)S(1)}, u32[]{:S(2)}, u32[]{:S(2)}) collective-permute-start(f32[2,4,1024]{2,1,0:T(4,128)S(1)} %get-tuple-element.126), channel_id=1, source_target_pairs={{0,2},{1,3},{2,0},{3,1},{4,6},{5,7},{6,4},{7,5},{8,10},{9,11},{10,... | collective-permute-start | bytes 98312 | tf_op jit(solution)/shard_map/ppermute | solution.py:18
  7.4 1.4 %collective-permute-start.1 = (bf16[4,128,512]{2,1,0:T(8,128)(2,1)S(1)}, bf16[4,128,512]{2,1,0:T(8,128)(2,1)S(1)}, u32[]{:S(2)}, u32[]{:S(2)}) collective-permute-start(bf16[4,128,512]{2,1,0:T(8,128)(2,1)S(1)} %pad_maximum_fusion.2), channel_id=1, source_target_pairs={{0,2},{1,3},{2,0},{3,1},{4,6},{5,7},{6,4},{7,5},{8,10},{9,11},{10,... | collective-permute-start | bytes 1572872 | tf_op jit(solution)/shard_map/ppermute | solution.py:18
  9.2 1.3 %collective-permute-done.5 = f32[2,4,1024]{2,1,0:T(4,128)S(1)} collective-permute-done((f32[2,4,1024]{2,1,0:T(4,128)S(1)}, f32[2,4,1024]{2,1,0:T(4,128)S(1)}, u32[]{:S(2)}, u32[]{:S(2)}) %collective-permute-start.5) | collective-permute-done | bytes 32800 | tf_op jit(solution)/shard_map/ppermute | solution.py:18
  10.6 1.1 %collective-permute-start.6 = (f32[2,16,1024]{2,1,0:T(8,128)S(1)}, f32[2,16,1024]{2,1,0:T(8,128)S(1)}, u32[]{:S(2)}, u32[]{:S(2)}) collective-permute-start(f32[2,16,1024]{2,1,0:T(8,128)S(1)} %pad_maximum_fusion.10), channel_id=1, source_target_pairs={{0,4},{4,0},{8,12},{12,8},{16,20},{20,16},{24,28},{28,24},{1,5},{5... | collective-permute-start | bytes 393224 | tf_op jit(solution)/shard_map/ppermute | solution.py:18
  12.4 3.4 %collective-permute-done.6 = f32[2,16,1024]{2,1,0:T(8,128)S(1)} collective-permute-done((f32[2,16,1024]{2,1,0:T(8,128)S(1)}, f32[2,16,1024]{2,1,0:T(8,128)S(1)}, u32[]{:S(2)}, u32[]{:S(2)}) %collective-permute-start.6) | collective-permute-done | bytes 131104 | tf_op jit(solution)/shard_map/ppermute | solution.py:18
  16.9 3.2 %collective-permute-done.7 = f32[2,16,1024]{2,1,0:T(8,128)S(1)} collective-permute-done((f32[2,16,1024]{2,1,0:T(8,128)S(1)}, f32[2,16,1024]{2,1,0:T(8,128)S(1)}, u32[]{:S(2)}, u32[]{:S(2)}) %collective-permute-start.7) | collective-permute-done | bytes 131104 | tf_op jit(solution)/shard_map/ppermute | solution.py:18
  20.1 1.8 %collective-permute-start.8 = (bf16[2,16,1024]{2,1,0:T(8,128)(2,1)S(1)}, bf16[2,16,1024]{2,1,0:T(8,128)(2,1)S(1)}, u32[]{:S(2)}, u32[]{:S(2)}) collective-permute-start(bf16[2,16,1024]{2,1,0:T(8,128)(2,1)S(1)} %add_multiply_fusion.2), channel_id=1, source_target_pairs={{0,16},{4,20},{8,24},{12,28},{16,0},{20,4},{24,8},{28,12},{1,17},{... | collective-permute-start | bytes 196616 | tf_op jit(solution)/shard_map/ppermute | solution.py:18
  22.0 2.9 %collective-permute-done.8 = bf16[2,16,1024]{2,1,0:T(8,128)(2,1)S(1)} collective-permute-done((bf16[2,16,1024]{2,1,0:T(8,128)(2,1)S(1)}, bf16[2,16,1024]{2,1,0:T(8,128)(2,1)S(1)}, u32[]{:S(2)}, u32[]{:S(2)}) %collective-permute-start.8) | collective-permute-done | bytes 65568 | tf_op jit(solution)/shard_map/ppermute | solution.py:18
  24.9 3.8 %collective-permute-start.12 = (bf16[4,128,512]{2,1,0:T(8,128)(2,1)S(1)}, bf16[4,128,512]{2,1,0:T(8,128)(2,1)S(1)}, u32[]{:S(2)}, u32[]{:S(2)}) collective-permute-start(bf16[4,128,512]{2,1,0:T(8,128)(2,1)S(1)} %pad_maximum_fusion.5), channel_id=1, source_target_pairs={{0,3},{1,2},{2,1},{3,0},{4,7},{5,6},{6,5},{7,4},{8,11},{9,10},{10,... | collective-permute-start | bytes 1572872 | tf_op jit(solution)/shard_map/ppermute | solution.py:18
  28.8 4.2 %collective-permute-done.2.refs_3_ = bf16[4,128,512]{2,1,0:T(8,128)(2,1)S(1)} collective-permute-done((bf16[4,128,512]{2,1,0:T(8,128)(2,1)S(1)}, bf16[4,128,512]{2,1,0:T(8,128)(2,1)S(1)}, u32[]{:S(2)}, u32[]{:S(2)}) %collective-permute-start.2) | collective-permute-done | bytes 524320 | tf_op jit(solution)/shard_map/ppermute | solution.py:18
  33.0 6.7 %attention.2 = (bf16[2,128,512]{2,1,0:T(8,128)(2,1)S(1)}, bf16[2,128,512]{2,1,0:T(8,128)(2,1)S(1)}, bf16[2,128,512]{2,1,0:T(8,128)(2,1)S(1)}, bf16[2,128,512]{2,...) custom-call(bf16[4,128,512]{2,1,0:T(8,128)(2,1)S(1)} %pad_maximum_fusion.refs_0_, ...), custom_call_target="tpu_custom_call" | custom-call | flops 1761607680 | bytes 6291456 | tf_op jit(solution)/shard_map/attention/pallas_call | solution.py:78
  39.7 1.6 %collective-permute-start.13 = (bf16[2,128,512]{2,1,0:T(8,128)(2,1)S(1)}, bf16[2,128,512]{2,1,0:T(8,128)(2,1)S(1)}, u32[]{:S(2)}, u32[]{:S(2)}) collective-permute-start(bf16[2,128,512]{2,1,0:T(8,128)(2,1)S(1)} %get-tuple-element.42), channel_id=1, source_target_pairs={{0,2},{1,3},{2,0},{3,1},{4,6},{5,7},{6,4},{7,5},{8,10},{9,11},{10,... | collective-permute-start | bytes 786440 | tf_op jit(solution)/shard_map/ppermute | solution.py:18
  41.8 1.3 %collective-permute-done.9 = bf16[2,128,512]{2,1,0:T(8,128)(2,1)S(1)} collective-permute-done((bf16[2,128,512]{2,1,0:T(8,128)(2,1)S(1)}, bf16[2,128,512]{2,1,0:T(8,128)(2,1)S(1)}, u32[]{:S(2)}, u32[]{:S(2)}) %collective-permute-start.9) | collective-permute-done | bytes 262176 | tf_op jit(solution)/shard_map/ppermute | solution.py:18
  43.8 11.6 %collective-permute-done.12.refs_3_ = bf16[4,128,512]{2,1,0:T(8,128)(2,1)S(1)} collective-permute-done((bf16[4,128,512]{2,1,0:T(8,128)(2,1)S(1)}, bf16[4,128,512]{2,1,0:T(8,128)(2,1)S(1)}, u32[]{:S(2)}, u32[]{:S(2)}) %collective-permute-start.12) | collective-permute-done | bytes 524320 | tf_op jit(solution)/shard_map/ppermute | solution.py:18
  55.5 6.7 %attention.3 = (bf16[2,128,512]{2,1,0:T(8,128)(2,1)S(1)}, bf16[2,128,512]{2,1,0:T(8,128)(2,1)S(1)}, bf16[2,128,512]{2,1,0:T(8,128)(2,1)S(1)}, bf16[2,128,512]{2,...) custom-call(bf16[4,128,512]{2,1,0:T(8,128)(2,1)S(1)} %pad_maximum_fusion.6.refs_0_, ...), custom_call_target="tpu_custom_call" | custom-call | flops 1761607680 | bytes 6291456 | tf_op jit(solution)/shard_map/attention/pallas_call | solution.py:78
  62.3 2.7 %collective-permute-start.14 = (bf16[2,16,1024]{2,1,0:T(8,128)(2,1)S(1)}, bf16[2,16,1024]{2,1,0:T(8,128)(2,1)S(1)}, u32[]{:S(2)}, u32[]{:S(2)}) collective-permute-start(bf16[2,16,1024]{2,1,0:T(8,128)(2,1)S(1)} %fusion.20), channel_id=1, source_target_pairs={{0,16},{4,20},{8,24},{12,28},{16,0},{20,4},{24,8},{28,12},{1,17},{... | collective-permute-start | bytes 196616 | tf_op jit(solution)/shard_map/ppermute | solution.py:18
  64.9 1.2 %collective-permute-start.18 = (bf16[2,128,512]{2,1,0:T(8,128)(2,1)S(1)}, bf16[2,128,512]{2,1,0:T(8,128)(2,1)S(1)}, u32[]{:S(2)}, u32[]{:S(2)}) collective-permute-start(bf16[2,128,512]{2,1,0:T(8,128)(2,1)S(1)} %get-tuple-element.50), channel_id=1, source_target_pairs={{0,2},{1,3},{2,0},{3,1},{4,6},{5,7},{6,4},{7,5},{8,10},{9,11},{10,... | collective-permute-start | bytes 786440 | tf_op jit(solution)/shard_map/ppermute | solution.py:18
  67.1 1.7 %collective-permute-done.14 = bf16[2,16,1024]{2,1,0:T(8,128)(2,1)S(1)} collective-permute-done((bf16[2,16,1024]{2,1,0:T(8,128)(2,1)S(1)}, bf16[2,16,1024]{2,1,0:T(8,128)(2,1)S(1)}, u32[]{:S(2)}, u32[]{:S(2)}) %collective-permute-start.14) | collective-permute-done | bytes 65568 | tf_op jit(solution)/shard_map/ppermute | solution.py:18
  69.6 2.7 %collective-permute-done.17 = bf16[2,16,1024]{2,1,0:T(8,128)(2,1)S(1)} collective-permute-done((bf16[2,16,1024]{2,1,0:T(8,128)(2,1)S(1)}, bf16[2,16,1024]{2,1,0:T(8,128)(2,1)S(1)}, u32[]{:S(2)}, u32[]{:S(2)}) %collective-permute-start.17) | collective-permute-done | bytes 65568 | tf_op jit(solution)/shard_map/ppermute | solution.py:18
  72.9 1.3 %collective-permute-start.19 = (bf16[2,16,1024]{2,1,0:T(8,128)(2,1)S(1)}, bf16[2,16,1024]{2,1,0:T(8,128)(2,1)S(1)}, u32[]{:S(2)}, u32[]{:S(2)}) collective-permute-start(bf16[2,16,1024]{2,1,0:T(8,128)(2,1)S(1)} %fusion.15), channel_id=1, source_target_pairs={{0,4},{4,0},{8,12},{12,8},{16,20},{20,16},{24,28},{28,24},{1,5},{5... | collective-permute-start | bytes 196616 | tf_op jit(solution)/shard_map/ppermute | solution.py:18
  74.3 4.3 %collective-permute-done.20 = bf16[2,128,512]{2,1,0:T(8,128)(2,1)S(1)} collective-permute-done((bf16[2,128,512]{2,1,0:T(8,128)(2,1)S(1)}, bf16[2,128,512]{2,1,0:T(8,128)(2,1)S(1)}, u32[]{:S(2)}, u32[]{:S(2)}) %collective-permute-start.20) | collective-permute-done | bytes 262176 | tf_op jit(solution)/shard_map/ppermute | solution.py:18
  78.8 1.6 %collective-permute-start.23 = (bf16[2,128,1024]{2,1,0:T(8,128)(2,1)S(1)}, bf16[2,128,1024]{2,1,0:T(8,128)(2,1)S(1)}, u32[]{:S(2)}, u32[]{:S(2)}) collective-permute-start(bf16[2,128,1024]{2,1,0:T(8,128)(2,1)S(1)} %fusion.3), channel_id=1, source_target_pairs={{0,3},{1,2},{2,1},{3,0},{4,7},{5,6},{6,5},{7,4},{8,11},{9,10},{10,... | collective-permute-start | bytes 1572872 | tf_op jit(solution)/shard_map/ppermute | solution.py:18
  82.9 21.1 %collective-permute-done.22 = bf16[2,128,1024]{2,1,0:T(8,128)(2,1)S(1)} collective-permute-done((bf16[2,128,1024]{2,1,0:T(8,128)(2,1)S(1)}, bf16[2,128,1024]{2,1,0:T(8,128)(2,1)S(1)}, u32[]{:S(2)}, u32[]{:S(2)}) %collective-permute-start.22) | collective-permute-done | bytes 524320 | tf_op jit(solution)/shard_map/ppermute | solution.py:18
  (88 shorter events, 11.9 us)
Async XLA Ops:
  4.0 4.8 %collective-permute-start.3 = (f32[2,4,1024]{2,1,0:T(4,128)S(1)}, f32[2,4,1024]{2,1,0:T(4,128)S(1)}, u32[]{:S(2)}, u32[]{:S(2)}) collective-permute-start(f32[2,4,1024]{2,1,0:T(4,128)S(1)} %get-tuple-element.125), channel_id=1, source_target_pairs={{0,1},{1,0},{2,3},{3,2},{4,5},{5,4},{6,7},{7,6},{8,9},{9,8},{10,11... | collective-permute-start | bytes 98312 | tf_op jit(solution)/shard_map/ppermute | solution.py:18
  4.2 5.0 %collective-permute-start.4 = (f32[2,4,1024]{2,1,0:T(4,128)S(1)}, f32[2,4,1024]{2,1,0:T(4,128)S(1)}, u32[]{:S(2)}, u32[]{:S(2)}) collective-permute-start(f32[2,4,1024]{2,1,0:T(4,128)S(1)} %get-tuple-element.126), channel_id=1, source_target_pairs={{0,2},{1,3},{2,0},{3,1},{4,6},{5,7},{6,4},{7,5},{8,10},{9,11},{10,... | collective-permute-start | bytes 98312 | tf_op jit(solution)/shard_map/ppermute | solution.py:18
  6.8 3.7 %collective-permute-start.5 = (f32[2,4,1024]{2,1,0:T(4,128)S(1)}, f32[2,4,1024]{2,1,0:T(4,128)S(1)}, u32[]{:S(2)}, u32[]{:S(2)}) collective-permute-start(f32[2,4,1024]{2,1,0:T(4,128)S(1)} %get-tuple-element.127), channel_id=1, source_target_pairs={{0,3},{1,2},{2,1},{3,0},{4,7},{5,6},{6,5},{7,4},{8,11},{9,10},{10,... | collective-permute-start | bytes 98312 | tf_op jit(solution)/shard_map/ppermute | solution.py:18
  6.9 36.4 %collective-permute-start.10 = (bf16[4,128,512]{2,1,0:T(8,128)(2,1)S(1)}, bf16[4,128,512]{2,1,0:T(8,128)(2,1)S(1)}, u32[]{:S(2)}, u32[]{:S(2)}) collective-permute-start(bf16[4,128,512]{2,1,0:T(8,128)(2,1)S(1)} %pad_maximum_fusion.7), channel_id=1, source_target_pairs={{0,1},{1,0},{2,3},{3,2},{4,5},{5,4},{6,7},{7,6},{8,9},{9,8},{10,11... | collective-permute-start | bytes 1572872 | tf_op jit(solution)/shard_map/ppermute | solution.py:18
  7.4 17.5 %collective-permute-start.1 = (bf16[4,128,512]{2,1,0:T(8,128)(2,1)S(1)}, bf16[4,128,512]{2,1,0:T(8,128)(2,1)S(1)}, u32[]{:S(2)}, u32[]{:S(2)}) collective-permute-start(bf16[4,128,512]{2,1,0:T(8,128)(2,1)S(1)} %pad_maximum_fusion.2), channel_id=1, source_target_pairs={{0,2},{1,3},{2,0},{3,1},{4,6},{5,7},{6,4},{7,5},{8,10},{9,11},{10,... | collective-permute-start | bytes 1572872 | tf_op jit(solution)/shard_map/ppermute | solution.py:18
  8.8 24.2 %collective-permute-start.2 = (bf16[4,128,512]{2,1,0:T(8,128)(2,1)S(1)}, bf16[4,128,512]{2,1,0:T(8,128)(2,1)S(1)}, u32[]{:S(2)}, u32[]{:S(2)}) collective-permute-start(bf16[4,128,512]{2,1,0:T(8,128)(2,1)S(1)} %pad_maximum_fusion.3), channel_id=1, source_target_pairs={{0,3},{1,2},{2,1},{3,0},{4,7},{5,6},{6,5},{7,4},{8,11},{9,10},{10,... | collective-permute-start | bytes 1572872 | tf_op jit(solution)/shard_map/ppermute | solution.py:18
  10.6 5.2 %collective-permute-start.6 = (f32[2,16,1024]{2,1,0:T(8,128)S(1)}, f32[2,16,1024]{2,1,0:T(8,128)S(1)}, u32[]{:S(2)}, u32[]{:S(2)}) collective-permute-start(f32[2,16,1024]{2,1,0:T(8,128)S(1)} %pad_maximum_fusion.10), channel_id=1, source_target_pairs={{0,4},{4,0},{8,12},{12,8},{16,20},{20,16},{24,28},{28,24},{1,5},{5... | collective-permute-start | bytes 393224 | tf_op jit(solution)/shard_map/ppermute | solution.py:18
  11.7 21.3 %collective-permute-start = (bf16[4,128,512]{2,1,0:T(8,128)(2,1)S(1)}, bf16[4,128,512]{2,1,0:T(8,128)(2,1)S(1)}, u32[]{:S(2)}, u32[]{:S(2)}) collective-permute-start(bf16[4,128,512]{2,1,0:T(8,128)(2,1)S(1)} %pad_maximum_fusion.1), channel_id=1, source_target_pairs={{0,1},{1,0},{2,3},{3,2},{4,5},{5,4},{6,7},{7,6},{8,9},{9,8},{10,11... | collective-permute-start | bytes 1572872 | tf_op jit(solution)/shard_map/ppermute | solution.py:18
  15.8 4.3 %collective-permute-start.7 = (f32[2,16,1024]{2,1,0:T(8,128)S(1)}, f32[2,16,1024]{2,1,0:T(8,128)S(1)}, u32[]{:S(2)}, u32[]{:S(2)}) collective-permute-start(f32[2,16,1024]{2,1,0:T(8,128)S(1)} %get-tuple-element.123), channel_id=1, source_target_pairs={{0,8},{4,12},{8,0},{12,4},{16,24},{20,28},{24,16},{28,20},{1,9},{5... | collective-permute-start | bytes 393224 | tf_op jit(solution)/shard_map/ppermute | solution.py:18
  20.1 4.8 %collective-permute-start.8 = (bf16[2,16,1024]{2,1,0:T(8,128)(2,1)S(1)}, bf16[2,16,1024]{2,1,0:T(8,128)(2,1)S(1)}, u32[]{:S(2)}, u32[]{:S(2)}) collective-permute-start(bf16[2,16,1024]{2,1,0:T(8,128)(2,1)S(1)} %add_multiply_fusion.2), channel_id=1, source_target_pairs={{0,16},{4,20},{8,24},{12,28},{16,0},{20,4},{24,8},{28,12},{1,17},{... | collective-permute-start | bytes 196616 | tf_op jit(solution)/shard_map/ppermute | solution.py:18
  24.9 18.9 %collective-permute-start.11 = (bf16[4,128,512]{2,1,0:T(8,128)(2,1)S(1)}, bf16[4,128,512]{2,1,0:T(8,128)(2,1)S(1)}, u32[]{:S(2)}, u32[]{:S(2)}) collective-permute-start(bf16[4,128,512]{2,1,0:T(8,128)(2,1)S(1)} %pad_maximum_fusion.4), channel_id=1, source_target_pairs={{0,2},{1,3},{2,0},{3,1},{4,6},{5,7},{6,4},{7,5},{8,10},{9,11},{10,... | collective-permute-start | bytes 1572872 | tf_op jit(solution)/shard_map/ppermute | solution.py:18
  24.9 30.5 %collective-permute-start.12 = (bf16[4,128,512]{2,1,0:T(8,128)(2,1)S(1)}, bf16[4,128,512]{2,1,0:T(8,128)(2,1)S(1)}, u32[]{:S(2)}, u32[]{:S(2)}) collective-permute-start(bf16[4,128,512]{2,1,0:T(8,128)(2,1)S(1)} %pad_maximum_fusion.5), channel_id=1, source_target_pairs={{0,3},{1,2},{2,1},{3,0},{4,7},{5,6},{6,5},{7,4},{8,11},{9,10},{10,... | collective-permute-start | bytes 1572872 | tf_op jit(solution)/shard_map/ppermute | solution.py:18
  39.7 22.5 %collective-permute-start.13 = (bf16[2,128,512]{2,1,0:T(8,128)(2,1)S(1)}, bf16[2,128,512]{2,1,0:T(8,128)(2,1)S(1)}, u32[]{:S(2)}, u32[]{:S(2)}) collective-permute-start(bf16[2,128,512]{2,1,0:T(8,128)(2,1)S(1)} %get-tuple-element.42), channel_id=1, source_target_pairs={{0,2},{1,3},{2,0},{3,1},{4,6},{5,7},{6,4},{7,5},{8,10},{9,11},{10,... | collective-permute-start | bytes 786440 | tf_op jit(solution)/shard_map/ppermute | solution.py:18
  41.5 1.6 %collective-permute-start.9 = (bf16[2,128,512]{2,1,0:T(8,128)(2,1)S(1)}, bf16[2,128,512]{2,1,0:T(8,128)(2,1)S(1)}, u32[]{:S(2)}, u32[]{:S(2)}) collective-permute-start(bf16[2,128,512]{2,1,0:T(8,128)(2,1)S(1)} %get-tuple-element.37), channel_id=1, source_target_pairs={{0,1},{1,0},{2,3},{3,2},{4,5},{5,4},{6,7},{7,6},{8,9},{9,8},{10,11... | collective-permute-start | bytes 786440 | tf_op jit(solution)/shard_map/ppermute | solution.py:18
  43.2 23.9 %collective-permute-start.15 = (bf16[2,128,512]{2,1,0:T(8,128)(2,1)S(1)}, bf16[2,128,512]{2,1,0:T(8,128)(2,1)S(1)}, u32[]{:S(2)}, u32[]{:S(2)}) collective-permute-start(bf16[2,128,512]{2,1,0:T(8,128)(2,1)S(1)} %get-tuple-element.45), channel_id=1, source_target_pairs={{0,3},{1,2},{2,1},{3,0},{4,7},{5,6},{6,5},{7,4},{8,11},{9,10},{10,... | collective-permute-start | bytes 786440 | tf_op jit(solution)/shard_map/ppermute | solution.py:18
  62.3 6.5 %collective-permute-start.14 = (bf16[2,16,1024]{2,1,0:T(8,128)(2,1)S(1)}, bf16[2,16,1024]{2,1,0:T(8,128)(2,1)S(1)}, u32[]{:S(2)}, u32[]{:S(2)}) collective-permute-start(bf16[2,16,1024]{2,1,0:T(8,128)(2,1)S(1)} %fusion.20), channel_id=1, source_target_pairs={{0,16},{4,20},{8,24},{12,28},{16,0},{20,4},{24,8},{28,12},{1,17},{... | collective-permute-start | bytes 196616 | tf_op jit(solution)/shard_map/ppermute | solution.py:18
  64.9 8.0 %collective-permute-start.18 = (bf16[2,128,512]{2,1,0:T(8,128)(2,1)S(1)}, bf16[2,128,512]{2,1,0:T(8,128)(2,1)S(1)}, u32[]{:S(2)}, u32[]{:S(2)}) collective-permute-start(bf16[2,128,512]{2,1,0:T(8,128)(2,1)S(1)} %get-tuple-element.50), channel_id=1, source_target_pairs={{0,2},{1,3},{2,0},{3,1},{4,6},{5,7},{6,4},{7,5},{8,10},{9,11},{10,... | collective-permute-start | bytes 786440 | tf_op jit(solution)/shard_map/ppermute | solution.py:18
  66.1 12.4 %collective-permute-start.20 = (bf16[2,128,512]{2,1,0:T(8,128)(2,1)S(1)}, bf16[2,128,512]{2,1,0:T(8,128)(2,1)S(1)}, u32[]{:S(2)}, u32[]{:S(2)}) collective-permute-start(bf16[2,128,512]{2,1,0:T(8,128)(2,1)S(1)} %get-tuple-element.53), channel_id=1, source_target_pairs={{0,3},{1,2},{2,1},{3,0},{4,7},{5,6},{6,5},{7,4},{8,11},{9,10},{10,... | collective-permute-start | bytes 786440 | tf_op jit(solution)/shard_map/ppermute | solution.py:18
  66.7 7.5 %collective-permute-start.16 = (bf16[2,128,512]{2,1,0:T(8,128)(2,1)S(1)}, bf16[2,128,512]{2,1,0:T(8,128)(2,1)S(1)}, u32[]{:S(2)}, u32[]{:S(2)}) collective-permute-start(bf16[2,128,512]{2,1,0:T(8,128)(2,1)S(1)} %get-tuple-element.48), channel_id=1, source_target_pairs={{0,1},{1,0},{2,3},{3,2},{4,5},{5,4},{6,7},{7,6},{8,9},{9,8},{10,11... | collective-permute-start | bytes 786440 | tf_op jit(solution)/shard_map/ppermute | solution.py:18
  68.8 3.5 %collective-permute-start.17 = (bf16[2,16,1024]{2,1,0:T(8,128)(2,1)S(1)}, bf16[2,16,1024]{2,1,0:T(8,128)(2,1)S(1)}, u32[]{:S(2)}, u32[]{:S(2)}) collective-permute-start(bf16[2,16,1024]{2,1,0:T(8,128)(2,1)S(1)} %fusion.17), channel_id=1, source_target_pairs={{0,8},{4,12},{8,0},{12,4},{16,24},{20,28},{24,16},{28,20},{1,9},{5... | collective-permute-start | bytes 196616 | tf_op jit(solution)/shard_map/ppermute | solution.py:18
  72.9 5.6 %collective-permute-start.19 = (bf16[2,16,1024]{2,1,0:T(8,128)(2,1)S(1)}, bf16[2,16,1024]{2,1,0:T(8,128)(2,1)S(1)}, u32[]{:S(2)}, u32[]{:S(2)}) collective-permute-start(bf16[2,16,1024]{2,1,0:T(8,128)(2,1)S(1)} %fusion.15), channel_id=1, source_target_pairs={{0,4},{4,0},{8,12},{12,8},{16,20},{20,16},{24,28},{28,24},{1,5},{5... | collective-permute-start | bytes 196616 | tf_op jit(solution)/shard_map/ppermute | solution.py:18
  78.8 25.2 %collective-permute-start.23 = (bf16[2,128,1024]{2,1,0:T(8,128)(2,1)S(1)}, bf16[2,128,1024]{2,1,0:T(8,128)(2,1)S(1)}, u32[]{:S(2)}, u32[]{:S(2)}) collective-permute-start(bf16[2,128,1024]{2,1,0:T(8,128)(2,1)S(1)} %fusion.3), channel_id=1, source_target_pairs={{0,3},{1,2},{2,1},{3,0},{4,7},{5,6},{6,5},{7,4},{8,11},{9,10},{10,... | collective-permute-start | bytes 1572872 | tf_op jit(solution)/shard_map/ppermute | solution.py:18
  80.5 23.5 %collective-permute-start.22 = (bf16[2,128,1024]{2,1,0:T(8,128)(2,1)S(1)}, bf16[2,128,1024]{2,1,0:T(8,128)(2,1)S(1)}, u32[]{:S(2)}, u32[]{:S(2)}) collective-permute-start(bf16[2,128,1024]{2,1,0:T(8,128)(2,1)S(1)} %fusion.2), channel_id=1, source_target_pairs={{0,2},{1,3},{2,0},{3,1},{4,6},{5,7},{6,4},{7,5},{8,10},{9,11},{10,... | collective-permute-start | bytes 1572872 | tf_op jit(solution)/shard_map/ppermute | solution.py:18
  80.8 2.1 %collective-permute-start.21 = (bf16[2,128,1024]{2,1,0:T(8,128)(2,1)S(1)}, bf16[2,128,1024]{2,1,0:T(8,128)(2,1)S(1)}, u32[]{:S(2)}, u32[]{:S(2)}) collective-permute-start(bf16[2,128,1024]{2,1,0:T(8,128)(2,1)S(1)} %fusion.1), channel_id=1, source_target_pairs={{0,1},{1,0},{2,3},{3,2},{4,5},{5,4},{6,7},{7,6},{8,9},{9,8},{10,11... | collective-permute-start | bytes 1572872 | tf_op jit(solution)/shard_map/ppermute | solution.py:18
  (6 other events, 51.3 us)

commit v3 on v2

--- a/solution.py
+++ b/solution.py
@@ -11,6 +11,11 @@
 HD = 128
 CROWS = 16
 SCALE = HD**-0.5
+FIRST = 1
+IN_GATE = 2
+PACE0 = ((), (), (), ())
+PACE1 = ((("mid", 0, 2),), (("mid", 0, 3),), (("last", 0, 2),), (("last", 0, 3),))
+F_PACE = ((("in", 0, 2, 0),), (), (("near", 1),))
 
 
 def swapped(block, axis, mask):
@@ -18,16 +23,24 @@
     return lax.ppermute(block, axis, [(i, i ^ mask) for i in range(count)])
 
 
-def attention_kernel(parts, depth, pool_size, *refs):
-    blocks = refs[:parts]
-    coarse_ref = refs[parts]
-    out_refs = refs[parts + 1 : 2 * parts + 1]
-    local_ref, coarse_grad_ref = refs[2 * parts + 1 :]
-    rows = blocks[0].shape[1]
+def attention_kernel(layout, depth, pool_size, *refs):
+    parts, count = len(layout), sum(layout)
+    blocks = []
+    for pieces in layout:
+        at = sum(len(b) for b in blocks)
+        blocks.append(refs[at : at + pieces])
+    coarse_ref = refs[count]
+    out_refs = refs[count + 1 : count + 1 + parts]
+    local_ref, coarse_grad_ref = refs[count + 1 + parts :]
+    rows = refs[0].shape[1]
     own = parts * rows
 
     def whole(which):
-        return jnp.concatenate([b[which] for b in blocks], axis=0)
+        taken = []
+        for pieces in blocks:
+            each = 4 // len(pieces)
+            taken.append(pieces[which // each][which % each])
+        return jnp.concatenate(taken, axis=0)
 
     keys = jnp.concatenate([whole(0), coarse_ref[0]], axis=0)
     values = jnp.concatenate([whole(1), coarse_ref[1]], axis=0)
@@ -65,7 +78,9 @@
 
 def attention(blocks, coarse, first, heads, depth, pool_size):
     parts = len(blocks)
-    rows = blocks[0].shape[1]
+    layout = tuple(len(pieces) for pieces in blocks)
+    flat = [piece for pieces in blocks for piece in pieces]
+    rows = flat[0].shape[1]
     width = heads * HD
     own = parts * rows
     extra = coarse.shape[1]
@@ -76,9 +91,9 @@
         return pl.BlockSpec((lead, height, HD), lambda h: (0, 0, skip + h))
 
     outs = pl.pallas_call(
-        functools.partial(attention_kernel, parts, depth, pool_size),
+        functools.partial(attention_kernel, layout, depth, pool_size),
         grid=(heads,),
-        in_specs=[block_spec(4, rows, b.shape[2]) for b in blocks]
+        in_specs=[block_spec(b.shape[0], rows, b.shape[2]) for b in flat]
         + [block_spec(2, extra, coarse.shape[2])],
         out_specs=[block_spec(2, rows, width)] * parts
         + [block_spec(2, own, width), block_spec(2, extra, width)],
@@ -94,7 +109,7 @@
             transcendentals=heads * own * seen,
         ),
         name="attention",
-    )(*blocks, coarse)
+    )(*flat, coarse)
     return outs[:parts], outs[parts], outs[parts + 1]
 
 
@@ -134,8 +149,12 @@
                 block, landed[name] = lax.optimization_barrier((block, landed[name]))
         return block
 
-    slabs = [[slab(part, starts[g], split[g] * HD) for part in far] for g in range(groups)]
-    *slabs[0], keys_now, values_now = lax.optimization_barrier((*slabs[0], keys_in, values_in))
+    def pieces(part, g):
+        whole = slab(part, starts[g], split[g] * HD)
+        return [whole[:2], whole[2:]] if g == 0 and 2 <= part < 2 + FIRST else [whole]
+
+    slabs = [[pieces(part, g) for part in far] for g in range(groups)]
+    slabs[0], keys_now, values_now = lax.optimization_barrier((slabs[0], keys_in, values_in))
     pooled_here = jnp.stack(
         [
             jnp.mean(x.astype(jnp.float32).reshape(per, pool_size, columns), axis=1)
@@ -146,56 +165,68 @@
     for part in range(parts):
         block = lax.dynamic_slice_in_dim(pooled_here, column(part), width, axis=2)
         pooled_parts.append(swapped(block, "head", part) if part else block)
+    for part in far[:FIRST]:
+        send(slabs[0][part - 2][0], part, ("in", 0, part, 0))
     mean_now = jnp.concatenate(pooled_parts, axis=1)
+    for g in range(groups):
+        send(slab(1, starts[g], split[g] * HD), 1, ("near", g))
     siblings = []
     for level in range(depth):
+        if level < len(F_PACE):
+            mean_now = after(mean_now, F_PACE[level])
         received = swapped(mean_now, "seq", 1 << level)
         siblings.append(received)
         mean_now = 0.5 * (mean_now + received)
 
     blocks = []
     for g in range(groups):
-        if g:
-            at = min(1, depth - 1)
-            *slabs[g], siblings[at] = lax.optimization_barrier((*slabs[g], siblings[at]))
-        for part in far:
-            send(slabs[g][part - 2], part, ("in", g, part))
-        size = split[g] * HD
-        blocks.append([slab(0, starts[g], size), swapped(slab(1, starts[g], size), "head", 1)])
+        if g and IN_GATE:
+            at = min(IN_GATE, depth) - 1
+            slabs[g], siblings[at] = lax.optimization_barrier((slabs[g], siblings[at]))
+        for part in far:
+            for at, piece in enumerate(slabs[g][part - 2]):
+                if ("in", g, part, at) not in landed:
+                    send(piece, part, ("in", g, part, at))
+        blocks.append([[slab(0, starts[g], split[g] * HD)], [landed["near", g]]])
     coarse = jnp.concatenate(siblings, axis=1).astype(jnp.bfloat16)
 
     kept, grads, sums = [], [], []
     for g in range(groups):
-        here = blocks[g] + [landed["in", g, part] for part in far]
+        blocks[g][1] = [landed["near", g]]
+        here = blocks[g] + [
+            [landed["in", g, part, at] for at in range(len(slabs[g][part - 2]))] for part in far
+        ]
         sent, local, coarse_grad = attention(here, coarse, starts[g], split[g], depth, pool_size)
         kept.append(sent)
         grads.append(local)
-        sums.append(coarse_grad)
-    for g in range(groups):
-        for part in far:
-            send(kept[g][part], part, ("mid", g, part))
-    coarse_grad = jnp.concatenate(sums, axis=2).reshape(2, depth, CROWS, width)
-    order = [("mid", g, part) for g in range(groups) for part in (2, 3)]
-    pace = [[name] for name in order] + [[]] * depth
-    coarse_grad = after(coarse_grad, pace[0])
-    above = jnp.zeros((2, CROWS, width), jnp.float32)
-    for level in reversed(range(depth)):
-        outgoing = coarse_grad[:, level] + 0.5 * above
-        received = swapped(outgoing.astype(jnp.bfloat16), "seq", 1 << level)
-        received = after(received, pace[depth - level])
-        above = 0.5 * above + received.astype(jnp.float32)
-    above = above / float(pool_size)
-
-    def total(part):
+        sums.append(coarse_grad.reshape(2, depth, CROWS, split[g] * HD))
+        for part in far:
+            send(sent[part], part, ("mid", g, part))
+
+    def chain(coarse_grad, pace):
+        pace = list(pace) + [()] * depth
+        coarse_grad = after(coarse_grad, pace[0])
+        above = jnp.zeros(coarse_grad[:, 0].shape, jnp.float32)
+        for level in reversed(range(depth)):
+            outgoing = coarse_grad[:, level] + 0.5 * above
+            received = swapped(outgoing.astype(jnp.bfloat16), "seq", 1 << level)
+            received = after(received, pace[depth - level])
+            above = 0.5 * above + received.astype(jnp.float32)
+        return above / float(pool_size)
+
+    def total(part, local, above):
         spread = jnp.repeat(above[:, part * per : (part + 1) * per], pool_size, axis=1)
-        local = jnp.concatenate([g[:, part * rows : (part + 1) * rows] for g in grads], axis=2)
-        return (local + spread).astype(jnp.bfloat16)
-
+        return (local[:, part * rows : (part + 1) * rows] + spread).astype(jnp.bfloat16)
+
+    own_last, near_last = [], []
+    for g in range(groups):
+        above = chain(sums[g], (PACE0, PACE1)[g])
+        for part in far:
+            send(total(part, grads[g], above), part, ("last", g, part))
+        own_last.append(total(0, grads[g], above))
+        near_last.append(total(1, grads[g], above))
     near = [swapped(kept[g][1], "head", 1) for g in range(groups)]
-    last = [total(part) for part in far]
-    near_last = swapped(total(1), "head", 1)
-    for part in far:
-        send(last[part - 2], part, ("last", 0, part))
+    near_last = [swapped(block, "head", 1) for block in near_last]
 
     outs = [jnp.zeros((rows, columns), jnp.bfloat16) for _ in range(4)]
 
@@ -208,12 +239,11 @@
     for g in range(groups):
         place(0, kept[g][0], 0, starts[g])
         place(0, near[g], 1, starts[g])
+        place(2, own_last[g], 0, starts[g])
+        place(2, near_last[g], 1, starts[g])
         for part in far:
             place(0, landed["mid", g, part], part, starts[g])
-    place(2, total(0), 0)
-    place(2, near_last, 1)
-    for part in far:
-        place(2, landed["last", 0, part], part)
+            place(2, landed["last", g, part], part, starts[g])
     return tuple(outs)
 
 

time: 106 us -> 99.2 us (0.936)
  waiting for transfers between devices: 60 us -> 31.5 us
  starting transfers between devices: 24 us -> 46.3 us
    ppermute x24 -> x31, waiting for transfers between devices: 60 us -> 31.5 us  [swapped(): return lax.ppermute(block, axis, [(i, i ^ mask) for i in range(count)])]
    ppermute x24 -> x31, starting transfers between devices: 24 us -> 46.3 us  [swapped(): return lax.ppermute(block, axis, [(i, i ^ mask) for i in range(count)])]
  transfers between devices with their start and end apart: 24 -> 31, of which waited for: 14 -> 12; matrix products, arithmetic and copies ran while one was open for 2% -> 3% of each run, Pallas kernels for 13% -> 14%
where the time goes in v3:
time: 99.2 us; the launch traced here: 99.1 us
  starting transfers between devices  46.3 us (47%)
  waiting for transfers between devices  31.5 us (32%)
  Pallas kernels  13.5 us (14%)
  local copies, waits for them, and re-layouts  4.67 us (5%)
  other arithmetic  1.93 us (2%)
  between operations  1.25 us (1%)
    ppermute x31, starting transfers between devices, swapped(): return lax.ppermute(block, axis, [(i, i ^ mask) for i in range(count)])  46.3 us
    ppermute x31, waiting for transfers between devices, swapped(): return lax.ppermute(block, axis, [(i, i ^ mask) for i in range(count)])  31.5 us
    pallas_call x2, Pallas kernels, attention(): pl.pallas_call(functools.partial(attention_kernel, layout, depth, pool_si...  13.5 us
    another operation x2, local copies, waits for them, and re-layouts, slab(): jnp.stack([lax.dynamic_slice_in_dim(x, column(part, head), size, axis=1)...  2.2 us
  transfers between devices with their start and end apart: 31, of which 12 were waited for; matrix products, arithmetic and copies ran while one was open for 3% of the time, Pallas kernels for 14%

profile of v3, /device:TPU:1, one launch (start us, length us, event | category | flops | bytes accessed | tf_op | source)
XLA Modules:
  0.0 99.1 jit_solution(10873130859144569488)
XLA Ops:
  0.7 1.9 %dynamic-slice_bitcast_fusion = (bf16[1,128,512]{2,1,0:T(8,128)(2,1)S(1)}, bf16[1,128,512]{2,1,0:T(8,128)(2,1)S(1)}, bf16[1,128,512]{2,1,0:T(8,128)(2,1)S(1)}, b...) fusion(bf16[128,4096]{1,0:T(8,128)(2,1)} %param.7, ...), kind=kLoop, calls=%fused_computation.89 | loop fusion | bytes 4194336 | tf_op jit(solution)/shard_map/stack | solution.py:137
  3.4 2.1 %collective-permute-start.4 = (bf16[2,128,512]{2,1,0:T(8,128)(2,1)S(1)}, bf16[2,128,512]{2,1,0:T(8,128)(2,1)S(1)}, u32[]{:S(2)}, u32[]{:S(2)}) collective-permute-start(bf16[2,128,512]{2,1,0:T(8,128)(2,1)S(1)} %pad_maximum_fusion.7), channel_id=1, source_target_pairs={{0,2},{1,3},{2,0},{3,1},{4,6},{5,7},{6,4},{7,5},{8,10},{9,11},{10,... | collective-permute-start | bytes 786440 | tf_op jit(solution)/shard_map/ppermute | solution.py:23
  7.2 1.7 %collective-permute-start.3 = (f32[2,4,1024]{2,1,0:T(4,128)S(1)}, f32[2,4,1024]{2,1,0:T(4,128)S(1)}, u32[]{:S(2)}, u32[]{:S(2)}) collective-permute-start(f32[2,4,1024]{2,1,0:T(4,128)S(1)} %get-tuple-element.143), channel_id=1, source_target_pairs={{0,3},{1,2},{2,1},{3,0},{4,7},{5,6},{6,5},{7,4},{8,11},{9,10},{10,... | collective-permute-start | bytes 98312 | tf_op jit(solution)/shard_map/ppermute | solution.py:23
  9.2 3.0 %collective-permute-done.2 = f32[2,4,1024]{2,1,0:T(4,128)S(1)} collective-permute-done((f32[2,4,1024]{2,1,0:T(4,128)S(1)}, f32[2,4,1024]{2,1,0:T(4,128)S(1)}, u32[]{:S(2)}, u32[]{:S(2)}) %collective-permute-start.2) | collective-permute-done | bytes 32800 | tf_op jit(solution)/shard_map/ppermute | solution.py:23
  14.6 1.9 %collective-permute-start.7 = (f32[2,16,1024]{2,1,0:T(8,128)S(1)}, f32[2,16,1024]{2,1,0:T(8,128)S(1)}, u32[]{:S(2)}, u32[]{:S(2)}) collective-permute-start(f32[2,16,1024]{2,1,0:T(8,128)S(1)} %pad_maximum_fusion.10), channel_id=1, source_target_pairs={{0,4},{4,0},{8,12},{12,8},{16,20},{20,16},{24,28},{28,24},{1,5},{5... | collective-permute-start | bytes 393224 | tf_op jit(solution)/shard_map/ppermute | solution.py:23
  16.6 1.5 %collective-permute-start = (bf16[4,128,512]{2,1,0:T(8,128)(2,1)S(1)}, bf16[4,128,512]{2,1,0:T(8,128)(2,1)S(1)}, u32[]{:S(2)}, u32[]{:S(2)}) collective-permute-start(bf16[4,128,512]{2,1,0:T(8,128)(2,1)S(1)} %pad_maximum_fusion.1), channel_id=1, source_target_pairs={{0,1},{1,0},{2,3},{3,2},{4,5},{5,4},{6,7},{7,6},{8,9},{9,8},{10,11... | collective-permute-start | bytes 1572872 | tf_op jit(solution)/shard_map/ppermute | solution.py:23
  19.2 1.6 %collective-permute-start.8 = (f32[2,16,1024]{2,1,0:T(8,128)S(1)}, f32[2,16,1024]{2,1,0:T(8,128)S(1)}, u32[]{:S(2)}, u32[]{:S(2)}) collective-permute-start(f32[2,16,1024]{2,1,0:T(8,128)S(1)} %get-tuple-element.139), channel_id=1, source_target_pairs={{0,8},{4,12},{8,0},{12,4},{16,24},{20,28},{24,16},{28,20},{1,9},{5... | collective-permute-start | bytes 393224 | tf_op jit(solution)/shard_map/ppermute | solution.py:23
  20.9 2.5 %collective-permute-done.8 = f32[2,16,1024]{2,1,0:T(8,128)S(1)} collective-permute-done((f32[2,16,1024]{2,1,0:T(8,128)S(1)}, f32[2,16,1024]{2,1,0:T(8,128)S(1)}, u32[]{:S(2)}, u32[]{:S(2)}) %collective-permute-start.8) | collective-permute-done | bytes 131104 | tf_op jit(solution)/shard_map/ppermute | solution.py:23
  23.5 2.5 %collective-permute-start.10 = (bf16[2,16,1024]{2,1,0:T(8,128)(2,1)S(1)}, bf16[2,16,1024]{2,1,0:T(8,128)(2,1)S(1)}, u32[]{:S(2)}, u32[]{:S(2)}) collective-permute-start(bf16[2,16,1024]{2,1,0:T(8,128)(2,1)S(1)} %add_multiply_fusion), channel_id=1, source_target_pairs={{0,16},{4,20},{8,24},{12,28},{16,0},{20,4},{24,8},{28,12},{1,17},{... | collective-permute-start | bytes 196616 | tf_op jit(solution)/shard_map/ppermute | solution.py:23
  26.1 1.8 %collective-permute-start.12 = (bf16[4,128,512]{2,1,0:T(8,128)(2,1)S(1)}, bf16[4,128,512]{2,1,0:T(8,128)(2,1)S(1)}, u32[]{:S(2)}, u32[]{:S(2)}) collective-permute-start(bf16[4,128,512]{2,1,0:T(8,128)(2,1)S(1)} %pad_maximum_fusion.3), channel_id=1, source_target_pairs={{0,2},{1,3},{2,0},{3,1},{4,6},{5,7},{6,4},{7,5},{8,10},{9,11},{10,... | collective-permute-start | bytes 1572872 | tf_op jit(solution)/shard_map/ppermute | solution.py:23
  27.9 5.1 %collective-permute-start.13 = (bf16[4,128,512]{2,1,0:T(8,128)(2,1)S(1)}, bf16[4,128,512]{2,1,0:T(8,128)(2,1)S(1)}, u32[]{:S(2)}, u32[]{:S(2)}) collective-permute-start(bf16[4,128,512]{2,1,0:T(8,128)(2,1)S(1)} %pad_maximum_fusion.4), channel_id=1, source_target_pairs={{0,3},{1,2},{2,1},{3,0},{4,7},{5,6},{6,5},{7,4},{8,11},{9,10},{10,... | collective-permute-start | bytes 1572872 | tf_op jit(solution)/shard_map/ppermute | solution.py:23
  33.0 6.7 %attention.2 = (bf16[2,128,512]{2,1,0:T(8,128)(2,1)S(1)}, bf16[2,128,512]{2,1,0:T(8,128)(2,1)S(1)}, bf16[2,128,512]{2,1,0:T(8,128)(2,1)S(1)}, bf16[2,128,512]{2,...) custom-call(bf16[4,128,512]{2,1,0:T(8,128)(2,1)S(1)} %pad_maximum_fusion.refs_0_, ...), custom_call_target="tpu_custom_call" | custom-call | flops 1761607680 | bytes 6291456 | tf_op jit(solution)/shard_map/attention/pallas_call | solution.py:93
  39.8 2.1 %collective-permute-start.20 = (bf16[2,16,512]{2,1,0:T(8,128)(2,1)S(1)}, bf16[2,16,512]{2,1,0:T(8,128)(2,1)S(1)}, u32[]{:S(2)}, u32[]{:S(2)}) collective-permute-start(bf16[2,16,512]{2,1,0:T(8,128)(2,1)S(1)} %fusion.36), channel_id=1, source_target_pairs={{0,16},{4,20},{8,24},{12,28},{16,0},{20,4},{24,8},{28,12},{1,17},{... | collective-permute-start | bytes 98312 | tf_op jit(solution)/shard_map/ppermute | solution.py:23
  43.5 1.6 %collective-permute-start.21 = (bf16[2,16,512]{2,1,0:T(8,128)(2,1)S(1)}, bf16[2,16,512]{2,1,0:T(8,128)(2,1)S(1)}, u32[]{:S(2)}, u32[]{:S(2)}) collective-permute-start(bf16[2,16,512]{2,1,0:T(8,128)(2,1)S(1)} %fusion.31), channel_id=1, source_target_pairs={{0,8},{4,12},{8,0},{12,4},{16,24},{20,28},{24,16},{28,20},{1,9},{5... | collective-permute-start | bytes 98312 | tf_op jit(solution)/shard_map/ppermute | solution.py:23
  48.2 1.8 %collective-permute-start.11 = (bf16[2,128,512]{2,1,0:T(8,128)(2,1)S(1)}, bf16[2,128,512]{2,1,0:T(8,128)(2,1)S(1)}, u32[]{:S(2)}, u32[]{:S(2)}) collective-permute-start(bf16[2,128,512]{2,1,0:T(8,128)(2,1)S(1)} %get-tuple-element.46), channel_id=1, source_target_pairs={{0,1},{1,0},{2,3},{3,2},{4,5},{5,4},{6,7},{7,6},{8,9},{9,8},{10,11... | collective-permute-start | bytes 786440 | tf_op jit(solution)/shard_map/ppermute | solution.py:23
  50.3 1.8 %collective-permute-start.23 = (bf16[2,128,512]{2,1,0:T(8,128)(2,1)S(1)}, bf16[2,128,512]{2,1,0:T(8,128)(2,1)S(1)}, u32[]{:S(2)}, u32[]{:S(2)}) collective-permute-start(bf16[2,128,512]{2,1,0:T(8,128)(2,1)S(1)} %get-tuple-element.74), channel_id=1, source_target_pairs={{0,1},{1,0},{2,3},{3,2},{4,5},{5,4},{6,7},{7,6},{8,9},{9,8},{10,11... | collective-permute-start | bytes 786440 | tf_op jit(solution)/shard_map/ppermute | solution.py:23
  56.2 6.7 %attention.3 = (bf16[2,128,512]{2,1,0:T(8,128)(2,1)S(1)}, bf16[2,128,512]{2,1,0:T(8,128)(2,1)S(1)}, bf16[2,128,512]{2,1,0:T(8,128)(2,1)S(1)}, bf16[2,128,512]{2,...) custom-call(bf16[4,128,512]{2,1,0:T(8,128)(2,1)S(1)} %pad_maximum_fusion.6.refs_0_, ...), custom_call_target="tpu_custom_call" | custom-call | flops 1761607680 | bytes 6291456 | tf_op jit(solution)/shard_map/attention/pallas_call | solution.py:93
  63.0 2.5 %collective-permute-start.15 = (bf16[2,16,512]{2,1,0:T(8,128)(2,1)S(1)}, bf16[2,16,512]{2,1,0:T(8,128)(2,1)S(1)}, u32[]{:S(2)}, u32[]{:S(2)}) collective-permute-start(bf16[2,16,512]{2,1,0:T(8,128)(2,1)S(1)} %fusion.35), channel_id=1, source_target_pairs={{0,16},{4,20},{8,24},{12,28},{16,0},{20,4},{24,8},{28,12},{1,17},{... | collective-permute-start | bytes 98312 | tf_op jit(solution)/shard_map/ppermute | solution.py:23
  67.3 1.6 %collective-permute-start.24 = (bf16[2,16,512]{2,1,0:T(8,128)(2,1)S(1)}, bf16[2,16,512]{2,1,0:T(8,128)(2,1)S(1)}, u32[]{:S(2)}, u32[]{:S(2)}) collective-permute-start(bf16[2,16,512]{2,1,0:T(8,128)(2,1)S(1)} %fusion.33), channel_id=1, source_target_pairs={{0,8},{4,12},{8,0},{12,4},{16,24},{20,28},{24,16},{28,20},{1,9},{5... | collective-permute-start | bytes 98312 | tf_op jit(solution)/shard_map/ppermute | solution.py:23
  69.0 4.1 %collective-permute-start.19 = (bf16[2,128,512]{2,1,0:T(8,128)(2,1)S(1)}, bf16[2,128,512]{2,1,0:T(8,128)(2,1)S(1)}, u32[]{:S(2)}, u32[]{:S(2)}) collective-permute-start(bf16[2,128,512]{2,1,0:T(8,128)(2,1)S(1)} %get-tuple-element.59), channel_id=1, source_target_pairs={{0,3},{1,2},{2,1},{3,0},{4,7},{5,6},{6,5},{7,4},{8,11},{9,10},{10,... | collective-permute-start | bytes 786440 | tf_op jit(solution)/shard_map/ppermute | solution.py:23
  74.5 2.7 %collective-permute-done.27 = bf16[2,128,512]{2,1,0:T(8,128)(2,1)S(1)} collective-permute-done((bf16[2,128,512]{2,1,0:T(8,128)(2,1)S(1)}, bf16[2,128,512]{2,1,0:T(8,128)(2,1)S(1)}, u32[]{:S(2)}, u32[]{:S(2)}) %collective-permute-start.27) | collective-permute-done | bytes 262176 | tf_op jit(solution)/shard_map/ppermute | solution.py:23
  80.0 8.5 %collective-permute-done.19 = bf16[2,128,512]{2,1,0:T(8,128)(2,1)S(1)} collective-permute-done((bf16[2,128,512]{2,1,0:T(8,128)(2,1)S(1)}, bf16[2,128,512]{2,1,0:T(8,128)(2,1)S(1)}, u32[]{:S(2)}, u32[]{:S(2)}) %collective-permute-start.19) | collective-permute-done | bytes 262176 | tf_op jit(solution)/shard_map/ppermute | solution.py:23
  88.5 2.0 %collective-permute-done.29 = bf16[2,128,512]{2,1,0:T(8,128)(2,1)S(1)} collective-permute-done((bf16[2,128,512]{2,1,0:T(8,128)(2,1)S(1)}, bf16[2,128,512]{2,1,0:T(8,128)(2,1)S(1)}, u32[]{:S(2)}, u32[]{:S(2)}) %collective-permute-start.29) | collective-permute-done | bytes 262176 | tf_op jit(solution)/shard_map/ppermute | solution.py:23
  90.5 7.2 %collective-permute-done.30 = bf16[2,128,512]{2,1,0:T(8,128)(2,1)S(1)} collective-permute-done((bf16[2,128,512]{2,1,0:T(8,128)(2,1)S(1)}, bf16[2,128,512]{2,1,0:T(8,128)(2,1)S(1)}, u32[]{:S(2)}, u32[]{:S(2)}) %collective-permute-start.30) | collective-permute-done | bytes 262176 | tf_op jit(solution)/shard_map/ppermute | solution.py:23
  (108 shorter events, 22.9 us)
Async XLA Ops:
  3.4 11.2 %collective-permute-start.4 = (bf16[2,128,512]{2,1,0:T(8,128)(2,1)S(1)}, bf16[2,128,512]{2,1,0:T(8,128)(2,1)S(1)}, u32[]{:S(2)}, u32[]{:S(2)}) collective-permute-start(bf16[2,128,512]{2,1,0:T(8,128)(2,1)S(1)} %pad_maximum_fusion.7), channel_id=1, source_target_pairs={{0,2},{1,3},{2,0},{3,1},{4,6},{5,7},{6,4},{7,5},{8,10},{9,11},{10,... | collective-permute-start | bytes 786440 | tf_op jit(solution)/shard_map/ppermute | solution.py:23
  7.1 5.1 %collective-permute-start.2 = (f32[2,4,1024]{2,1,0:T(4,128)S(1)}, f32[2,4,1024]{2,1,0:T(4,128)S(1)}, u32[]{:S(2)}, u32[]{:S(2)}) collective-permute-start(f32[2,4,1024]{2,1,0:T(4,128)S(1)} %get-tuple-element.142), channel_id=1, source_target_pairs={{0,2},{1,3},{2,0},{3,1},{4,6},{5,7},{6,4},{7,5},{8,10},{9,11},{10,... | collective-permute-start | bytes 98312 | tf_op jit(solution)/shard_map/ppermute | solution.py:23
  7.2 7.4 %collective-permute-start.3 = (f32[2,4,1024]{2,1,0:T(4,128)S(1)}, f32[2,4,1024]{2,1,0:T(4,128)S(1)}, u32[]{:S(2)}, u32[]{:S(2)}) collective-permute-start(f32[2,4,1024]{2,1,0:T(4,128)S(1)} %get-tuple-element.143), channel_id=1, source_target_pairs={{0,3},{1,2},{2,1},{3,0},{4,7},{5,6},{6,5},{7,4},{8,11},{9,10},{10,... | collective-permute-start | bytes 98312 | tf_op jit(solution)/shard_map/ppermute | solution.py:23
  8.9 14.5 %collective-permute-start.9 = (bf16[4,128,512]{2,1,0:T(8,128)(2,1)S(1)}, bf16[4,128,512]{2,1,0:T(8,128)(2,1)S(1)}, u32[]{:S(2)}, u32[]{:S(2)}) collective-permute-start(bf16[4,128,512]{2,1,0:T(8,128)(2,1)S(1)} %pad_maximum_fusion.5), channel_id=1, source_target_pairs={{0,1},{1,0},{2,3},{3,2},{4,5},{5,4},{6,7},{7,6},{8,9},{9,8},{10,11... | collective-permute-start | bytes 1572872 | tf_op jit(solution)/shard_map/ppermute | solution.py:23
  9.2 23.8 %collective-permute-start.6 = (bf16[4,128,512]{2,1,0:T(8,128)(2,1)S(1)}, bf16[4,128,512]{2,1,0:T(8,128)(2,1)S(1)}, u32[]{:S(2)}, u32[]{:S(2)}) collective-permute-start(bf16[4,128,512]{2,1,0:T(8,128)(2,1)S(1)} %pad_maximum_fusion.2), channel_id=1, source_target_pairs={{0,3},{1,2},{2,1},{3,0},{4,7},{5,6},{6,5},{7,4},{8,11},{9,10},{10,... | collective-permute-start | bytes 1572872 | tf_op jit(solution)/shard_map/ppermute | solution.py:23
  12.2 20.8 %collective-permute-start.5 = (bf16[2,128,512]{2,1,0:T(8,128)(2,1)S(1)}, bf16[2,128,512]{2,1,0:T(8,128)(2,1)S(1)}, u32[]{:S(2)}, u32[]{:S(2)}) collective-permute-start(bf16[2,128,512]{2,1,0:T(8,128)(2,1)S(1)} %pad_maximum_fusion.8), channel_id=1, source_target_pairs={{0,2},{1,3},{2,0},{3,1},{4,6},{5,7},{6,4},{7,5},{8,10},{9,11},{10,... | collective-permute-start | bytes 786440 | tf_op jit(solution)/shard_map/ppermute | solution.py:23
  14.6 4.5 %collective-permute-start.7 = (f32[2,16,1024]{2,1,0:T(8,128)S(1)}, f32[2,16,1024]{2,1,0:T(8,128)S(1)}, u32[]{:S(2)}, u32[]{:S(2)}) collective-permute-start(f32[2,16,1024]{2,1,0:T(8,128)S(1)} %pad_maximum_fusion.10), channel_id=1, source_target_pairs={{0,4},{4,0},{8,12},{12,8},{16,20},{20,16},{24,28},{28,24},{1,5},{5... | collective-permute-start | bytes 393224 | tf_op jit(solution)/shard_map/ppermute | solution.py:23
  16.6 16.4 %collective-permute-start = (bf16[4,128,512]{2,1,0:T(8,128)(2,1)S(1)}, bf16[4,128,512]{2,1,0:T(8,128)(2,1)S(1)}, u32[]{:S(2)}, u32[]{:S(2)}) collective-permute-start(bf16[4,128,512]{2,1,0:T(8,128)(2,1)S(1)} %pad_maximum_fusion.1), channel_id=1, source_target_pairs={{0,1},{1,0},{2,3},{3,2},{4,5},{5,4},{6,7},{7,6},{8,9},{9,8},{10,11... | collective-permute-start | bytes 1572872 | tf_op jit(solution)/shard_map/ppermute | solution.py:23
  19.2 4.2 %collective-permute-start.8 = (f32[2,16,1024]{2,1,0:T(8,128)S(1)}, f32[2,16,1024]{2,1,0:T(8,128)S(1)}, u32[]{:S(2)}, u32[]{:S(2)}) collective-permute-start(f32[2,16,1024]{2,1,0:T(8,128)S(1)} %get-tuple-element.139), channel_id=1, source_target_pairs={{0,8},{4,12},{8,0},{12,4},{16,24},{20,28},{24,16},{28,20},{1,9},{5... | collective-permute-start | bytes 393224 | tf_op jit(solution)/shard_map/ppermute | solution.py:23
  23.5 4.4 %collective-permute-start.10 = (bf16[2,16,1024]{2,1,0:T(8,128)(2,1)S(1)}, bf16[2,16,1024]{2,1,0:T(8,128)(2,1)S(1)}, u32[]{:S(2)}, u32[]{:S(2)}) collective-permute-start(bf16[2,16,1024]{2,1,0:T(8,128)(2,1)S(1)} %add_multiply_fusion), channel_id=1, source_target_pairs={{0,16},{4,20},{8,24},{12,28},{16,0},{20,4},{24,8},{28,12},{1,17},{... | collective-permute-start | bytes 196616 | tf_op jit(solution)/shard_map/ppermute | solution.py:23
  26.1 28.8 %collective-permute-start.12 = (bf16[4,128,512]{2,1,0:T(8,128)(2,1)S(1)}, bf16[4,128,512]{2,1,0:T(8,128)(2,1)S(1)}, u32[]{:S(2)}, u32[]{:S(2)}) collective-permute-start(bf16[4,128,512]{2,1,0:T(8,128)(2,1)S(1)} %pad_maximum_fusion.3), channel_id=1, source_target_pairs={{0,2},{1,3},{2,0},{3,1},{4,6},{5,7},{6,4},{7,5},{8,10},{9,11},{10,... | collective-permute-start | bytes 1572872 | tf_op jit(solution)/shard_map/ppermute | solution.py:23
  27.9 28.4 %collective-permute-start.13 = (bf16[4,128,512]{2,1,0:T(8,128)(2,1)S(1)}, bf16[4,128,512]{2,1,0:T(8,128)(2,1)S(1)}, u32[]{:S(2)}, u32[]{:S(2)}) collective-permute-start(bf16[4,128,512]{2,1,0:T(8,128)(2,1)S(1)} %pad_maximum_fusion.4), channel_id=1, source_target_pairs={{0,3},{1,2},{2,1},{3,0},{4,7},{5,6},{6,5},{7,4},{8,11},{9,10},{10,... | collective-permute-start | bytes 1572872 | tf_op jit(solution)/shard_map/ppermute | solution.py:23
  41.9 21.1 %collective-permute-start.14 = (bf16[2,128,512]{2,1,0:T(8,128)(2,1)S(1)}, bf16[2,128,512]{2,1,0:T(8,128)(2,1)S(1)}, u32[]{:S(2)}, u32[]{:S(2)}) collective-permute-start(bf16[2,128,512]{2,1,0:T(8,128)(2,1)S(1)} %get-tuple-element.51), channel_id=1, source_target_pairs={{0,2},{1,3},{2,0},{3,1},{4,6},{5,7},{6,4},{7,5},{8,10},{9,11},{10,... | collective-permute-start | bytes 786440 | tf_op jit(solution)/shard_map/ppermute | solution.py:23
  52.4 13.5 %collective-permute-start.16 = (bf16[2,128,512]{2,1,0:T(8,128)(2,1)S(1)}, bf16[2,128,512]{2,1,0:T(8,128)(2,1)S(1)}, u32[]{:S(2)}, u32[]{:S(2)}) collective-permute-start(bf16[2,128,512]{2,1,0:T(8,128)(2,1)S(1)} %get-tuple-element.54), channel_id=1, source_target_pairs={{0,3},{1,2},{2,1},{3,0},{4,7},{5,6},{6,5},{7,4},{8,11},{9,10},{10,... | collective-permute-start | bytes 786440 | tf_op jit(solution)/shard_map/ppermute | solution.py:23
  53.9 15.0 %collective-permute-start.25 = (bf16[2,128,512]{2,1,0:T(8,128)(2,1)S(1)}, bf16[2,128,512]{2,1,0:T(8,128)(2,1)S(1)}, u32[]{:S(2)}, u32[]{:S(2)}) collective-permute-start(bf16[2,128,512]{2,1,0:T(8,128)(2,1)S(1)} %get-tuple-element.73), channel_id=1, source_target_pairs={{0,2},{1,3},{2,0},{3,1},{4,6},{5,7},{6,4},{7,5},{8,10},{9,11},{10,... | collective-permute-start | bytes 786440 | tf_op jit(solution)/shard_map/ppermute | solution.py:23
  54.9 22.3 %collective-permute-start.27 = (bf16[2,128,512]{2,1,0:T(8,128)(2,1)S(1)}, bf16[2,128,512]{2,1,0:T(8,128)(2,1)S(1)}, u32[]{:S(2)}, u32[]{:S(2)}) collective-permute-start(bf16[2,128,512]{2,1,0:T(8,128)(2,1)S(1)} %get-tuple-element.72), channel_id=1, source_target_pairs={{0,3},{1,2},{2,1},{3,0},{4,7},{5,6},{6,5},{7,4},{8,11},{9,10},{10,... | collective-permute-start | bytes 786440 | tf_op jit(solution)/shard_map/ppermute | solution.py:23
  63.0 4.3 %collective-permute-start.15 = (bf16[2,16,512]{2,1,0:T(8,128)(2,1)S(1)}, bf16[2,16,512]{2,1,0:T(8,128)(2,1)S(1)}, u32[]{:S(2)}, u32[]{:S(2)}) collective-permute-start(bf16[2,16,512]{2,1,0:T(8,128)(2,1)S(1)} %fusion.35), channel_id=1, source_target_pairs={{0,16},{4,20},{8,24},{12,28},{16,0},{20,4},{24,8},{28,12},{1,17},{... | collective-permute-start | bytes 98312 | tf_op jit(solution)/shard_map/ppermute | solution.py:23
  65.5 13.2 %collective-permute-start.17 = (bf16[2,128,512]{2,1,0:T(8,128)(2,1)S(1)}, bf16[2,128,512]{2,1,0:T(8,128)(2,1)S(1)}, u32[]{:S(2)}, u32[]{:S(2)}) collective-permute-start(bf16[2,128,512]{2,1,0:T(8,128)(2,1)S(1)} %get-tuple-element.57), channel_id=1, source_target_pairs={{0,1},{1,0},{2,3},{3,2},{4,5},{5,4},{6,7},{7,6},{8,9},{9,8},{10,11... | collective-permute-start | bytes 786440 | tf_op jit(solution)/shard_map/ppermute | solution.py:23
  65.9 14.0 %collective-permute-start.18 = (bf16[2,128,512]{2,1,0:T(8,128)(2,1)S(1)}, bf16[2,128,512]{2,1,0:T(8,128)(2,1)S(1)}, u32[]{:S(2)}, u32[]{:S(2)}) collective-permute-start(bf16[2,128,512]{2,1,0:T(8,128)(2,1)S(1)} %get-tuple-element.58), channel_id=1, source_target_pairs={{0,2},{1,3},{2,0},{3,1},{4,6},{5,7},{6,4},{7,5},{8,10},{9,11},{10,... | collective-permute-start | bytes 786440 | tf_op jit(solution)/shard_map/ppermute | solution.py:23
  67.3 5.8 %collective-permute-start.24 = (bf16[2,16,512]{2,1,0:T(8,128)(2,1)S(1)}, bf16[2,16,512]{2,1,0:T(8,128)(2,1)S(1)}, u32[]{:S(2)}, u32[]{:S(2)}) collective-permute-start(bf16[2,16,512]{2,1,0:T(8,128)(2,1)S(1)} %fusion.33), channel_id=1, source_target_pairs={{0,8},{4,12},{8,0},{12,4},{16,24},{20,28},{24,16},{28,20},{1,9},{5... | collective-permute-start | bytes 98312 | tf_op jit(solution)/shard_map/ppermute | solution.py:23
  69.0 19.4 %collective-permute-start.19 = (bf16[2,128,512]{2,1,0:T(8,128)(2,1)S(1)}, bf16[2,128,512]{2,1,0:T(8,128)(2,1)S(1)}, u32[]{:S(2)}, u32[]{:S(2)}) collective-permute-start(bf16[2,128,512]{2,1,0:T(8,128)(2,1)S(1)} %get-tuple-element.59), channel_id=1, source_target_pairs={{0,3},{1,2},{2,1},{3,0},{4,7},{5,6},{6,5},{7,4},{8,11},{9,10},{10,... | collective-permute-start | bytes 786440 | tf_op jit(solution)/shard_map/ppermute | solution.py:23
  77.5 10.9 %collective-permute-start.28 = (bf16[2,128,512]{2,1,0:T(8,128)(2,1)S(1)}, bf16[2,128,512]{2,1,0:T(8,128)(2,1)S(1)}, u32[]{:S(2)}, u32[]{:S(2)}) collective-permute-start(bf16[2,128,512]{2,1,0:T(8,128)(2,1)S(1)} %get-tuple-element.70), channel_id=1, source_target_pairs={{0,1},{1,0},{2,3},{3,2},{4,5},{5,4},{6,7},{7,6},{8,9},{9,8},{10,11... | collective-permute-start | bytes 786440 | tf_op jit(solution)/shard_map/ppermute | solution.py:23
  77.6 12.9 %collective-permute-start.29 = (bf16[2,128,512]{2,1,0:T(8,128)(2,1)S(1)}, bf16[2,128,512]{2,1,0:T(8,128)(2,1)S(1)}, u32[]{:S(2)}, u32[]{:S(2)}) collective-permute-start(bf16[2,128,512]{2,1,0:T(8,128)(2,1)S(1)} %get-tuple-element.69), channel_id=1, source_target_pairs={{0,2},{1,3},{2,0},{3,1},{4,6},{5,7},{6,4},{7,5},{8,10},{9,11},{10,... | collective-permute-start | bytes 786440 | tf_op jit(solution)/shard_map/ppermute | solution.py:23
  78.7 19.0 %collective-permute-start.30 = (bf16[2,128,512]{2,1,0:T(8,128)(2,1)S(1)}, bf16[2,128,512]{2,1,0:T(8,128)(2,1)S(1)}, u32[]{:S(2)}, u32[]{:S(2)}) collective-permute-start(bf16[2,128,512]{2,1,0:T(8,128)(2,1)S(1)} %get-tuple-element.68), channel_id=1, source_target_pairs={{0,3},{1,2},{2,1},{3,0},{4,7},{5,6},{6,5},{7,4},{8,11},{9,10},{10,... | collective-permute-start | bytes 786440 | tf_op jit(solution)/shard_map/ppermute | solution.py:23
  (13 other events, 50.2 us)

commit v4 on v3

--- a/solution.py
+++ b/solution.py
@@ -11,11 +11,11 @@
 HD = 128
 CROWS = 16
 SCALE = HD**-0.5
-FIRST = 1
-IN_GATE = 2
-PACE0 = ((), (), (), ())
-PACE1 = ((("mid", 0, 2),), (("mid", 0, 3),), (("last", 0, 2),), (("last", 0, 3),))
-F_PACE = ((("in", 0, 2, 0),), (), (("near", 1),))
+PACE = (
+    (),
+    ((("mid", 0, 2),), (("mid", 0, 3),), (("last", 0, 2),), (("last", 0, 3),)),
+)
+PACE_IN = ((("in", 0, 2, 0),), (), (("near", 1),))
 
 
 def swapped(block, axis, mask):
@@ -24,11 +24,11 @@
 
 
 def attention_kernel(layout, depth, pool_size, *refs):
-    parts, count = len(layout), sum(layout)
-    blocks = []
-    for pieces in layout:
-        at = sum(len(b) for b in blocks)
-        blocks.append(refs[at : at + pieces])
+    parts, count = len(layout), sum(len(sizes) for sizes in layout)
+    blocks, at = [], 0
+    for sizes in layout:
+        blocks.append([(ref, i) for ref, size in zip(refs[at:], sizes) for i in range(size)])
+        at += len(sizes)
     coarse_ref = refs[count]
     out_refs = refs[count + 1 : count + 1 + parts]
     local_ref, coarse_grad_ref = refs[count + 1 + parts :]
@@ -36,11 +36,7 @@
     own = parts * rows
 
     def whole(which):
-        taken = []
-        for pieces in blocks:
-            each = 4 // len(pieces)
-            taken.append(pieces[which // each][which % each])
-        return jnp.concatenate(taken, axis=0)
+        return jnp.concatenate([block[which][0][block[which][1]] for block in blocks], axis=0)
 
     keys = jnp.concatenate([whole(0), coarse_ref[0]], axis=0)
     values = jnp.concatenate([whole(1), coarse_ref[1]], axis=0)
@@ -78,7 +74,7 @@
 
 def attention(blocks, coarse, first, heads, depth, pool_size):
     parts = len(blocks)
-    layout = tuple(len(pieces) for pieces in blocks)
+    layout = tuple(tuple(piece.shape[0] for piece in pieces) for pieces in blocks)
     flat = [piece for pieces in blocks for piece in pieces]
     rows = flat[0].shape[1]
     width = heads * HD
@@ -151,10 +147,17 @@
 
     def pieces(part, g):
         whole = slab(part, starts[g], split[g] * HD)
-        return [whole[:2], whole[2:]] if g == 0 and 2 <= part < 2 + FIRST else [whole]
-
+        return [whole[:2], whole[2:]] if g == 0 and part == 2 else [whole]
+
+    both = jnp.concatenate([keys_in, values_in])
+    opening = lax.dynamic_slice_in_dim(both, column(2), split[0] * HD, axis=1)
+    opening = opening.reshape(2, rows, split[0] * HD)
+    keys_in, values_in = lax.optimization_barrier((keys_in, values_in))
+    arrays = (keys_in, values_in, queries, grad_out)
     slabs = [[pieces(part, g) for part in far] for g in range(groups)]
-    slabs[0], keys_now, values_now = lax.optimization_barrier((slabs[0], keys_in, values_in))
+    others = (slabs[0][0][1:], slabs[0][1:])
+    others, keys_now, values_now = lax.optimization_barrier((others, keys_in, values_in))
+    slabs[0] = [[opening, *others[0]], *others[1]]
     pooled_here = jnp.stack(
         [
             jnp.mean(x.astype(jnp.float32).reshape(per, pool_size, columns), axis=1)
@@ -165,23 +168,22 @@
     for part in range(parts):
         block = lax.dynamic_slice_in_dim(pooled_here, column(part), width, axis=2)
         pooled_parts.append(swapped(block, "head", part) if part else block)
-    for part in far[:FIRST]:
-        send(slabs[0][part - 2][0], part, ("in", 0, part, 0))
+    send(slabs[0][0][0], 2, ("in", 0, 2, 0))
     mean_now = jnp.concatenate(pooled_parts, axis=1)
     for g in range(groups):
         send(slab(1, starts[g], split[g] * HD), 1, ("near", g))
     siblings = []
     for level in range(depth):
-        if level < len(F_PACE):
-            mean_now = after(mean_now, F_PACE[level])
+        if level < len(PACE_IN):
+            mean_now = after(mean_now, PACE_IN[level])
         received = swapped(mean_now, "seq", 1 << level)
         siblings.append(received)
         mean_now = 0.5 * (mean_now + received)
 
     blocks = []
     for g in range(groups):
-        if g and IN_GATE:
-            at = min(IN_GATE, depth) - 1
+        if g:
+            at = min(2, depth) - 1
             slabs[g], siblings[at] = lax.optimization_barrier((slabs[g], siblings[at]))
         for part in far:
             for at, piece in enumerate(slabs[g][part - 2]):
@@ -204,7 +206,7 @@
             send(sent[part], part, ("mid", g, part))
 
     def chain(coarse_grad, pace):
-        pace = list(pace) + [()] * depth
+        pace = list(pace) + [()] * (depth + 1)
         coarse_grad = after(coarse_grad, pace[0])
         above = jnp.zeros(coarse_grad[:, 0].shape, jnp.float32)
         for level in reversed(range(depth)):
@@ -220,7 +222,7 @@
 
     own_last, near_last = [], []
     for g in range(groups):
-        above = chain(sums[g], (PACE0, PACE1)[g])
+        above = chain(sums[g], PACE[g])
         for part in far:
             send(total(part, grads[g], above), part, ("last", g, part))
         own_last.append(total(0, grads[g], above))

time: 99.2 us -> 97.9 us (0.987)
  waiting for transfers between devices: 31.5 us -> 28 us
  starting transfers between devices: 46.3 us -> 48.1 us
  other arithmetic: 1.93 us -> 3.04 us
    ppermute x31, waiting for transfers between devices: 31.5 us -> 28 us  [swapped(): return lax.ppermute(block, axis, [(i, i ^ mask) for i in range(count)])]
    ppermute x31, starting transfers between devices: 46.3 us -> 48.1 us  [swapped(): return lax.ppermute(block, axis, [(i, i ^ mask) for i in range(count)])]
    another operation x2, local copies, waits for them, and re-layouts: 2.2 us -> 0.51 us  [slab(): jnp.stack([lax.dynamic_slice_in_dim(x, column(part, head), size, axis=1)...]
    concatenate x0 -> x1, other arithmetic: none -> 1.13 us  [on_device(): both = jnp.concatenate([keys_in, values_in])]
    unnamed x12 -> x16, local copies, waits for them, and re-layouts: 1.62 us -> 2.53 us
where the time goes in v4:
time: 97.9 us; the launch traced here: 97.7 us
  starting transfers between devices  48.1 us (49%)
  waiting for transfers between devices  28 us (29%)
  Pallas kernels  13.5 us (14%)
  local copies, waits for them, and re-layouts  3.87 us (4%)
  other arithmetic  3.04 us (3%)
  between operations  1.23 us (1%)
    ppermute x31, starting transfers between devices, swapped(): return lax.ppermute(block, axis, [(i, i ^ mask) for i in range(count)])  48.1 us
    ppermute x31, waiting for transfers between devices, swapped(): return lax.ppermute(block, axis, [(i, i ^ mask) for i in range(count)])  28 us
    pallas_call x2, Pallas kernels, attention(): pl.pallas_call(functools.partial(attention_kernel, layout, depth, pool_si...  13.5 us
    unnamed x16, local copies, waits for them, and re-layouts  2.53 us
  transfers between devices with their start and end apart: 31, of which 12 were waited for; matrix products, arithmetic and copies ran while one was open for 3% of the time, Pallas kernels for 14%

profile of v4, /device:TPU:1, one launch (start us, length us, event | category | flops | bytes accessed | tf_op | source)
XLA Modules:
  0.0 97.7 jit_solution(2812260285383651085)
XLA Ops:
  1.8 2.1 %collective-permute-start.4 = (bf16[2,128,512]{2,1,0:T(8,128)(2,1)S(1)}, bf16[2,128,512]{2,1,0:T(8,128)(2,1)S(1)}, u32[]{:S(2)}, u32[]{:S(2)}) collective-permute-start(bf16[2,128,512]{2,1,0:T(8,128)(2,1)S(1)} %bitcast.240), channel_id=1, source_target_pairs={{0,2},{1,3},{2,0},{3,1},{4,6},{5,7},{6,4},{7,5},{8,10},{9,11},{10,... | collective-permute-start | bytes 786440 | tf_op jit(solution)/shard_map/ppermute | solution.py:23
  7.6 1.5 %collective-permute-start.3 = (f32[2,4,1024]{2,1,0:T(4,128)S(1)}, f32[2,4,1024]{2,1,0:T(4,128)S(1)}, u32[]{:S(2)}, u32[]{:S(2)}) collective-permute-start(f32[2,4,1024]{2,1,0:T(4,128)S(1)} %get-tuple-element.143), channel_id=1, source_target_pairs={{0,3},{1,2},{2,1},{3,0},{4,7},{5,6},{6,5},{7,4},{8,11},{9,10},{10,... | collective-permute-start | bytes 98312 | tf_op jit(solution)/shard_map/ppermute | solution.py:23
  11.9 1.6 %collective-permute-start.7 = (f32[2,16,1024]{2,1,0:T(8,128)S(1)}, f32[2,16,1024]{2,1,0:T(8,128)S(1)}, u32[]{:S(2)}, u32[]{:S(2)}) collective-permute-start(f32[2,16,1024]{2,1,0:T(8,128)S(1)} %pad_maximum_fusion.9), channel_id=1, source_target_pairs={{0,4},{4,0},{8,12},{12,8},{16,20},{20,16},{24,28},{28,24},{1,5},{5... | collective-permute-start | bytes 393224 | tf_op jit(solution)/shard_map/ppermute | solution.py:23
  13.6 2.7 %collective-permute-start = (bf16[4,128,512]{2,1,0:T(8,128)(2,1)S(1)}, bf16[4,128,512]{2,1,0:T(8,128)(2,1)S(1)}, u32[]{:S(2)}, u32[]{:S(2)}) collective-permute-start(bf16[4,128,512]{2,1,0:T(8,128)(2,1)S(1)} %pad_maximum_fusion.1), channel_id=1, source_target_pairs={{0,1},{1,0},{2,3},{3,2},{4,5},{5,4},{6,7},{7,6},{8,9},{9,8},{10,11... | collective-permute-start | bytes 1572872 | tf_op jit(solution)/shard_map/ppermute | solution.py:23
  16.4 1.4 %collective-permute-start.8 = (f32[2,16,1024]{2,1,0:T(8,128)S(1)}, f32[2,16,1024]{2,1,0:T(8,128)S(1)}, u32[]{:S(2)}, u32[]{:S(2)}) collective-permute-start(f32[2,16,1024]{2,1,0:T(8,128)S(1)} %get-tuple-element.139), channel_id=1, source_target_pairs={{0,8},{4,12},{8,0},{12,4},{16,24},{20,28},{24,16},{28,20},{1,9},{5... | collective-permute-start | bytes 393224 | tf_op jit(solution)/shard_map/ppermute | solution.py:23
  17.9 2.7 %collective-permute-done.8 = f32[2,16,1024]{2,1,0:T(8,128)S(1)} collective-permute-done((f32[2,16,1024]{2,1,0:T(8,128)S(1)}, f32[2,16,1024]{2,1,0:T(8,128)S(1)}, u32[]{:S(2)}, u32[]{:S(2)}) %collective-permute-start.8) | collective-permute-done | bytes 131104 | tf_op jit(solution)/shard_map/ppermute | solution.py:23
  20.6 2.4 %collective-permute-start.10 = (bf16[2,16,1024]{2,1,0:T(8,128)(2,1)S(1)}, bf16[2,16,1024]{2,1,0:T(8,128)(2,1)S(1)}, u32[]{:S(2)}, u32[]{:S(2)}) collective-permute-start(bf16[2,16,1024]{2,1,0:T(8,128)(2,1)S(1)} %add_multiply_fusion), channel_id=1, source_target_pairs={{0,16},{4,20},{8,24},{12,28},{16,0},{20,4},{24,8},{28,12},{1,17},{... | collective-permute-start | bytes 196616 | tf_op jit(solution)/shard_map/ppermute | solution.py:23
  23.1 4.1 %collective-permute-start.12 = (bf16[4,128,512]{2,1,0:T(8,128)(2,1)S(1)}, bf16[4,128,512]{2,1,0:T(8,128)(2,1)S(1)}, u32[]{:S(2)}, u32[]{:S(2)}) collective-permute-start(bf16[4,128,512]{2,1,0:T(8,128)(2,1)S(1)} %pad_maximum_fusion.3), channel_id=1, source_target_pairs={{0,2},{1,3},{2,0},{3,1},{4,6},{5,7},{6,4},{7,5},{8,10},{9,11},{10,... | collective-permute-start | bytes 1572872 | tf_op jit(solution)/shard_map/ppermute | solution.py:23
  27.2 4.1 %collective-permute-start.13 = (bf16[4,128,512]{2,1,0:T(8,128)(2,1)S(1)}, bf16[4,128,512]{2,1,0:T(8,128)(2,1)S(1)}, u32[]{:S(2)}, u32[]{:S(2)}) collective-permute-start(bf16[4,128,512]{2,1,0:T(8,128)(2,1)S(1)} %pad_maximum_fusion.4), channel_id=1, source_target_pairs={{0,3},{1,2},{2,1},{3,0},{4,7},{5,6},{6,5},{7,4},{8,11},{9,10},{10,... | collective-permute-start | bytes 1572872 | tf_op jit(solution)/shard_map/ppermute | solution.py:23
  31.3 6.7 %attention.2 = (bf16[2,128,512]{2,1,0:T(8,128)(2,1)S(1)}, bf16[2,128,512]{2,1,0:T(8,128)(2,1)S(1)}, bf16[2,128,512]{2,1,0:T(8,128)(2,1)S(1)}, bf16[2,128,512]{2,...) custom-call(bf16[4,128,512]{2,1,0:T(8,128)(2,1)S(1)} %pad_maximum_fusion.refs_0_, ...), custom_call_target="tpu_custom_call" | custom-call | flops 1761607680 | bytes 6291456 | tf_op jit(solution)/shard_map/attention/pallas_call | solution.py:89
  38.1 2.3 %collective-permute-start.20 = (bf16[2,16,512]{2,1,0:T(8,128)(2,1)S(1)}, bf16[2,16,512]{2,1,0:T(8,128)(2,1)S(1)}, u32[]{:S(2)}, u32[]{:S(2)}) collective-permute-start(bf16[2,16,512]{2,1,0:T(8,128)(2,1)S(1)} %fusion.37), channel_id=1, source_target_pairs={{0,16},{4,20},{8,24},{12,28},{16,0},{20,4},{24,8},{28,12},{1,17},{... | collective-permute-start | bytes 98312 | tf_op jit(solution)/shard_map/ppermute | solution.py:23
  41.8 1.8 %collective-permute-start.21 = (bf16[2,16,512]{2,1,0:T(8,128)(2,1)S(1)}, bf16[2,16,512]{2,1,0:T(8,128)(2,1)S(1)}, u32[]{:S(2)}, u32[]{:S(2)}) collective-permute-start(bf16[2,16,512]{2,1,0:T(8,128)(2,1)S(1)} %fusion.32), channel_id=1, source_target_pairs={{0,8},{4,12},{8,0},{12,4},{16,24},{20,28},{24,16},{28,20},{1,9},{5... | collective-permute-start | bytes 98312 | tf_op jit(solution)/shard_map/ppermute | solution.py:23
  43.8 1.5 %collective-permute-done.21 = bf16[2,16,512]{2,1,0:T(8,128)(2,1)S(1)} collective-permute-done((bf16[2,16,512]{2,1,0:T(8,128)(2,1)S(1)}, bf16[2,16,512]{2,1,0:T(8,128)(2,1)S(1)}, u32[]{:S(2)}, u32[]{:S(2)}) %collective-permute-start.21) | collective-permute-done | bytes 32800 | tf_op jit(solution)/shard_map/ppermute | solution.py:23
  48.7 1.8 %collective-permute-start.23 = (bf16[2,128,512]{2,1,0:T(8,128)(2,1)S(1)}, bf16[2,128,512]{2,1,0:T(8,128)(2,1)S(1)}, u32[]{:S(2)}, u32[]{:S(2)}) collective-permute-start(bf16[2,128,512]{2,1,0:T(8,128)(2,1)S(1)} %get-tuple-element.76), channel_id=1, source_target_pairs={{0,1},{1,0},{2,3},{3,2},{4,5},{5,4},{6,7},{7,6},{8,9},{9,8},{10,11... | collective-permute-start | bytes 786440 | tf_op jit(solution)/shard_map/ppermute | solution.py:23
  52.9 1.4 %collective-permute-start.27 = (bf16[2,128,512]{2,1,0:T(8,128)(2,1)S(1)}, bf16[2,128,512]{2,1,0:T(8,128)(2,1)S(1)}, u32[]{:S(2)}, u32[]{:S(2)}) collective-permute-start(bf16[2,128,512]{2,1,0:T(8,128)(2,1)S(1)} %get-tuple-element.74), channel_id=1, source_target_pairs={{0,3},{1,2},{2,1},{3,0},{4,7},{5,6},{6,5},{7,4},{8,11},{9,10},{10,... | collective-permute-start | bytes 786440 | tf_op jit(solution)/shard_map/ppermute | solution.py:23
  54.3 6.7 %attention.3 = (bf16[2,128,512]{2,1,0:T(8,128)(2,1)S(1)}, bf16[2,128,512]{2,1,0:T(8,128)(2,1)S(1)}, bf16[2,128,512]{2,1,0:T(8,128)(2,1)S(1)}, bf16[2,128,512]{2,...) custom-call(bf16[4,128,512]{2,1,0:T(8,128)(2,1)S(1)} %pad_maximum_fusion.6.refs_0_, ...), custom_call_target="tpu_custom_call" | custom-call | flops 1761607680 | bytes 6291456 | tf_op jit(solution)/shard_map/attention/pallas_call | solution.py:89
  61.1 2.9 %collective-permute-start.15 = (bf16[2,16,512]{2,1,0:T(8,128)(2,1)S(1)}, bf16[2,16,512]{2,1,0:T(8,128)(2,1)S(1)}, u32[]{:S(2)}, u32[]{:S(2)}) collective-permute-start(bf16[2,16,512]{2,1,0:T(8,128)(2,1)S(1)} %fusion.36), channel_id=1, source_target_pairs={{0,16},{4,20},{8,24},{12,28},{16,0},{20,4},{24,8},{28,12},{1,17},{... | collective-permute-start | bytes 98312 | tf_op jit(solution)/shard_map/ppermute | solution.py:23
  65.7 1.8 %collective-permute-start.24 = (bf16[2,16,512]{2,1,0:T(8,128)(2,1)S(1)}, bf16[2,16,512]{2,1,0:T(8,128)(2,1)S(1)}, u32[]{:S(2)}, u32[]{:S(2)}) collective-permute-start(bf16[2,16,512]{2,1,0:T(8,128)(2,1)S(1)} %fusion.34), channel_id=1, source_target_pairs={{0,8},{4,12},{8,0},{12,4},{16,24},{20,28},{24,16},{28,20},{1,9},{5... | collective-permute-start | bytes 98312 | tf_op jit(solution)/shard_map/ppermute | solution.py:23
  67.6 4.1 %collective-permute-start.19 = (bf16[2,128,512]{2,1,0:T(8,128)(2,1)S(1)}, bf16[2,128,512]{2,1,0:T(8,128)(2,1)S(1)}, u32[]{:S(2)}, u32[]{:S(2)}) collective-permute-start(bf16[2,128,512]{2,1,0:T(8,128)(2,1)S(1)} %get-tuple-element.61), channel_id=1, source_target_pairs={{0,3},{1,2},{2,1},{3,0},{4,7},{5,6},{6,5},{7,4},{8,11},{9,10},{10,... | collective-permute-start | bytes 786440 | tf_op jit(solution)/shard_map/ppermute | solution.py:23
  73.1 3.0 %collective-permute-done.27 = bf16[2,128,512]{2,1,0:T(8,128)(2,1)S(1)} collective-permute-done((bf16[2,128,512]{2,1,0:T(8,128)(2,1)S(1)}, bf16[2,128,512]{2,1,0:T(8,128)(2,1)S(1)}, u32[]{:S(2)}, u32[]{:S(2)}) %collective-permute-start.27) | collective-permute-done | bytes 262176 | tf_op jit(solution)/shard_map/ppermute | solution.py:23
  77.3 1.5 %collective-permute-start.30 = (bf16[2,128,512]{2,1,0:T(8,128)(2,1)S(1)}, bf16[2,128,512]{2,1,0:T(8,128)(2,1)S(1)}, u32[]{:S(2)}, u32[]{:S(2)}) collective-permute-start(bf16[2,128,512]{2,1,0:T(8,128)(2,1)S(1)} %get-tuple-element.70), channel_id=1, source_target_pairs={{0,3},{1,2},{2,1},{3,0},{4,7},{5,6},{6,5},{7,4},{8,11},{9,10},{10,... | collective-permute-start | bytes 786440 | tf_op jit(solution)/shard_map/ppermute | solution.py:23
  78.9 8.5 %collective-permute-done.19 = bf16[2,128,512]{2,1,0:T(8,128)(2,1)S(1)} collective-permute-done((bf16[2,128,512]{2,1,0:T(8,128)(2,1)S(1)}, bf16[2,128,512]{2,1,0:T(8,128)(2,1)S(1)}, u32[]{:S(2)}, u32[]{:S(2)}) %collective-permute-start.19) | collective-permute-done | bytes 262176 | tf_op jit(solution)/shard_map/ppermute | solution.py:23
  87.4 1.4 %collective-permute-done.29 = bf16[2,128,512]{2,1,0:T(8,128)(2,1)S(1)} collective-permute-done((bf16[2,128,512]{2,1,0:T(8,128)(2,1)S(1)}, bf16[2,128,512]{2,1,0:T(8,128)(2,1)S(1)}, u32[]{:S(2)}, u32[]{:S(2)}) %collective-permute-start.29) | collective-permute-done | bytes 262176 | tf_op jit(solution)/shard_map/ppermute | solution.py:23
  88.9 7.5 %collective-permute-done.30 = bf16[2,128,512]{2,1,0:T(8,128)(2,1)S(1)} collective-permute-done((bf16[2,128,512]{2,1,0:T(8,128)(2,1)S(1)}, bf16[2,128,512]{2,1,0:T(8,128)(2,1)S(1)}, u32[]{:S(2)}, u32[]{:S(2)}) %collective-permute-start.30) | collective-permute-done | bytes 262176 | tf_op jit(solution)/shard_map/ppermute | solution.py:23
  (112 shorter events, 21.1 us)
Async XLA Ops:
  1.8 10.1 %collective-permute-start.4 = (bf16[2,128,512]{2,1,0:T(8,128)(2,1)S(1)}, bf16[2,128,512]{2,1,0:T(8,128)(2,1)S(1)}, u32[]{:S(2)}, u32[]{:S(2)}) collective-permute-start(bf16[2,128,512]{2,1,0:T(8,128)(2,1)S(1)} %bitcast.240), channel_id=1, source_target_pairs={{0,2},{1,3},{2,0},{3,1},{4,6},{5,7},{6,4},{7,5},{8,10},{9,11},{10,... | collective-permute-start | bytes 786440 | tf_op jit(solution)/shard_map/ppermute | solution.py:23
  7.6 4.3 %collective-permute-start.3 = (f32[2,4,1024]{2,1,0:T(4,128)S(1)}, f32[2,4,1024]{2,1,0:T(4,128)S(1)}, u32[]{:S(2)}, u32[]{:S(2)}) collective-permute-start(f32[2,4,1024]{2,1,0:T(4,128)S(1)} %get-tuple-element.143), channel_id=1, source_target_pairs={{0,3},{1,2},{2,1},{3,0},{4,7},{5,6},{6,5},{7,4},{8,11},{9,10},{10,... | collective-permute-start | bytes 98312 | tf_op jit(solution)/shard_map/ppermute | solution.py:23
  9.2 11.4 %collective-permute-start.9 = (bf16[4,128,512]{2,1,0:T(8,128)(2,1)S(1)}, bf16[4,128,512]{2,1,0:T(8,128)(2,1)S(1)}, u32[]{:S(2)}, u32[]{:S(2)}) collective-permute-start(bf16[4,128,512]{2,1,0:T(8,128)(2,1)S(1)} %pad_maximum_fusion.5), channel_id=1, source_target_pairs={{0,1},{1,0},{2,3},{3,2},{4,5},{5,4},{6,7},{7,6},{8,9},{9,8},{10,11... | collective-permute-start | bytes 1572872 | tf_op jit(solution)/shard_map/ppermute | solution.py:23
  9.5 21.8 %collective-permute-start.6 = (bf16[4,128,512]{2,1,0:T(8,128)(2,1)S(1)}, bf16[4,128,512]{2,1,0:T(8,128)(2,1)S(1)}, u32[]{:S(2)}, u32[]{:S(2)}) collective-permute-start(bf16[4,128,512]{2,1,0:T(8,128)(2,1)S(1)} %pad_maximum_fusion.2), channel_id=1, source_target_pairs={{0,3},{1,2},{2,1},{3,0},{4,7},{5,6},{6,5},{7,4},{8,11},{9,10},{10,... | collective-permute-start | bytes 1572872 | tf_op jit(solution)/shard_map/ppermute | solution.py:23
  10.9 20.4 %collective-permute-start.5 = (bf16[2,128,512]{2,1,0:T(8,128)(2,1)S(1)}, bf16[2,128,512]{2,1,0:T(8,128)(2,1)S(1)}, u32[]{:S(2)}, u32[]{:S(2)}) collective-permute-start(bf16[2,128,512]{2,1,0:T(8,128)(2,1)S(1)} %pad_maximum_fusion.7), channel_id=1, source_target_pairs={{0,2},{1,3},{2,0},{3,1},{4,6},{5,7},{6,4},{7,5},{8,10},{9,11},{10,... | collective-permute-start | bytes 786440 | tf_op jit(solution)/shard_map/ppermute | solution.py:23
  11.9 4.4 %collective-permute-start.7 = (f32[2,16,1024]{2,1,0:T(8,128)S(1)}, f32[2,16,1024]{2,1,0:T(8,128)S(1)}, u32[]{:S(2)}, u32[]{:S(2)}) collective-permute-start(f32[2,16,1024]{2,1,0:T(8,128)S(1)} %pad_maximum_fusion.9), channel_id=1, source_target_pairs={{0,4},{4,0},{8,12},{12,8},{16,20},{20,16},{24,28},{28,24},{1,5},{5... | collective-permute-start | bytes 393224 | tf_op jit(solution)/shard_map/ppermute | solution.py:23
  13.6 17.8 %collective-permute-start = (bf16[4,128,512]{2,1,0:T(8,128)(2,1)S(1)}, bf16[4,128,512]{2,1,0:T(8,128)(2,1)S(1)}, u32[]{:S(2)}, u32[]{:S(2)}) collective-permute-start(bf16[4,128,512]{2,1,0:T(8,128)(2,1)S(1)} %pad_maximum_fusion.1), channel_id=1, source_target_pairs={{0,1},{1,0},{2,3},{3,2},{4,5},{5,4},{6,7},{7,6},{8,9},{9,8},{10,11... | collective-permute-start | bytes 1572872 | tf_op jit(solution)/shard_map/ppermute | solution.py:23
  16.4 4.2 %collective-permute-start.8 = (f32[2,16,1024]{2,1,0:T(8,128)S(1)}, f32[2,16,1024]{2,1,0:T(8,128)S(1)}, u32[]{:S(2)}, u32[]{:S(2)}) collective-permute-start(f32[2,16,1024]{2,1,0:T(8,128)S(1)} %get-tuple-element.139), channel_id=1, source_target_pairs={{0,8},{4,12},{8,0},{12,4},{16,24},{20,28},{24,16},{28,20},{1,9},{5... | collective-permute-start | bytes 393224 | tf_op jit(solution)/shard_map/ppermute | solution.py:23
  20.6 6.5 %collective-permute-start.10 = (bf16[2,16,1024]{2,1,0:T(8,128)(2,1)S(1)}, bf16[2,16,1024]{2,1,0:T(8,128)(2,1)S(1)}, u32[]{:S(2)}, u32[]{:S(2)}) collective-permute-start(bf16[2,16,1024]{2,1,0:T(8,128)(2,1)S(1)} %add_multiply_fusion), channel_id=1, source_target_pairs={{0,16},{4,20},{8,24},{12,28},{16,0},{20,4},{24,8},{28,12},{1,17},{... | collective-permute-start | bytes 196616 | tf_op jit(solution)/shard_map/ppermute | solution.py:23
  23.1 29.9 %collective-permute-start.12 = (bf16[4,128,512]{2,1,0:T(8,128)(2,1)S(1)}, bf16[4,128,512]{2,1,0:T(8,128)(2,1)S(1)}, u32[]{:S(2)}, u32[]{:S(2)}) collective-permute-start(bf16[4,128,512]{2,1,0:T(8,128)(2,1)S(1)} %pad_maximum_fusion.3), channel_id=1, source_target_pairs={{0,2},{1,3},{2,0},{3,1},{4,6},{5,7},{6,4},{7,5},{8,10},{9,11},{10,... | collective-permute-start | bytes 1572872 | tf_op jit(solution)/shard_map/ppermute | solution.py:23
  27.2 27.1 %collective-permute-start.13 = (bf16[4,128,512]{2,1,0:T(8,128)(2,1)S(1)}, bf16[4,128,512]{2,1,0:T(8,128)(2,1)S(1)}, u32[]{:S(2)}, u32[]{:S(2)}) collective-permute-start(bf16[4,128,512]{2,1,0:T(8,128)(2,1)S(1)} %pad_maximum_fusion.4), channel_id=1, source_target_pairs={{0,3},{1,2},{2,1},{3,0},{4,7},{5,6},{6,5},{7,4},{8,11},{9,10},{10,... | collective-permute-start | bytes 1572872 | tf_op jit(solution)/shard_map/ppermute | solution.py:23
  40.4 20.6 %collective-permute-start.14 = (bf16[2,128,512]{2,1,0:T(8,128)(2,1)S(1)}, bf16[2,128,512]{2,1,0:T(8,128)(2,1)S(1)}, u32[]{:S(2)}, u32[]{:S(2)}) collective-permute-start(bf16[2,128,512]{2,1,0:T(8,128)(2,1)S(1)} %get-tuple-element.53), channel_id=1, source_target_pairs={{0,2},{1,3},{2,0},{3,1},{4,6},{5,7},{6,4},{7,5},{8,10},{9,11},{10,... | collective-permute-start | bytes 786440 | tf_op jit(solution)/shard_map/ppermute | solution.py:23
  50.8 14.3 %collective-permute-start.16 = (bf16[2,128,512]{2,1,0:T(8,128)(2,1)S(1)}, bf16[2,128,512]{2,1,0:T(8,128)(2,1)S(1)}, u32[]{:S(2)}, u32[]{:S(2)}) collective-permute-start(bf16[2,128,512]{2,1,0:T(8,128)(2,1)S(1)} %get-tuple-element.56), channel_id=1, source_target_pairs={{0,3},{1,2},{2,1},{3,0},{4,7},{5,6},{6,5},{7,4},{8,11},{9,10},{10,... | collective-permute-start | bytes 786440 | tf_op jit(solution)/shard_map/ppermute | solution.py:23
  52.0 15.6 %collective-permute-start.25 = (bf16[2,128,512]{2,1,0:T(8,128)(2,1)S(1)}, bf16[2,128,512]{2,1,0:T(8,128)(2,1)S(1)}, u32[]{:S(2)}, u32[]{:S(2)}) collective-permute-start(bf16[2,128,512]{2,1,0:T(8,128)(2,1)S(1)} %get-tuple-element.75), channel_id=1, source_target_pairs={{0,2},{1,3},{2,0},{3,1},{4,6},{5,7},{6,4},{7,5},{8,10},{9,11},{10,... | collective-permute-start | bytes 786440 | tf_op jit(solution)/shard_map/ppermute | solution.py:23
  52.9 23.1 %collective-permute-start.27 = (bf16[2,128,512]{2,1,0:T(8,128)(2,1)S(1)}, bf16[2,128,512]{2,1,0:T(8,128)(2,1)S(1)}, u32[]{:S(2)}, u32[]{:S(2)}) collective-permute-start(bf16[2,128,512]{2,1,0:T(8,128)(2,1)S(1)} %get-tuple-element.74), channel_id=1, source_target_pairs={{0,3},{1,2},{2,1},{3,0},{4,7},{5,6},{6,5},{7,4},{8,11},{9,10},{10,... | collective-permute-start | bytes 786440 | tf_op jit(solution)/shard_map/ppermute | solution.py:23
  61.1 4.7 %collective-permute-start.15 = (bf16[2,16,512]{2,1,0:T(8,128)(2,1)S(1)}, bf16[2,16,512]{2,1,0:T(8,128)(2,1)S(1)}, u32[]{:S(2)}, u32[]{:S(2)}) collective-permute-start(bf16[2,16,512]{2,1,0:T(8,128)(2,1)S(1)} %fusion.36), channel_id=1, source_target_pairs={{0,16},{4,20},{8,24},{12,28},{16,0},{20,4},{24,8},{28,12},{1,17},{... | collective-permute-start | bytes 98312 | tf_op jit(solution)/shard_map/ppermute | solution.py:23
  64.0 13.3 %collective-permute-start.17 = (bf16[2,128,512]{2,1,0:T(8,128)(2,1)S(1)}, bf16[2,128,512]{2,1,0:T(8,128)(2,1)S(1)}, u32[]{:S(2)}, u32[]{:S(2)}) collective-permute-start(bf16[2,128,512]{2,1,0:T(8,128)(2,1)S(1)} %get-tuple-element.59), channel_id=1, source_target_pairs={{0,1},{1,0},{2,3},{3,2},{4,5},{5,4},{6,7},{7,6},{8,9},{9,8},{10,11... | collective-permute-start | bytes 786440 | tf_op jit(solution)/shard_map/ppermute | solution.py:23
  65.1 13.7 %collective-permute-start.18 = (bf16[2,128,512]{2,1,0:T(8,128)(2,1)S(1)}, bf16[2,128,512]{2,1,0:T(8,128)(2,1)S(1)}, u32[]{:S(2)}, u32[]{:S(2)}) collective-permute-start(bf16[2,128,512]{2,1,0:T(8,128)(2,1)S(1)} %get-tuple-element.60), channel_id=1, source_target_pairs={{0,2},{1,3},{2,0},{3,1},{4,6},{5,7},{6,4},{7,5},{8,10},{9,11},{10,... | collective-permute-start | bytes 786440 | tf_op jit(solution)/shard_map/ppermute | solution.py:23
  65.7 5.9 %collective-permute-start.24 = (bf16[2,16,512]{2,1,0:T(8,128)(2,1)S(1)}, bf16[2,16,512]{2,1,0:T(8,128)(2,1)S(1)}, u32[]{:S(2)}, u32[]{:S(2)}) collective-permute-start(bf16[2,16,512]{2,1,0:T(8,128)(2,1)S(1)} %fusion.34), channel_id=1, source_target_pairs={{0,8},{4,12},{8,0},{12,4},{16,24},{20,28},{24,16},{28,20},{1,9},{5... | collective-permute-start | bytes 98312 | tf_op jit(solution)/shard_map/ppermute | solution.py:23
  67.6 19.7 %collective-permute-start.19 = (bf16[2,128,512]{2,1,0:T(8,128)(2,1)S(1)}, bf16[2,128,512]{2,1,0:T(8,128)(2,1)S(1)}, u32[]{:S(2)}, u32[]{:S(2)}) collective-permute-start(bf16[2,128,512]{2,1,0:T(8,128)(2,1)S(1)} %get-tuple-element.61), channel_id=1, source_target_pairs={{0,3},{1,2},{2,1},{3,0},{4,7},{5,6},{6,5},{7,4},{8,11},{9,10},{10,... | collective-permute-start | bytes 786440 | tf_op jit(solution)/shard_map/ppermute | solution.py:23
  71.7 4.4 %collective-permute-start.26 = (bf16[2,16,512]{2,1,0:T(8,128)(2,1)S(1)}, bf16[2,16,512]{2,1,0:T(8,128)(2,1)S(1)}, u32[]{:S(2)}, u32[]{:S(2)}) collective-permute-start(bf16[2,16,512]{2,1,0:T(8,128)(2,1)S(1)} %fusion.35), channel_id=1, source_target_pairs={{0,4},{4,0},{8,12},{12,8},{16,20},{20,16},{24,28},{28,24},{1,5},{5... | collective-permute-start | bytes 98312 | tf_op jit(solution)/shard_map/ppermute | solution.py:23
  76.4 10.9 %collective-permute-start.28 = (bf16[2,128,512]{2,1,0:T(8,128)(2,1)S(1)}, bf16[2,128,512]{2,1,0:T(8,128)(2,1)S(1)}, u32[]{:S(2)}, u32[]{:S(2)}) collective-permute-start(bf16[2,128,512]{2,1,0:T(8,128)(2,1)S(1)} %get-tuple-element.72), channel_id=1, source_target_pairs={{0,1},{1,0},{2,3},{3,2},{4,5},{5,4},{6,7},{7,6},{8,9},{9,8},{10,11... | collective-permute-start | bytes 786440 | tf_op jit(solution)/shard_map/ppermute | solution.py:23
  76.5 12.3 %collective-permute-start.29 = (bf16[2,128,512]{2,1,0:T(8,128)(2,1)S(1)}, bf16[2,128,512]{2,1,0:T(8,128)(2,1)S(1)}, u32[]{:S(2)}, u32[]{:S(2)}) collective-permute-start(bf16[2,128,512]{2,1,0:T(8,128)(2,1)S(1)} %get-tuple-element.71), channel_id=1, source_target_pairs={{0,2},{1,3},{2,0},{3,1},{4,6},{5,7},{6,4},{7,5},{8,10},{9,11},{10,... | collective-permute-start | bytes 786440 | tf_op jit(solution)/shard_map/ppermute | solution.py:23
  77.3 19.1 %collective-permute-start.30 = (bf16[2,128,512]{2,1,0:T(8,128)(2,1)S(1)}, bf16[2,128,512]{2,1,0:T(8,128)(2,1)S(1)}, u32[]{:S(2)}, u32[]{:S(2)}) collective-permute-start(bf16[2,128,512]{2,1,0:T(8,128)(2,1)S(1)} %get-tuple-element.70), channel_id=1, source_target_pairs={{0,3},{1,2},{2,1},{3,0},{4,7},{5,6},{6,5},{7,4},{8,11},{9,10},{10,... | collective-permute-start | bytes 786440 | tf_op jit(solution)/shard_map/ppermute | solution.py:23
  (15 other events, 53.9 us)

commit v5 on v4

--- a/solution.py
+++ b/solution.py
@@ -11,6 +11,7 @@
 HD = 128
 CROWS = 16
 SCALE = HD**-0.5
+LOW = ((2,), ())
 PACE = (
     (),
     ((("mid", 0, 2),), (("mid", 0, 3),), (("last", 0, 2),), (("last", 0, 3),)),
@@ -205,13 +206,15 @@
         for part in far:
             send(sent[part], part, ("mid", g, part))
 
-    def chain(coarse_grad, pace):
+    def chain(coarse_grad, pace, low):
         pace = list(pace) + [()] * (depth + 1)
         coarse_grad = after(coarse_grad, pace[0])
         above = jnp.zeros(coarse_grad[:, 0].shape, jnp.float32)
         for level in reversed(range(depth)):
             outgoing = coarse_grad[:, level] + 0.5 * above
-            received = swapped(outgoing.astype(jnp.bfloat16), "seq", 1 << level)
+            if level in low:
+                outgoing = outgoing.astype(jnp.bfloat16)
+            received = swapped(outgoing, "seq", 1 << level)
             received = after(received, pace[depth - level])
             above = 0.5 * above + received.astype(jnp.float32)
         return above / float(pool_size)
@@ -222,9 +225,14 @@
 
     own_last, near_last = [], []
     for g in range(groups):
-        above = chain(sums[g], PACE[g])
-        for part in far:
-            send(total(part, grads[g], above), part, ("last", g, part))
+        above = chain(sums[g], PACE[g], LOW[g])
+        for part in far:
+            block = total(part, grads[g], above)
+            if g == groups - 1:
+                send(block[:1], part, ("last", g, part, 0))
+                send(block[1:], part, ("last", g, part, 1))
+            else:
+                send(block, part, ("last", g, part))
         own_last.append(total(0, grads[g], above))
         near_last.append(total(1, grads[g], above))
     near = [swapped(kept[g][1], "head", 1) for g in range(groups)]
@@ -245,7 +253,11 @@
         place(2, near_last[g], 1, starts[g])
         for part in far:
             place(0, landed["mid", g, part], part, starts[g])
-            place(2, landed["last", g, part], part, starts[g])
+            if g == groups - 1:
+                place(2, landed["last", g, part, 0], part, starts[g])
+                place(3, landed["last", g, part, 1], part, starts[g])
+            else:
+                place(2, landed["last", g, part], part, starts[g])
     return tuple(outs)
 
 

time: 97.9 us -> 97.5 us (level)
    ppermute x31 -> x33, starting transfers between devices: 48.1 us -> 47.6 us  [swapped(): return lax.ppermute(block, axis, [(i, i ^ mask) for i in range(count)])]
    ppermute x31 -> x33, waiting for transfers between devices: 28 us -> 28.4 us  [swapped(): return lax.ppermute(block, axis, [(i, i ^ mask) for i in range(count)])]
  transfers between devices with their start and end apart: 31 -> 33, of which waited for: 12 -> 11; matrix products, arithmetic and copies ran while one was open for 3% -> 3% of each run, Pallas kernels for 14% -> 14%
where the time goes in v5:
time: 97.5 us; the launch traced here: 97.4 us
  starting transfers between devices  47.6 us (49%)
  waiting for transfers between devices  28.4 us (29%)
  Pallas kernels  13.5 us (14%)
  local copies, waits for them, and re-layouts  3.58 us (4%)
  other arithmetic  3.01 us (3%)
  between operations  1.26 us (1%)
    ppermute x33, starting transfers between devices, swapped(): return lax.ppermute(block, axis, [(i, i ^ mask) for i in range(count)])  47.6 us
    ppermute x33, waiting for transfers between devices, swapped(): return lax.ppermute(block, axis, [(i, i ^ mask) for i in range(count)])  28.4 us
    pallas_call x2, Pallas kernels, attention(): pl.pallas_call(functools.partial(attention_kernel, layout, depth, pool_si...  13.5 us
    unnamed x16, local copies, waits for them, and re-layouts  2.19 us
  transfers between devices with their start and end apart: 33, of which 11 were waited for; matrix products, arithmetic and copies ran while one was open for 3% of the time, Pallas kernels for 14%

profile of v5, /device:TPU:1, one launch (start us, length us, event | category | flops | bytes accessed | tf_op | source)
XLA Modules:
  0.0 97.4 jit_solution(12883557165875535108)
XLA Ops:
  1.8 2.1 %collective-permute-start.4 = (bf16[2,128,512]{2,1,0:T(8,128)(2,1)S(1)}, bf16[2,128,512]{2,1,0:T(8,128)(2,1)S(1)}, u32[]{:S(2)}, u32[]{:S(2)}) collective-permute-start(bf16[2,128,512]{2,1,0:T(8,128)(2,1)S(1)} %bitcast.224), channel_id=1, source_target_pairs={{0,2},{1,3},{2,0},{3,1},{4,6},{5,7},{6,4},{7,5},{8,10},{9,11},{10,... | collective-permute-start | bytes 786440 | tf_op jit(solution)/shard_map/ppermute | solution.py:24
  7.6 1.5 %collective-permute-start.3 = (f32[2,4,1024]{2,1,0:T(4,128)S(1)}, f32[2,4,1024]{2,1,0:T(4,128)S(1)}, u32[]{:S(2)}, u32[]{:S(2)}) collective-permute-start(f32[2,4,1024]{2,1,0:T(4,128)S(1)} %get-tuple-element.143), channel_id=1, source_target_pairs={{0,3},{1,2},{2,1},{3,0},{4,7},{5,6},{6,5},{7,4},{8,11},{9,10},{10,... | collective-permute-start | bytes 98312 | tf_op jit(solution)/shard_map/ppermute | solution.py:24
  11.9 1.6 %collective-permute-start.7 = (f32[2,16,1024]{2,1,0:T(8,128)S(1)}, f32[2,16,1024]{2,1,0:T(8,128)S(1)}, u32[]{:S(2)}, u32[]{:S(2)}) collective-permute-start(f32[2,16,1024]{2,1,0:T(8,128)S(1)} %pad_maximum_fusion.9), channel_id=1, source_target_pairs={{0,4},{4,0},{8,12},{12,8},{16,20},{20,16},{24,28},{28,24},{1,5},{5... | collective-permute-start | bytes 393224 | tf_op jit(solution)/shard_map/ppermute | solution.py:24
  13.6 2.7 %collective-permute-start = (bf16[4,128,512]{2,1,0:T(8,128)(2,1)S(1)}, bf16[4,128,512]{2,1,0:T(8,128)(2,1)S(1)}, u32[]{:S(2)}, u32[]{:S(2)}) collective-permute-start(bf16[4,128,512]{2,1,0:T(8,128)(2,1)S(1)} %pad_maximum_fusion.1), channel_id=1, source_target_pairs={{0,1},{1,0},{2,3},{3,2},{4,5},{5,4},{6,7},{7,6},{8,9},{9,8},{10,11... | collective-permute-start | bytes 1572872 | tf_op jit(solution)/shard_map/ppermute | solution.py:24
  16.4 1.4 %collective-permute-start.8 = (f32[2,16,1024]{2,1,0:T(8,128)S(1)}, f32[2,16,1024]{2,1,0:T(8,128)S(1)}, u32[]{:S(2)}, u32[]{:S(2)}) collective-permute-start(f32[2,16,1024]{2,1,0:T(8,128)S(1)} %get-tuple-element.139), channel_id=1, source_target_pairs={{0,8},{4,12},{8,0},{12,4},{16,24},{20,28},{24,16},{28,20},{1,9},{5... | collective-permute-start | bytes 393224 | tf_op jit(solution)/shard_map/ppermute | solution.py:24
  17.9 2.7 %collective-permute-done.8 = f32[2,16,1024]{2,1,0:T(8,128)S(1)} collective-permute-done((f32[2,16,1024]{2,1,0:T(8,128)S(1)}, f32[2,16,1024]{2,1,0:T(8,128)S(1)}, u32[]{:S(2)}, u32[]{:S(2)}) %collective-permute-start.8) | collective-permute-done | bytes 131104 | tf_op jit(solution)/shard_map/ppermute | solution.py:24
  20.6 2.4 %collective-permute-start.10 = (bf16[2,16,1024]{2,1,0:T(8,128)(2,1)S(1)}, bf16[2,16,1024]{2,1,0:T(8,128)(2,1)S(1)}, u32[]{:S(2)}, u32[]{:S(2)}) collective-permute-start(bf16[2,16,1024]{2,1,0:T(8,128)(2,1)S(1)} %add_multiply_fusion), channel_id=1, source_target_pairs={{0,16},{4,20},{8,24},{12,28},{16,0},{20,4},{24,8},{28,12},{1,17},{... | collective-permute-start | bytes 196616 | tf_op jit(solution)/shard_map/ppermute | solution.py:24
  23.1 4.1 %collective-permute-start.12 = (bf16[4,128,512]{2,1,0:T(8,128)(2,1)S(1)}, bf16[4,128,512]{2,1,0:T(8,128)(2,1)S(1)}, u32[]{:S(2)}, u32[]{:S(2)}) collective-permute-start(bf16[4,128,512]{2,1,0:T(8,128)(2,1)S(1)} %pad_maximum_fusion.3), channel_id=1, source_target_pairs={{0,2},{1,3},{2,0},{3,1},{4,6},{5,7},{6,4},{7,5},{8,10},{9,11},{10,... | collective-permute-start | bytes 1572872 | tf_op jit(solution)/shard_map/ppermute | solution.py:24
  27.2 4.1 %collective-permute-start.13 = (bf16[4,128,512]{2,1,0:T(8,128)(2,1)S(1)}, bf16[4,128,512]{2,1,0:T(8,128)(2,1)S(1)}, u32[]{:S(2)}, u32[]{:S(2)}) collective-permute-start(bf16[4,128,512]{2,1,0:T(8,128)(2,1)S(1)} %pad_maximum_fusion.4), channel_id=1, source_target_pairs={{0,3},{1,2},{2,1},{3,0},{4,7},{5,6},{6,5},{7,4},{8,11},{9,10},{10,... | collective-permute-start | bytes 1572872 | tf_op jit(solution)/shard_map/ppermute | solution.py:24
  31.3 6.7 %attention.2 = (bf16[2,128,512]{2,1,0:T(8,128)(2,1)S(1)}, bf16[2,128,512]{2,1,0:T(8,128)(2,1)S(1)}, bf16[2,128,512]{2,1,0:T(8,128)(2,1)S(1)}, bf16[2,128,512]{2,...) custom-call(bf16[4,128,512]{2,1,0:T(8,128)(2,1)S(1)} %pad_maximum_fusion.refs_0_, ...), custom_call_target="tpu_custom_call" | custom-call | flops 1761607680 | bytes 6291456 | tf_op jit(solution)/shard_map/attention/pallas_call | solution.py:90
  38.1 2.3 %collective-permute-start.20 = (bf16[2,16,512]{2,1,0:T(8,128)(2,1)S(1)}, bf16[2,16,512]{2,1,0:T(8,128)(2,1)S(1)}, u32[]{:S(2)}, u32[]{:S(2)}) collective-permute-start(bf16[2,16,512]{2,1,0:T(8,128)(2,1)S(1)} %fusion.28), channel_id=1, source_target_pairs={{0,16},{4,20},{8,24},{12,28},{16,0},{20,4},{24,8},{28,12},{1,17},{... | collective-permute-start | bytes 98312 | tf_op jit(solution)/shard_map/ppermute | solution.py:24
  41.8 1.8 %collective-permute-start.21 = (f32[2,16,512]{2,1,0:T(8,128)S(1)}, f32[2,16,512]{2,1,0:T(8,128)S(1)}, u32[]{:S(2)}, u32[]{:S(2)}) collective-permute-start(f32[2,16,512]{2,1,0:T(8,128)S(1)} %fusion.26), channel_id=1, source_target_pairs={{0,8},{4,12},{8,0},{12,4},{16,24},{20,28},{24,16},{28,20},{1,9},{5... | collective-permute-start | bytes 196616 | tf_op jit(solution)/shard_map/ppermute | solution.py:24
  43.8 2.1 %collective-permute-done.21 = f32[2,16,512]{2,1,0:T(8,128)S(1)} collective-permute-done((f32[2,16,512]{2,1,0:T(8,128)S(1)}, f32[2,16,512]{2,1,0:T(8,128)S(1)}, u32[]{:S(2)}, u32[]{:S(2)}) %collective-permute-start.21) | collective-permute-done | bytes 65568 | tf_op jit(solution)/shard_map/ppermute | solution.py:24
  49.7 1.7 %collective-permute-start.23 = (bf16[2,128,512]{2,1,0:T(8,128)(2,1)S(1)}, bf16[2,128,512]{2,1,0:T(8,128)(2,1)S(1)}, u32[]{:S(2)}, u32[]{:S(2)}) collective-permute-start(bf16[2,128,512]{2,1,0:T(8,128)(2,1)S(1)} %get-tuple-element.76), channel_id=1, source_target_pairs={{0,1},{1,0},{2,3},{3,2},{4,5},{5,4},{6,7},{7,6},{8,9},{9,8},{10,11... | collective-permute-start | bytes 786440 | tf_op jit(solution)/shard_map/ppermute | solution.py:24
  53.6 1.4 %collective-permute-start.27 = (bf16[2,128,512]{2,1,0:T(8,128)(2,1)S(1)}, bf16[2,128,512]{2,1,0:T(8,128)(2,1)S(1)}, u32[]{:S(2)}, u32[]{:S(2)}) collective-permute-start(bf16[2,128,512]{2,1,0:T(8,128)(2,1)S(1)} %get-tuple-element.74), channel_id=1, source_target_pairs={{0,3},{1,2},{2,1},{3,0},{4,7},{5,6},{6,5},{7,4},{8,11},{9,10},{10,... | collective-permute-start | bytes 786440 | tf_op jit(solution)/shard_map/ppermute | solution.py:24
  55.0 6.7 %attention.3 = (bf16[2,128,512]{2,1,0:T(8,128)(2,1)S(1)}, bf16[2,128,512]{2,1,0:T(8,128)(2,1)S(1)}, bf16[2,128,512]{2,1,0:T(8,128)(2,1)S(1)}, bf16[2,128,512]{2,...) custom-call(bf16[4,128,512]{2,1,0:T(8,128)(2,1)S(1)} %pad_maximum_fusion.6.refs_0_, ...), custom_call_target="tpu_custom_call" | custom-call | flops 1761607680 | bytes 6291456 | tf_op jit(solution)/shard_map/attention/pallas_call | solution.py:90
  61.8 3.0 %collective-permute-start.15 = (f32[2,16,512]{2,1,0:T(8,128)S(1)}, f32[2,16,512]{2,1,0:T(8,128)S(1)}, u32[]{:S(2)}, u32[]{:S(2)}) collective-permute-start(f32[2,16,512]{2,1,0:T(8,128)S(1)} %slice_bitcast_fusion.17), channel_id=1, source_target_pairs={{0,16},{4,20},{8,24},{12,28},{16,0},{20,4},{24,8},{28,12},{1,17},{... | collective-permute-start | bytes 196616 | tf_op jit(solution)/shard_map/ppermute | solution.py:24
  65.7 1.5 %collective-permute-done.15 = f32[2,16,512]{2,1,0:T(8,128)S(1)} collective-permute-done((f32[2,16,512]{2,1,0:T(8,128)S(1)}, f32[2,16,512]{2,1,0:T(8,128)S(1)}, u32[]{:S(2)}, u32[]{:S(2)}) %collective-permute-start.15) | collective-permute-done | bytes 65568 | tf_op jit(solution)/shard_map/ppermute | solution.py:24
  67.2 2.1 %collective-permute-start.24 = (f32[2,16,512]{2,1,0:T(8,128)S(1)}, f32[2,16,512]{2,1,0:T(8,128)S(1)}, u32[]{:S(2)}, u32[]{:S(2)}) collective-permute-start(f32[2,16,512]{2,1,0:T(8,128)S(1)} %fusion.27), channel_id=1, source_target_pairs={{0,8},{4,12},{8,0},{12,4},{16,24},{20,28},{24,16},{28,20},{1,9},{5... | collective-permute-start | bytes 196616 | tf_op jit(solution)/shard_map/ppermute | solution.py:24
  69.4 2.3 %collective-permute-start.19 = (bf16[2,128,512]{2,1,0:T(8,128)(2,1)S(1)}, bf16[2,128,512]{2,1,0:T(8,128)(2,1)S(1)}, u32[]{:S(2)}, u32[]{:S(2)}) collective-permute-start(bf16[2,128,512]{2,1,0:T(8,128)(2,1)S(1)} %get-tuple-element.61), channel_id=1, source_target_pairs={{0,3},{1,2},{2,1},{3,0},{4,7},{5,6},{6,5},{7,4},{8,11},{9,10},{10,... | collective-permute-start | bytes 786440 | tf_op jit(solution)/shard_map/ppermute | solution.py:24
  73.1 3.2 %collective-permute-done.27 = bf16[2,128,512]{2,1,0:T(8,128)(2,1)S(1)} collective-permute-done((bf16[2,128,512]{2,1,0:T(8,128)(2,1)S(1)}, bf16[2,128,512]{2,1,0:T(8,128)(2,1)S(1)}, u32[]{:S(2)}, u32[]{:S(2)}) %collective-permute-start.27) | collective-permute-done | bytes 262176 | tf_op jit(solution)/shard_map/ppermute | solution.py:24
  80.0 7.6 %collective-permute-done.19 = bf16[2,128,512]{2,1,0:T(8,128)(2,1)S(1)} collective-permute-done((bf16[2,128,512]{2,1,0:T(8,128)(2,1)S(1)}, bf16[2,128,512]{2,1,0:T(8,128)(2,1)S(1)}, u32[]{:S(2)}, u32[]{:S(2)}) %collective-permute-start.19) | collective-permute-done | bytes 262176 | tf_op jit(solution)/shard_map/ppermute | solution.py:24
  87.7 5.5 %collective-permute-done.32 = bf16[1,128,512]{2,1,0:T(8,128)(2,1)S(1)} collective-permute-done((bf16[1,128,512]{2,1,0:T(8,128)(2,1)S(1)}, bf16[1,128,512]{2,1,0:T(8,128)(2,1)S(1)}, u32[]{:S(2)}, u32[]{:S(2)}) %collective-permute-start.32) | collective-permute-done | bytes 131104 | tf_op jit(solution)/shard_map/ppermute | solution.py:24
  93.3 3.1 %collective-permute-done.30 = bf16[1,128,512]{2,1,0:T(8,128)(2,1)S(1)} collective-permute-done((bf16[1,128,512]{2,1,0:T(8,128)(2,1)S(1)}, bf16[1,128,512]{2,1,0:T(8,128)(2,1)S(1)}, u32[]{:S(2)}, u32[]{:S(2)}) %collective-permute-start.30) | collective-permute-done | bytes 131104 | tf_op jit(solution)/shard_map/ppermute | solution.py:24
  (120 shorter events, 22.4 us)
Async XLA Ops:
  1.8 10.1 %collective-permute-start.4 = (bf16[2,128,512]{2,1,0:T(8,128)(2,1)S(1)}, bf16[2,128,512]{2,1,0:T(8,128)(2,1)S(1)}, u32[]{:S(2)}, u32[]{:S(2)}) collective-permute-start(bf16[2,128,512]{2,1,0:T(8,128)(2,1)S(1)} %bitcast.224), channel_id=1, source_target_pairs={{0,2},{1,3},{2,0},{3,1},{4,6},{5,7},{6,4},{7,5},{8,10},{9,11},{10,... | collective-permute-start | bytes 786440 | tf_op jit(solution)/shard_map/ppermute | solution.py:24
  9.2 11.4 %collective-permute-start.9 = (bf16[4,128,512]{2,1,0:T(8,128)(2,1)S(1)}, bf16[4,128,512]{2,1,0:T(8,128)(2,1)S(1)}, u32[]{:S(2)}, u32[]{:S(2)}) collective-permute-start(bf16[4,128,512]{2,1,0:T(8,128)(2,1)S(1)} %pad_maximum_fusion.5), channel_id=1, source_target_pairs={{0,1},{1,0},{2,3},{3,2},{4,5},{5,4},{6,7},{7,6},{8,9},{9,8},{10,11... | collective-permute-start | bytes 1572872 | tf_op jit(solution)/shard_map/ppermute | solution.py:24
  9.5 21.8 %collective-permute-start.6 = (bf16[4,128,512]{2,1,0:T(8,128)(2,1)S(1)}, bf16[4,128,512]{2,1,0:T(8,128)(2,1)S(1)}, u32[]{:S(2)}, u32[]{:S(2)}) collective-permute-start(bf16[4,128,512]{2,1,0:T(8,128)(2,1)S(1)} %pad_maximum_fusion.2), channel_id=1, source_target_pairs={{0,3},{1,2},{2,1},{3,0},{4,7},{5,6},{6,5},{7,4},{8,11},{9,10},{10,... | collective-permute-start | bytes 1572872 | tf_op jit(solution)/shard_map/ppermute | solution.py:24
  10.9 20.4 %collective-permute-start.5 = (bf16[2,128,512]{2,1,0:T(8,128)(2,1)S(1)}, bf16[2,128,512]{2,1,0:T(8,128)(2,1)S(1)}, u32[]{:S(2)}, u32[]{:S(2)}) collective-permute-start(bf16[2,128,512]{2,1,0:T(8,128)(2,1)S(1)} %pad_maximum_fusion.7), channel_id=1, source_target_pairs={{0,2},{1,3},{2,0},{3,1},{4,6},{5,7},{6,4},{7,5},{8,10},{9,11},{10,... | collective-permute-start | bytes 786440 | tf_op jit(solution)/shard_map/ppermute | solution.py:24
  11.9 4.4 %collective-permute-start.7 = (f32[2,16,1024]{2,1,0:T(8,128)S(1)}, f32[2,16,1024]{2,1,0:T(8,128)S(1)}, u32[]{:S(2)}, u32[]{:S(2)}) collective-permute-start(f32[2,16,1024]{2,1,0:T(8,128)S(1)} %pad_maximum_fusion.9), channel_id=1, source_target_pairs={{0,4},{4,0},{8,12},{12,8},{16,20},{20,16},{24,28},{28,24},{1,5},{5... | collective-permute-start | bytes 393224 | tf_op jit(solution)/shard_map/ppermute | solution.py:24
  13.6 17.8 %collective-permute-start = (bf16[4,128,512]{2,1,0:T(8,128)(2,1)S(1)}, bf16[4,128,512]{2,1,0:T(8,128)(2,1)S(1)}, u32[]{:S(2)}, u32[]{:S(2)}) collective-permute-start(bf16[4,128,512]{2,1,0:T(8,128)(2,1)S(1)} %pad_maximum_fusion.1), channel_id=1, source_target_pairs={{0,1},{1,0},{2,3},{3,2},{4,5},{5,4},{6,7},{7,6},{8,9},{9,8},{10,11... | collective-permute-start | bytes 1572872 | tf_op jit(solution)/shard_map/ppermute | solution.py:24
  20.6 6.5 %collective-permute-start.10 = (bf16[2,16,1024]{2,1,0:T(8,128)(2,1)S(1)}, bf16[2,16,1024]{2,1,0:T(8,128)(2,1)S(1)}, u32[]{:S(2)}, u32[]{:S(2)}) collective-permute-start(bf16[2,16,1024]{2,1,0:T(8,128)(2,1)S(1)} %add_multiply_fusion), channel_id=1, source_target_pairs={{0,16},{4,20},{8,24},{12,28},{16,0},{20,4},{24,8},{28,12},{1,17},{... | collective-permute-start | bytes 196616 | tf_op jit(solution)/shard_map/ppermute | solution.py:24
  23.1 30.5 %collective-permute-start.12 = (bf16[4,128,512]{2,1,0:T(8,128)(2,1)S(1)}, bf16[4,128,512]{2,1,0:T(8,128)(2,1)S(1)}, u32[]{:S(2)}, u32[]{:S(2)}) collective-permute-start(bf16[4,128,512]{2,1,0:T(8,128)(2,1)S(1)} %pad_maximum_fusion.3), channel_id=1, source_target_pairs={{0,2},{1,3},{2,0},{3,1},{4,6},{5,7},{6,4},{7,5},{8,10},{9,11},{10,... | collective-permute-start | bytes 1572872 | tf_op jit(solution)/shard_map/ppermute | solution.py:24
  27.2 27.8 %collective-permute-start.13 = (bf16[4,128,512]{2,1,0:T(8,128)(2,1)S(1)}, bf16[4,128,512]{2,1,0:T(8,128)(2,1)S(1)}, u32[]{:S(2)}, u32[]{:S(2)}) collective-permute-start(bf16[4,128,512]{2,1,0:T(8,128)(2,1)S(1)} %pad_maximum_fusion.4), channel_id=1, source_target_pairs={{0,3},{1,2},{2,1},{3,0},{4,7},{5,6},{6,5},{7,4},{8,11},{9,10},{10,... | collective-permute-start | bytes 1572872 | tf_op jit(solution)/shard_map/ppermute | solution.py:24
  40.4 21.3 %collective-permute-start.14 = (bf16[2,128,512]{2,1,0:T(8,128)(2,1)S(1)}, bf16[2,128,512]{2,1,0:T(8,128)(2,1)S(1)}, u32[]{:S(2)}, u32[]{:S(2)}) collective-permute-start(bf16[2,128,512]{2,1,0:T(8,128)(2,1)S(1)} %get-tuple-element.53), channel_id=1, source_target_pairs={{0,2},{1,3},{2,0},{3,1},{4,6},{5,7},{6,4},{7,5},{8,10},{9,11},{10,... | collective-permute-start | bytes 786440 | tf_op jit(solution)/shard_map/ppermute | solution.py:24
  51.7 13.1 %collective-permute-start.16 = (bf16[2,128,512]{2,1,0:T(8,128)(2,1)S(1)}, bf16[2,128,512]{2,1,0:T(8,128)(2,1)S(1)}, u32[]{:S(2)}, u32[]{:S(2)}) collective-permute-start(bf16[2,128,512]{2,1,0:T(8,128)(2,1)S(1)} %get-tuple-element.56), channel_id=1, source_target_pairs={{0,3},{1,2},{2,1},{3,0},{4,7},{5,6},{6,5},{7,4},{8,11},{9,10},{10,... | collective-permute-start | bytes 786440 | tf_op jit(solution)/shard_map/ppermute | solution.py:24
  52.7 16.7 %collective-permute-start.25 = (bf16[2,128,512]{2,1,0:T(8,128)(2,1)S(1)}, bf16[2,128,512]{2,1,0:T(8,128)(2,1)S(1)}, u32[]{:S(2)}, u32[]{:S(2)}) collective-permute-start(bf16[2,128,512]{2,1,0:T(8,128)(2,1)S(1)} %get-tuple-element.75), channel_id=1, source_target_pairs={{0,2},{1,3},{2,0},{3,1},{4,6},{5,7},{6,4},{7,5},{8,10},{9,11},{10,... | collective-permute-start | bytes 786440 | tf_op jit(solution)/shard_map/ppermute | solution.py:24
  53.6 22.7 %collective-permute-start.27 = (bf16[2,128,512]{2,1,0:T(8,128)(2,1)S(1)}, bf16[2,128,512]{2,1,0:T(8,128)(2,1)S(1)}, u32[]{:S(2)}, u32[]{:S(2)}) collective-permute-start(bf16[2,128,512]{2,1,0:T(8,128)(2,1)S(1)} %get-tuple-element.74), channel_id=1, source_target_pairs={{0,3},{1,2},{2,1},{3,0},{4,7},{5,6},{6,5},{7,4},{8,11},{9,10},{10,... | collective-permute-start | bytes 786440 | tf_op jit(solution)/shard_map/ppermute | solution.py:24
  61.8 5.5 %collective-permute-start.15 = (f32[2,16,512]{2,1,0:T(8,128)S(1)}, f32[2,16,512]{2,1,0:T(8,128)S(1)}, u32[]{:S(2)}, u32[]{:S(2)}) collective-permute-start(f32[2,16,512]{2,1,0:T(8,128)S(1)} %slice_bitcast_fusion.17), channel_id=1, source_target_pairs={{0,16},{4,20},{8,24},{12,28},{16,0},{20,4},{24,8},{28,12},{1,17},{... | collective-permute-start | bytes 196616 | tf_op jit(solution)/shard_map/ppermute | solution.py:24
  64.7 13.2 %collective-permute-start.17 = (bf16[2,128,512]{2,1,0:T(8,128)(2,1)S(1)}, bf16[2,128,512]{2,1,0:T(8,128)(2,1)S(1)}, u32[]{:S(2)}, u32[]{:S(2)}) collective-permute-start(bf16[2,128,512]{2,1,0:T(8,128)(2,1)S(1)} %get-tuple-element.59), channel_id=1, source_target_pairs={{0,1},{1,0},{2,3},{3,2},{4,5},{5,4},{6,7},{7,6},{8,9},{9,8},{10,11... | collective-permute-start | bytes 786440 | tf_op jit(solution)/shard_map/ppermute | solution.py:24
  64.8 14.3 %collective-permute-start.18 = (bf16[2,128,512]{2,1,0:T(8,128)(2,1)S(1)}, bf16[2,128,512]{2,1,0:T(8,128)(2,1)S(1)}, u32[]{:S(2)}, u32[]{:S(2)}) collective-permute-start(bf16[2,128,512]{2,1,0:T(8,128)(2,1)S(1)} %get-tuple-element.60), channel_id=1, source_target_pairs={{0,2},{1,3},{2,0},{3,1},{4,6},{5,7},{6,4},{7,5},{8,10},{9,11},{10,... | collective-permute-start | bytes 786440 | tf_op jit(solution)/shard_map/ppermute | solution.py:24
  67.2 4.4 %collective-permute-start.24 = (f32[2,16,512]{2,1,0:T(8,128)S(1)}, f32[2,16,512]{2,1,0:T(8,128)S(1)}, u32[]{:S(2)}, u32[]{:S(2)}) collective-permute-start(f32[2,16,512]{2,1,0:T(8,128)S(1)} %fusion.27), channel_id=1, source_target_pairs={{0,8},{4,12},{8,0},{12,4},{16,24},{20,28},{24,16},{28,20},{1,9},{5... | collective-permute-start | bytes 196616 | tf_op jit(solution)/shard_map/ppermute | solution.py:24
  69.4 18.2 %collective-permute-start.19 = (bf16[2,128,512]{2,1,0:T(8,128)(2,1)S(1)}, bf16[2,128,512]{2,1,0:T(8,128)(2,1)S(1)}, u32[]{:S(2)}, u32[]{:S(2)}) collective-permute-start(bf16[2,128,512]{2,1,0:T(8,128)(2,1)S(1)} %get-tuple-element.61), channel_id=1, source_target_pairs={{0,3},{1,2},{2,1},{3,0},{4,7},{5,6},{6,5},{7,4},{8,11},{9,10},{10,... | collective-permute-start | bytes 786440 | tf_op jit(solution)/shard_map/ppermute | solution.py:24
  71.7 4.6 %collective-permute-start.26 = (f32[2,16,512]{2,1,0:T(8,128)S(1)}, f32[2,16,512]{2,1,0:T(8,128)S(1)}, u32[]{:S(2)}, u32[]{:S(2)}) collective-permute-start(f32[2,16,512]{2,1,0:T(8,128)S(1)} %bitcast_add_fusion.8), channel_id=1, source_target_pairs={{0,4},{4,0},{8,12},{12,8},{16,20},{20,16},{24,28},{28,24},{1,5},{5... | collective-permute-start | bytes 196616 | tf_op jit(solution)/shard_map/ppermute | solution.py:24
  76.7 11.0 %collective-permute-start.28 = (bf16[2,128,512]{2,1,0:T(8,128)(2,1)S(1)}, bf16[2,128,512]{2,1,0:T(8,128)(2,1)S(1)}, u32[]{:S(2)}, u32[]{:S(2)}) collective-permute-start(bf16[2,128,512]{2,1,0:T(8,128)(2,1)S(1)} %get-tuple-element.72), channel_id=1, source_target_pairs={{0,1},{1,0},{2,3},{3,2},{4,5},{5,4},{6,7},{7,6},{8,9},{9,8},{10,11... | collective-permute-start | bytes 786440 | tf_op jit(solution)/shard_map/ppermute | solution.py:24
  77.1 10.6 %collective-permute-start.31 = (bf16[1,128,512]{2,1,0:T(8,128)(2,1)S(1)}, bf16[1,128,512]{2,1,0:T(8,128)(2,1)S(1)}, u32[]{:S(2)}, u32[]{:S(2)}) collective-permute-start(bf16[1,128,512]{2,1,0:T(8,128)(2,1)S(1)} %get-tuple-element.110), channel_id=1, source_target_pairs={{0,2},{1,3},{2,0},{3,1},{4,6},{5,7},{6,4},{7,5},{8,10},{9,11},{10,... | collective-permute-start | bytes 393224 | tf_op jit(solution)/shard_map/ppermute | solution.py:24
  78.0 15.2 %collective-permute-start.32 = (bf16[1,128,512]{2,1,0:T(8,128)(2,1)S(1)}, bf16[1,128,512]{2,1,0:T(8,128)(2,1)S(1)}, u32[]{:S(2)}, u32[]{:S(2)}) collective-permute-start(bf16[1,128,512]{2,1,0:T(8,128)(2,1)S(1)} %get-tuple-element.108), channel_id=1, source_target_pairs={{0,3},{1,2},{2,1},{3,0},{4,7},{5,6},{6,5},{7,4},{8,11},{9,10},{10,... | collective-permute-start | bytes 393224 | tf_op jit(solution)/shard_map/ppermute | solution.py:24
  79.2 14.1 %collective-permute-start.29 = (bf16[1,128,512]{2,1,0:T(8,128)(2,1)S(1)}, bf16[1,128,512]{2,1,0:T(8,128)(2,1)S(1)}, u32[]{:S(2)}, u32[]{:S(2)}) collective-permute-start(bf16[1,128,512]{2,1,0:T(8,128)(2,1)S(1)} %get-tuple-element.111), channel_id=1, source_target_pairs={{0,2},{1,3},{2,0},{3,1},{4,6},{5,7},{6,4},{7,5},{8,10},{9,11},{10,... | collective-permute-start | bytes 393224 | tf_op jit(solution)/shard_map/ppermute | solution.py:24
  87.6 8.8 %collective-permute-start.30 = (bf16[1,128,512]{2,1,0:T(8,128)(2,1)S(1)}, bf16[1,128,512]{2,1,0:T(8,128)(2,1)S(1)}, u32[]{:S(2)}, u32[]{:S(2)}) collective-permute-start(bf16[1,128,512]{2,1,0:T(8,128)(2,1)S(1)} %get-tuple-element.109), channel_id=1, source_target_pairs={{0,3},{1,2},{2,1},{3,0},{4,7},{5,6},{6,5},{7,4},{8,11},{9,10},{10,... | collective-permute-start | bytes 393224 | tf_op jit(solution)/shard_map/ppermute | solution.py:24
  (17 other events, 64.6 us)

commit v6 on v5

--- a/solution.py
+++ b/solution.py
@@ -110,6 +110,18 @@
     return outs[:parts], outs[parts], outs[parts + 1]
 
 
+def held(array):
+    hbm = pl.BlockSpec(memory_space=pltpu.HBM)
+    return pl.pallas_call(
+        lambda *refs: None,
+        in_specs=[hbm],
+        out_specs=hbm,
+        out_shape=jax.ShapeDtypeStruct(array.shape, array.dtype),
+        input_output_aliases={0: 0},
+        name="held",
+    )(array)
+
+
 def on_device(queries, keys_in, values_in, grad_out):
     seq_count = lax.axis_size("seq")
     parts = lax.axis_size("head")
@@ -253,11 +265,14 @@
         place(2, near_last[g], 1, starts[g])
         for part in far:
             place(0, landed["mid", g, part], part, starts[g])
-            if g == groups - 1:
+            if g < groups - 1:
+                place(2, landed["last", g, part], part, starts[g])
+            else:
                 place(2, landed["last", g, part, 0], part, starts[g])
-                place(3, landed["last", g, part, 1], part, starts[g])
-            else:
-                place(2, landed["last", g, part], part, starts[g])
+    for at, part in enumerate(far):
+        if at == 1:
+            outs[3] = held(outs[3])
+        place(3, landed["last", groups - 1, part, 1], part, starts[-1])
     return tuple(outs)
 
 

time: 97.5 us -> 97.2 us (level)
  waiting for transfers between devices: 28.4 us -> 23.9 us
  local copies, waits for them, and re-layouts: 3.58 us -> 7.93 us
    ppermute x33, waiting for transfers between devices: 28.4 us -> 23.9 us  [swapped(): return lax.ppermute(block, axis, [(i, i ^ mask) for i in range(count)])]
    dynamic_update_slice x20, local copies, waits for them, and re-layouts: 0.42 us -> 2.36 us  [place(): lax.dynamic_update_slice(outs[first + which], back[which], (0, column(par...]
    slice x2, local copies, waits for them, and re-layouts: 0.04 us -> 1.39 us  [on_device(): send(block[1:], part, ('last', g, part, 1))]
    unnamed x16, local copies, waits for them, and re-layouts: 2.19 us -> 3.23 us
  transfers between devices with their start and end apart: 33 -> 33, of which waited for: 11 -> 11; matrix products, arithmetic and copies ran while one was open for 3% -> 6% of each run, Pallas kernels for 14% -> 14%
where the time goes in v6:
time: 97.2 us; the launch traced here: 97 us
  starting transfers between devices  47.5 us (49%)
  waiting for transfers between devices  23.9 us (25%)
  Pallas kernels  13.5 us (14%)
  local copies, waits for them, and re-layouts  7.93 us (8%)
  other arithmetic  3.01 us (3%)
  between operations  1.21 us (1%)
    ppermute x33, starting transfers between devices, swapped(): return lax.ppermute(block, axis, [(i, i ^ mask) for i in range(count)])  47.5 us
    ppermute x33, waiting for transfers between devices, swapped(): return lax.ppermute(block, axis, [(i, i ^ mask) for i in range(count)])  23.9 us
    pallas_call x2, Pallas kernels, attention(): pl.pallas_call(functools.partial(attention_kernel, layout, depth, pool_si...  13.5 us
    unnamed x16, local copies, waits for them, and re-layouts  3.23 us
    dynamic_update_slice x20, local copies, waits for them, and re-layouts, place(): lax.dynamic_update_slice(outs[first + which], back[which], (0, column(par...  2.36 us
  transfers between devices with their start and end apart: 33, of which 11 were waited for; matrix products, arithmetic and copies ran while one was open for 6% of the time, Pallas kernels for 14%

profile of v6, /device:TPU:1, one launch (start us, length us, event | category | flops | bytes accessed | tf_op | source)
XLA Modules:
  0.0 97.0 jit_solution(12897564966028445889)
XLA Ops:
  1.8 2.1 %collective-permute-start.4 = (bf16[2,128,512]{2,1,0:T(8,128)(2,1)S(1)}, bf16[2,128,512]{2,1,0:T(8,128)(2,1)S(1)}, u32[]{:S(2)}, u32[]{:S(2)}) collective-permute-start(bf16[2,128,512]{2,1,0:T(8,128)(2,1)S(1)} %bitcast.224), channel_id=1, source_target_pairs={{0,2},{1,3},{2,0},{3,1},{4,6},{5,7},{6,4},{7,5},{8,10},{9,11},{10,... | collective-permute-start | bytes 786440 | tf_op jit(solution)/shard_map/ppermute | solution.py:24
  7.6 1.5 %collective-permute-start.3 = (f32[2,4,1024]{2,1,0:T(4,128)S(1)}, f32[2,4,1024]{2,1,0:T(4,128)S(1)}, u32[]{:S(2)}, u32[]{:S(2)}) collective-permute-start(f32[2,4,1024]{2,1,0:T(4,128)S(1)} %get-tuple-element.143), channel_id=1, source_target_pairs={{0,3},{1,2},{2,1},{3,0},{4,7},{5,6},{6,5},{7,4},{8,11},{9,10},{10,... | collective-permute-start | bytes 98312 | tf_op jit(solution)/shard_map/ppermute | solution.py:24
  11.9 1.6 %collective-permute-start.7 = (f32[2,16,1024]{2,1,0:T(8,128)S(1)}, f32[2,16,1024]{2,1,0:T(8,128)S(1)}, u32[]{:S(2)}, u32[]{:S(2)}) collective-permute-start(f32[2,16,1024]{2,1,0:T(8,128)S(1)} %pad_maximum_fusion.9), channel_id=1, source_target_pairs={{0,4},{4,0},{8,12},{12,8},{16,20},{20,16},{24,28},{28,24},{1,5},{5... | collective-permute-start | bytes 393224 | tf_op jit(solution)/shard_map/ppermute | solution.py:24
  13.6 2.7 %collective-permute-start = (bf16[4,128,512]{2,1,0:T(8,128)(2,1)S(1)}, bf16[4,128,512]{2,1,0:T(8,128)(2,1)S(1)}, u32[]{:S(2)}, u32[]{:S(2)}) collective-permute-start(bf16[4,128,512]{2,1,0:T(8,128)(2,1)S(1)} %pad_maximum_fusion.1), channel_id=1, source_target_pairs={{0,1},{1,0},{2,3},{3,2},{4,5},{5,4},{6,7},{7,6},{8,9},{9,8},{10,11... | collective-permute-start | bytes 1572872 | tf_op jit(solution)/shard_map/ppermute | solution.py:24
  16.4 1.4 %collective-permute-start.8 = (f32[2,16,1024]{2,1,0:T(8,128)S(1)}, f32[2,16,1024]{2,1,0:T(8,128)S(1)}, u32[]{:S(2)}, u32[]{:S(2)}) collective-permute-start(f32[2,16,1024]{2,1,0:T(8,128)S(1)} %get-tuple-element.139), channel_id=1, source_target_pairs={{0,8},{4,12},{8,0},{12,4},{16,24},{20,28},{24,16},{28,20},{1,9},{5... | collective-permute-start | bytes 393224 | tf_op jit(solution)/shard_map/ppermute | solution.py:24
  17.9 2.7 %collective-permute-done.8 = f32[2,16,1024]{2,1,0:T(8,128)S(1)} collective-permute-done((f32[2,16,1024]{2,1,0:T(8,128)S(1)}, f32[2,16,1024]{2,1,0:T(8,128)S(1)}, u32[]{:S(2)}, u32[]{:S(2)}) %collective-permute-start.8) | collective-permute-done | bytes 131104 | tf_op jit(solution)/shard_map/ppermute | solution.py:24
  20.6 2.4 %collective-permute-start.10 = (bf16[2,16,1024]{2,1,0:T(8,128)(2,1)S(1)}, bf16[2,16,1024]{2,1,0:T(8,128)(2,1)S(1)}, u32[]{:S(2)}, u32[]{:S(2)}) collective-permute-start(bf16[2,16,1024]{2,1,0:T(8,128)(2,1)S(1)} %add_multiply_fusion), channel_id=1, source_target_pairs={{0,16},{4,20},{8,24},{12,28},{16,0},{20,4},{24,8},{28,12},{1,17},{... | collective-permute-start | bytes 196616 | tf_op jit(solution)/shard_map/ppermute | solution.py:24
  23.1 4.1 %collective-permute-start.12 = (bf16[4,128,512]{2,1,0:T(8,128)(2,1)S(1)}, bf16[4,128,512]{2,1,0:T(8,128)(2,1)S(1)}, u32[]{:S(2)}, u32[]{:S(2)}) collective-permute-start(bf16[4,128,512]{2,1,0:T(8,128)(2,1)S(1)} %pad_maximum_fusion.3), channel_id=1, source_target_pairs={{0,2},{1,3},{2,0},{3,1},{4,6},{5,7},{6,4},{7,5},{8,10},{9,11},{10,... | collective-permute-start | bytes 1572872 | tf_op jit(solution)/shard_map/ppermute | solution.py:24
  27.2 4.1 %collective-permute-start.13 = (bf16[4,128,512]{2,1,0:T(8,128)(2,1)S(1)}, bf16[4,128,512]{2,1,0:T(8,128)(2,1)S(1)}, u32[]{:S(2)}, u32[]{:S(2)}) collective-permute-start(bf16[4,128,512]{2,1,0:T(8,128)(2,1)S(1)} %pad_maximum_fusion.4), channel_id=1, source_target_pairs={{0,3},{1,2},{2,1},{3,0},{4,7},{5,6},{6,5},{7,4},{8,11},{9,10},{10,... | collective-permute-start | bytes 1572872 | tf_op jit(solution)/shard_map/ppermute | solution.py:24
  31.3 6.7 %attention.2 = (bf16[2,128,512]{2,1,0:T(8,128)(2,1)S(1)}, bf16[2,128,512]{2,1,0:T(8,128)(2,1)S(1)}, bf16[2,128,512]{2,1,0:T(8,128)(2,1)S(1)}, bf16[2,128,512]{2,...) custom-call(bf16[4,128,512]{2,1,0:T(8,128)(2,1)S(1)} %pad_maximum_fusion.refs_0_, ...), custom_call_target="tpu_custom_call" | custom-call | flops 1761607680 | bytes 6291456 | tf_op jit(solution)/shard_map/attention/pallas_call | solution.py:90
  38.1 2.3 %collective-permute-start.20 = (bf16[2,16,512]{2,1,0:T(8,128)(2,1)S(1)}, bf16[2,16,512]{2,1,0:T(8,128)(2,1)S(1)}, u32[]{:S(2)}, u32[]{:S(2)}) collective-permute-start(bf16[2,16,512]{2,1,0:T(8,128)(2,1)S(1)} %fusion.28), channel_id=1, source_target_pairs={{0,16},{4,20},{8,24},{12,28},{16,0},{20,4},{24,8},{28,12},{1,17},{... | collective-permute-start | bytes 98312 | tf_op jit(solution)/shard_map/ppermute | solution.py:24
  41.8 1.8 %collective-permute-start.21 = (f32[2,16,512]{2,1,0:T(8,128)S(1)}, f32[2,16,512]{2,1,0:T(8,128)S(1)}, u32[]{:S(2)}, u32[]{:S(2)}) collective-permute-start(f32[2,16,512]{2,1,0:T(8,128)S(1)} %fusion.26), channel_id=1, source_target_pairs={{0,8},{4,12},{8,0},{12,4},{16,24},{20,28},{24,16},{28,20},{1,9},{5... | collective-permute-start | bytes 196616 | tf_op jit(solution)/shard_map/ppermute | solution.py:24
  43.8 2.1 %collective-permute-done.21 = f32[2,16,512]{2,1,0:T(8,128)S(1)} collective-permute-done((f32[2,16,512]{2,1,0:T(8,128)S(1)}, f32[2,16,512]{2,1,0:T(8,128)S(1)}, u32[]{:S(2)}, u32[]{:S(2)}) %collective-permute-start.21) | collective-permute-done | bytes 65568 | tf_op jit(solution)/shard_map/ppermute | solution.py:24
  49.7 1.7 %collective-permute-start.23 = (bf16[2,128,512]{2,1,0:T(8,128)(2,1)S(1)}, bf16[2,128,512]{2,1,0:T(8,128)(2,1)S(1)}, u32[]{:S(2)}, u32[]{:S(2)}) collective-permute-start(bf16[2,128,512]{2,1,0:T(8,128)(2,1)S(1)} %get-tuple-element.76), channel_id=1, source_target_pairs={{0,1},{1,0},{2,3},{3,2},{4,5},{5,4},{6,7},{7,6},{8,9},{9,8},{10,11... | collective-permute-start | bytes 786440 | tf_op jit(solution)/shard_map/ppermute | solution.py:24
  53.6 1.4 %collective-permute-start.27 = (bf16[2,128,512]{2,1,0:T(8,128)(2,1)S(1)}, bf16[2,128,512]{2,1,0:T(8,128)(2,1)S(1)}, u32[]{:S(2)}, u32[]{:S(2)}) collective-permute-start(bf16[2,128,512]{2,1,0:T(8,128)(2,1)S(1)} %get-tuple-element.74), channel_id=1, source_target_pairs={{0,3},{1,2},{2,1},{3,0},{4,7},{5,6},{6,5},{7,4},{8,11},{9,10},{10,... | collective-permute-start | bytes 786440 | tf_op jit(solution)/shard_map/ppermute | solution.py:24
  55.0 6.7 %attention.3 = (bf16[2,128,512]{2,1,0:T(8,128)(2,1)S(1)}, bf16[2,128,512]{2,1,0:T(8,128)(2,1)S(1)}, bf16[2,128,512]{2,1,0:T(8,128)(2,1)S(1)}, bf16[2,128,512]{2,...) custom-call(bf16[4,128,512]{2,1,0:T(8,128)(2,1)S(1)} %pad_maximum_fusion.6.refs_0_, ...), custom_call_target="tpu_custom_call" | custom-call | flops 1761607680 | bytes 6291456 | tf_op jit(solution)/shard_map/attention/pallas_call | solution.py:90
  61.8 3.0 %collective-permute-start.15 = (f32[2,16,512]{2,1,0:T(8,128)S(1)}, f32[2,16,512]{2,1,0:T(8,128)S(1)}, u32[]{:S(2)}, u32[]{:S(2)}) collective-permute-start(f32[2,16,512]{2,1,0:T(8,128)S(1)} %slice_bitcast_fusion.17), channel_id=1, source_target_pairs={{0,16},{4,20},{8,24},{12,28},{16,0},{20,4},{24,8},{28,12},{1,17},{... | collective-permute-start | bytes 196616 | tf_op jit(solution)/shard_map/ppermute | solution.py:24
  65.7 1.5 %collective-permute-done.15 = f32[2,16,512]{2,1,0:T(8,128)S(1)} collective-permute-done((f32[2,16,512]{2,1,0:T(8,128)S(1)}, f32[2,16,512]{2,1,0:T(8,128)S(1)}, u32[]{:S(2)}, u32[]{:S(2)}) %collective-permute-start.15) | collective-permute-done | bytes 65568 | tf_op jit(solution)/shard_map/ppermute | solution.py:24
  67.2 2.1 %collective-permute-start.24 = (f32[2,16,512]{2,1,0:T(8,128)S(1)}, f32[2,16,512]{2,1,0:T(8,128)S(1)}, u32[]{:S(2)}, u32[]{:S(2)}) collective-permute-start(f32[2,16,512]{2,1,0:T(8,128)S(1)} %fusion.27), channel_id=1, source_target_pairs={{0,8},{4,12},{8,0},{12,4},{16,24},{20,28},{24,16},{28,20},{1,9},{5... | collective-permute-start | bytes 196616 | tf_op jit(solution)/shard_map/ppermute | solution.py:24
  69.4 2.3 %collective-permute-start.19 = (bf16[2,128,512]{2,1,0:T(8,128)(2,1)S(1)}, bf16[2,128,512]{2,1,0:T(8,128)(2,1)S(1)}, u32[]{:S(2)}, u32[]{:S(2)}) collective-permute-start(bf16[2,128,512]{2,1,0:T(8,128)(2,1)S(1)} %get-tuple-element.61), channel_id=1, source_target_pairs={{0,3},{1,2},{2,1},{3,0},{4,7},{5,6},{6,5},{7,4},{8,11},{9,10},{10,... | collective-permute-start | bytes 786440 | tf_op jit(solution)/shard_map/ppermute | solution.py:24
  73.1 3.2 %collective-permute-done.27 = bf16[2,128,512]{2,1,0:T(8,128)(2,1)S(1)} collective-permute-done((bf16[2,128,512]{2,1,0:T(8,128)(2,1)S(1)}, bf16[2,128,512]{2,1,0:T(8,128)(2,1)S(1)}, u32[]{:S(2)}, u32[]{:S(2)}) %collective-permute-start.27) | collective-permute-done | bytes 262176 | tf_op jit(solution)/shard_map/ppermute | solution.py:24
  81.3 6.3 %collective-permute-done.19 = bf16[2,128,512]{2,1,0:T(8,128)(2,1)S(1)} collective-permute-done((bf16[2,128,512]{2,1,0:T(8,128)(2,1)S(1)}, bf16[2,128,512]{2,1,0:T(8,128)(2,1)S(1)}, u32[]{:S(2)}, u32[]{:S(2)}) %collective-permute-start.19) | collective-permute-done | bytes 262176 | tf_op jit(solution)/shard_map/ppermute | solution.py:24
  89.7 3.5 %collective-permute-done.32 = bf16[1,128,512]{2,1,0:T(8,128)(2,1)S(1)} collective-permute-done((bf16[1,128,512]{2,1,0:T(8,128)(2,1)}, bf16[1,128,512]{2,1,0:T(8,128)(2,1)S(1)}, u32[]{:S(2)}, u32[]{:S(2)}) %collective-permute-start.32) | collective-permute-done | bytes 131104 | tf_op jit(solution)/shard_map/ppermute | solution.py:24
  94.6 1.8 %collective-permute-done.30 = bf16[1,128,512]{2,1,0:T(8,128)(2,1)S(1)} collective-permute-done((bf16[1,128,512]{2,1,0:T(8,128)(2,1)}, bf16[1,128,512]{2,1,0:T(8,128)(2,1)S(1)}, u32[]{:S(2)}, u32[]{:S(2)}) %collective-permute-start.30) | collective-permute-done | bytes 131104 | tf_op jit(solution)/shard_map/ppermute | solution.py:24
  (121 shorter events, 26.7 us)
Async XLA Ops:
  1.8 10.1 %collective-permute-start.4 = (bf16[2,128,512]{2,1,0:T(8,128)(2,1)S(1)}, bf16[2,128,512]{2,1,0:T(8,128)(2,1)S(1)}, u32[]{:S(2)}, u32[]{:S(2)}) collective-permute-start(bf16[2,128,512]{2,1,0:T(8,128)(2,1)S(1)} %bitcast.224), channel_id=1, source_target_pairs={{0,2},{1,3},{2,0},{3,1},{4,6},{5,7},{6,4},{7,5},{8,10},{9,11},{10,... | collective-permute-start | bytes 786440 | tf_op jit(solution)/shard_map/ppermute | solution.py:24
  9.2 11.4 %collective-permute-start.9 = (bf16[4,128,512]{2,1,0:T(8,128)(2,1)S(1)}, bf16[4,128,512]{2,1,0:T(8,128)(2,1)S(1)}, u32[]{:S(2)}, u32[]{:S(2)}) collective-permute-start(bf16[4,128,512]{2,1,0:T(8,128)(2,1)S(1)} %pad_maximum_fusion.5), channel_id=1, source_target_pairs={{0,1},{1,0},{2,3},{3,2},{4,5},{5,4},{6,7},{7,6},{8,9},{9,8},{10,11... | collective-permute-start | bytes 1572872 | tf_op jit(solution)/shard_map/ppermute | solution.py:24
  9.5 21.8 %collective-permute-start.6 = (bf16[4,128,512]{2,1,0:T(8,128)(2,1)S(1)}, bf16[4,128,512]{2,1,0:T(8,128)(2,1)S(1)}, u32[]{:S(2)}, u32[]{:S(2)}) collective-permute-start(bf16[4,128,512]{2,1,0:T(8,128)(2,1)S(1)} %pad_maximum_fusion.2), channel_id=1, source_target_pairs={{0,3},{1,2},{2,1},{3,0},{4,7},{5,6},{6,5},{7,4},{8,11},{9,10},{10,... | collective-permute-start | bytes 1572872 | tf_op jit(solution)/shard_map/ppermute | solution.py:24
  10.9 20.4 %collective-permute-start.5 = (bf16[2,128,512]{2,1,0:T(8,128)(2,1)S(1)}, bf16[2,128,512]{2,1,0:T(8,128)(2,1)S(1)}, u32[]{:S(2)}, u32[]{:S(2)}) collective-permute-start(bf16[2,128,512]{2,1,0:T(8,128)(2,1)S(1)} %pad_maximum_fusion.7), channel_id=1, source_target_pairs={{0,2},{1,3},{2,0},{3,1},{4,6},{5,7},{6,4},{7,5},{8,10},{9,11},{10,... | collective-permute-start | bytes 786440 | tf_op jit(solution)/shard_map/ppermute | solution.py:24
  11.9 4.4 %collective-permute-start.7 = (f32[2,16,1024]{2,1,0:T(8,128)S(1)}, f32[2,16,1024]{2,1,0:T(8,128)S(1)}, u32[]{:S(2)}, u32[]{:S(2)}) collective-permute-start(f32[2,16,1024]{2,1,0:T(8,128)S(1)} %pad_maximum_fusion.9), channel_id=1, source_target_pairs={{0,4},{4,0},{8,12},{12,8},{16,20},{20,16},{24,28},{28,24},{1,5},{5... | collective-permute-start | bytes 393224 | tf_op jit(solution)/shard_map/ppermute | solution.py:24
  13.6 17.8 %collective-permute-start = (bf16[4,128,512]{2,1,0:T(8,128)(2,1)S(1)}, bf16[4,128,512]{2,1,0:T(8,128)(2,1)S(1)}, u32[]{:S(2)}, u32[]{:S(2)}) collective-permute-start(bf16[4,128,512]{2,1,0:T(8,128)(2,1)S(1)} %pad_maximum_fusion.1), channel_id=1, source_target_pairs={{0,1},{1,0},{2,3},{3,2},{4,5},{5,4},{6,7},{7,6},{8,9},{9,8},{10,11... | collective-permute-start | bytes 1572872 | tf_op jit(solution)/shard_map/ppermute | solution.py:24
  20.6 6.5 %collective-permute-start.10 = (bf16[2,16,1024]{2,1,0:T(8,128)(2,1)S(1)}, bf16[2,16,1024]{2,1,0:T(8,128)(2,1)S(1)}, u32[]{:S(2)}, u32[]{:S(2)}) collective-permute-start(bf16[2,16,1024]{2,1,0:T(8,128)(2,1)S(1)} %add_multiply_fusion), channel_id=1, source_target_pairs={{0,16},{4,20},{8,24},{12,28},{16,0},{20,4},{24,8},{28,12},{1,17},{... | collective-permute-start | bytes 196616 | tf_op jit(solution)/shard_map/ppermute | solution.py:24
  23.1 30.5 %collective-permute-start.12 = (bf16[4,128,512]{2,1,0:T(8,128)(2,1)S(1)}, bf16[4,128,512]{2,1,0:T(8,128)(2,1)S(1)}, u32[]{:S(2)}, u32[]{:S(2)}) collective-permute-start(bf16[4,128,512]{2,1,0:T(8,128)(2,1)S(1)} %pad_maximum_fusion.3), channel_id=1, source_target_pairs={{0,2},{1,3},{2,0},{3,1},{4,6},{5,7},{6,4},{7,5},{8,10},{9,11},{10,... | collective-permute-start | bytes 1572872 | tf_op jit(solution)/shard_map/ppermute | solution.py:24
  27.2 27.8 %collective-permute-start.13 = (bf16[4,128,512]{2,1,0:T(8,128)(2,1)S(1)}, bf16[4,128,512]{2,1,0:T(8,128)(2,1)S(1)}, u32[]{:S(2)}, u32[]{:S(2)}) collective-permute-start(bf16[4,128,512]{2,1,0:T(8,128)(2,1)S(1)} %pad_maximum_fusion.4), channel_id=1, source_target_pairs={{0,3},{1,2},{2,1},{3,0},{4,7},{5,6},{6,5},{7,4},{8,11},{9,10},{10,... | collective-permute-start | bytes 1572872 | tf_op jit(solution)/shard_map/ppermute | solution.py:24
  40.4 21.3 %collective-permute-start.14 = (bf16[2,128,512]{2,1,0:T(8,128)(2,1)S(1)}, bf16[2,128,512]{2,1,0:T(8,128)(2,1)S(1)}, u32[]{:S(2)}, u32[]{:S(2)}) collective-permute-start(bf16[2,128,512]{2,1,0:T(8,128)(2,1)S(1)} %get-tuple-element.53), channel_id=1, source_target_pairs={{0,2},{1,3},{2,0},{3,1},{4,6},{5,7},{6,4},{7,5},{8,10},{9,11},{10,... | collective-permute-start | bytes 786440 | tf_op jit(solution)/shard_map/ppermute | solution.py:24
  51.7 13.1 %collective-permute-start.16 = (bf16[2,128,512]{2,1,0:T(8,128)(2,1)S(1)}, bf16[2,128,512]{2,1,0:T(8,128)(2,1)S(1)}, u32[]{:S(2)}, u32[]{:S(2)}) collective-permute-start(bf16[2,128,512]{2,1,0:T(8,128)(2,1)S(1)} %get-tuple-element.56), channel_id=1, source_target_pairs={{0,3},{1,2},{2,1},{3,0},{4,7},{5,6},{6,5},{7,4},{8,11},{9,10},{10,... | collective-permute-start | bytes 786440 | tf_op jit(solution)/shard_map/ppermute | solution.py:24
  52.7 16.7 %collective-permute-start.25 = (bf16[2,128,512]{2,1,0:T(8,128)(2,1)S(1)}, bf16[2,128,512]{2,1,0:T(8,128)(2,1)S(1)}, u32[]{:S(2)}, u32[]{:S(2)}) collective-permute-start(bf16[2,128,512]{2,1,0:T(8,128)(2,1)S(1)} %get-tuple-element.75), channel_id=1, source_target_pairs={{0,2},{1,3},{2,0},{3,1},{4,6},{5,7},{6,4},{7,5},{8,10},{9,11},{10,... | collective-permute-start | bytes 786440 | tf_op jit(solution)/shard_map/ppermute | solution.py:24
  53.6 22.7 %collective-permute-start.27 = (bf16[2,128,512]{2,1,0:T(8,128)(2,1)S(1)}, bf16[2,128,512]{2,1,0:T(8,128)(2,1)S(1)}, u32[]{:S(2)}, u32[]{:S(2)}) collective-permute-start(bf16[2,128,512]{2,1,0:T(8,128)(2,1)S(1)} %get-tuple-element.74), channel_id=1, source_target_pairs={{0,3},{1,2},{2,1},{3,0},{4,7},{5,6},{6,5},{7,4},{8,11},{9,10},{10,... | collective-permute-start | bytes 786440 | tf_op jit(solution)/shard_map/ppermute | solution.py:24
  61.8 5.5 %collective-permute-start.15 = (f32[2,16,512]{2,1,0:T(8,128)S(1)}, f32[2,16,512]{2,1,0:T(8,128)S(1)}, u32[]{:S(2)}, u32[]{:S(2)}) collective-permute-start(f32[2,16,512]{2,1,0:T(8,128)S(1)} %slice_bitcast_fusion.17), channel_id=1, source_target_pairs={{0,16},{4,20},{8,24},{12,28},{16,0},{20,4},{24,8},{28,12},{1,17},{... | collective-permute-start | bytes 196616 | tf_op jit(solution)/shard_map/ppermute | solution.py:24
  64.7 14.5 %collective-permute-start.17 = (bf16[2,128,512]{2,1,0:T(8,128)(2,1)S(1)}, bf16[2,128,512]{2,1,0:T(8,128)(2,1)S(1)}, u32[]{:S(2)}, u32[]{:S(2)}) collective-permute-start(bf16[2,128,512]{2,1,0:T(8,128)(2,1)S(1)} %get-tuple-element.59), channel_id=1, source_target_pairs={{0,1},{1,0},{2,3},{3,2},{4,5},{5,4},{6,7},{7,6},{8,9},{9,8},{10,11... | collective-permute-start | bytes 786440 | tf_op jit(solution)/shard_map/ppermute | solution.py:24
  64.8 15.6 %collective-permute-start.18 = (bf16[2,128,512]{2,1,0:T(8,128)(2,1)S(1)}, bf16[2,128,512]{2,1,0:T(8,128)(2,1)S(1)}, u32[]{:S(2)}, u32[]{:S(2)}) collective-permute-start(bf16[2,128,512]{2,1,0:T(8,128)(2,1)S(1)} %get-tuple-element.60), channel_id=1, source_target_pairs={{0,2},{1,3},{2,0},{3,1},{4,6},{5,7},{6,4},{7,5},{8,10},{9,11},{10,... | collective-permute-start | bytes 786440 | tf_op jit(solution)/shard_map/ppermute | solution.py:24
  67.2 4.4 %collective-permute-start.24 = (f32[2,16,512]{2,1,0:T(8,128)S(1)}, f32[2,16,512]{2,1,0:T(8,128)S(1)}, u32[]{:S(2)}, u32[]{:S(2)}) collective-permute-start(f32[2,16,512]{2,1,0:T(8,128)S(1)} %fusion.27), channel_id=1, source_target_pairs={{0,8},{4,12},{8,0},{12,4},{16,24},{20,28},{24,16},{28,20},{1,9},{5... | collective-permute-start | bytes 196616 | tf_op jit(solution)/shard_map/ppermute | solution.py:24
  69.4 18.2 %collective-permute-start.19 = (bf16[2,128,512]{2,1,0:T(8,128)(2,1)S(1)}, bf16[2,128,512]{2,1,0:T(8,128)(2,1)S(1)}, u32[]{:S(2)}, u32[]{:S(2)}) collective-permute-start(bf16[2,128,512]{2,1,0:T(8,128)(2,1)S(1)} %get-tuple-element.61), channel_id=1, source_target_pairs={{0,3},{1,2},{2,1},{3,0},{4,7},{5,6},{6,5},{7,4},{8,11},{9,10},{10,... | collective-permute-start | bytes 786440 | tf_op jit(solution)/shard_map/ppermute | solution.py:24
  71.7 4.6 %collective-permute-start.26 = (f32[2,16,512]{2,1,0:T(8,128)S(1)}, f32[2,16,512]{2,1,0:T(8,128)S(1)}, u32[]{:S(2)}, u32[]{:S(2)}) collective-permute-start(f32[2,16,512]{2,1,0:T(8,128)S(1)} %bitcast_add_fusion.8), channel_id=1, source_target_pairs={{0,4},{4,0},{8,12},{12,8},{16,20},{20,16},{24,28},{28,24},{1,5},{5... | collective-permute-start | bytes 196616 | tf_op jit(solution)/shard_map/ppermute | solution.py:24
  76.7 11.0 %collective-permute-start.28 = (bf16[2,128,512]{2,1,0:T(8,128)(2,1)S(1)}, bf16[2,128,512]{2,1,0:T(8,128)(2,1)S(1)}, u32[]{:S(2)}, u32[]{:S(2)}) collective-permute-start(bf16[2,128,512]{2,1,0:T(8,128)(2,1)S(1)} %get-tuple-element.72), channel_id=1, source_target_pairs={{0,1},{1,0},{2,3},{3,2},{4,5},{5,4},{6,7},{7,6},{8,9},{9,8},{10,11... | collective-permute-start | bytes 786440 | tf_op jit(solution)/shard_map/ppermute | solution.py:24
  77.8 9.9 %collective-permute-start.31 = (bf16[1,128,512]{2,1,0:T(8,128)(2,1)S(1)}, bf16[1,128,512]{2,1,0:T(8,128)(2,1)S(1)}, u32[]{:S(2)}, u32[]{:S(2)}) collective-permute-start(bf16[1,128,512]{2,1,0:T(8,128)(2,1)S(1)} %get-tuple-element.110), channel_id=1, source_target_pairs={{0,2},{1,3},{2,0},{3,1},{4,6},{5,7},{6,4},{7,5},{8,10},{9,11},{10,... | collective-permute-start | bytes 393224 | tf_op jit(solution)/shard_map/ppermute | solution.py:24
  79.3 13.9 %collective-permute-start.32 = (bf16[1,128,512]{2,1,0:T(8,128)(2,1)}, bf16[1,128,512]{2,1,0:T(8,128)(2,1)S(1)}, u32[]{:S(2)}, u32[]{:S(2)}) collective-permute-start(bf16[1,128,512]{2,1,0:T(8,128)(2,1)} %get-tuple-element.108), channel_id=1, source_target_pairs={{0,3},{1,2},{2,1},{3,0},{4,7},{5,6},{6,5},{7,4},{8,11},{9,10},{10,... | collective-permute-start | bytes 393224 | tf_op jit(solution)/shard_map/ppermute | solution.py:24
  80.5 13.4 %collective-permute-start.29 = (bf16[1,128,512]{2,1,0:T(8,128)(2,1)}, bf16[1,128,512]{2,1,0:T(8,128)(2,1)S(1)}, u32[]{:S(2)}, u32[]{:S(2)}) collective-permute-start(bf16[1,128,512]{2,1,0:T(8,128)(2,1)} %get-tuple-element.111), channel_id=1, source_target_pairs={{0,2},{1,3},{2,0},{3,1},{4,6},{5,7},{6,4},{7,5},{8,10},{9,11},{10,... | collective-permute-start | bytes 393224 | tf_op jit(solution)/shard_map/ppermute | solution.py:24
  87.6 8.8 %collective-permute-start.30 = (bf16[1,128,512]{2,1,0:T(8,128)(2,1)}, bf16[1,128,512]{2,1,0:T(8,128)(2,1)S(1)}, u32[]{:S(2)}, u32[]{:S(2)}) collective-permute-start(bf16[1,128,512]{2,1,0:T(8,128)(2,1)} %get-tuple-element.109), channel_id=1, source_target_pairs={{0,3},{1,2},{2,1},{3,0},{4,7},{5,6},{6,5},{7,4},{8,11},{9,10},{10,... | collective-permute-start | bytes 393224 | tf_op jit(solution)/shard_map/ppermute | solution.py:24
  (17 other events, 63.7 us)

commit v7 on v6

--- a/solution.py
+++ b/solution.py
@@ -269,7 +269,7 @@
                 place(2, landed["last", g, part], part, starts[g])
             else:
                 place(2, landed["last", g, part, 0], part, starts[g])
-    for at, part in enumerate(far):
+    for at, part in enumerate(reversed(far)):
         if at == 1:
             outs[3] = held(outs[3])
         place(3, landed["last", groups - 1, part, 1], part, starts[-1])

time: 97.2 us -> 97.2 us (level)
  waiting for transfers between devices: 23.9 us -> 25.2 us
  local copies, waits for them, and re-layouts: 7.93 us -> 6.9 us
    ppermute x33, waiting for transfers between devices: 23.9 us -> 25.2 us  [swapped(): return lax.ppermute(block, axis, [(i, i ^ mask) for i in range(count)])]
    unnamed x16, local copies, waits for them, and re-layouts: 3.23 us -> 2.21 us
where the time goes in v7:
time: 97.2 us; the launch traced here: 97 us
  starting transfers between devices  47.3 us (49%)
  waiting for transfers between devices  25.2 us (26%)
  Pallas kernels  13.5 us (14%)
  local copies, waits for them, and re-layouts  6.9 us (7%)
  other arithmetic  3.01 us (3%)
  between operations  1.2 us (1%)
    ppermute x33, starting transfers between devices, swapped(): return lax.ppermute(block, axis, [(i, i ^ mask) for i in range(count)])  47.3 us
    ppermute x33, waiting for transfers between devices, swapped(): return lax.ppermute(block, axis, [(i, i ^ mask) for i in range(count)])  25.2 us
    pallas_call x2, Pallas kernels, attention(): pl.pallas_call(functools.partial(attention_kernel, layout, depth, pool_si...  13.5 us
    dynamic_update_slice x20, local copies, waits for them, and re-layouts, place(): lax.dynamic_update_slice(outs[first + which], back[which], (0, column(par...  2.36 us
    unnamed x16, local copies, waits for them, and re-layouts  2.21 us
  transfers between devices with their start and end apart: 33, of which 11 were waited for; matrix products, arithmetic and copies ran while one was open for 6% of the time, Pallas kernels for 14%

profile of v7, /device:TPU:1, one launch (start us, length us, event | category | flops | bytes accessed | tf_op | source)
XLA Modules:
  0.0 97.0 jit_solution(745567608154958429)
XLA Ops:
  1.8 2.1 %collective-permute-start.4 = (bf16[2,128,512]{2,1,0:T(8,128)(2,1)S(1)}, bf16[2,128,512]{2,1,0:T(8,128)(2,1)S(1)}, u32[]{:S(2)}, u32[]{:S(2)}) collective-permute-start(bf16[2,128,512]{2,1,0:T(8,128)(2,1)S(1)} %bitcast.224), channel_id=1, source_target_pairs={{0,2},{1,3},{2,0},{3,1},{4,6},{5,7},{6,4},{7,5},{8,10},{9,11},{10,... | collective-permute-start | bytes 786440 | tf_op jit(solution)/shard_map/ppermute | solution.py:24
  7.6 1.5 %collective-permute-start.3 = (f32[2,4,1024]{2,1,0:T(4,128)S(1)}, f32[2,4,1024]{2,1,0:T(4,128)S(1)}, u32[]{:S(2)}, u32[]{:S(2)}) collective-permute-start(f32[2,4,1024]{2,1,0:T(4,128)S(1)} %get-tuple-element.143), channel_id=1, source_target_pairs={{0,3},{1,2},{2,1},{3,0},{4,7},{5,6},{6,5},{7,4},{8,11},{9,10},{10,... | collective-permute-start | bytes 98312 | tf_op jit(solution)/shard_map/ppermute | solution.py:24
  11.9 1.6 %collective-permute-start.7 = (f32[2,16,1024]{2,1,0:T(8,128)S(1)}, f32[2,16,1024]{2,1,0:T(8,128)S(1)}, u32[]{:S(2)}, u32[]{:S(2)}) collective-permute-start(f32[2,16,1024]{2,1,0:T(8,128)S(1)} %pad_maximum_fusion.9), channel_id=1, source_target_pairs={{0,4},{4,0},{8,12},{12,8},{16,20},{20,16},{24,28},{28,24},{1,5},{5... | collective-permute-start | bytes 393224 | tf_op jit(solution)/shard_map/ppermute | solution.py:24
  13.6 2.7 %collective-permute-start = (bf16[4,128,512]{2,1,0:T(8,128)(2,1)S(1)}, bf16[4,128,512]{2,1,0:T(8,128)(2,1)S(1)}, u32[]{:S(2)}, u32[]{:S(2)}) collective-permute-start(bf16[4,128,512]{2,1,0:T(8,128)(2,1)S(1)} %pad_maximum_fusion.1), channel_id=1, source_target_pairs={{0,1},{1,0},{2,3},{3,2},{4,5},{5,4},{6,7},{7,6},{8,9},{9,8},{10,11... | collective-permute-start | bytes 1572872 | tf_op jit(solution)/shard_map/ppermute | solution.py:24
  16.4 1.4 %collective-permute-start.8 = (f32[2,16,1024]{2,1,0:T(8,128)S(1)}, f32[2,16,1024]{2,1,0:T(8,128)S(1)}, u32[]{:S(2)}, u32[]{:S(2)}) collective-permute-start(f32[2,16,1024]{2,1,0:T(8,128)S(1)} %get-tuple-element.139), channel_id=1, source_target_pairs={{0,8},{4,12},{8,0},{12,4},{16,24},{20,28},{24,16},{28,20},{1,9},{5... | collective-permute-start | bytes 393224 | tf_op jit(solution)/shard_map/ppermute | solution.py:24
  17.9 2.7 %collective-permute-done.8 = f32[2,16,1024]{2,1,0:T(8,128)S(1)} collective-permute-done((f32[2,16,1024]{2,1,0:T(8,128)S(1)}, f32[2,16,1024]{2,1,0:T(8,128)S(1)}, u32[]{:S(2)}, u32[]{:S(2)}) %collective-permute-start.8) | collective-permute-done | bytes 131104 | tf_op jit(solution)/shard_map/ppermute | solution.py:24
  20.6 2.4 %collective-permute-start.10 = (bf16[2,16,1024]{2,1,0:T(8,128)(2,1)S(1)}, bf16[2,16,1024]{2,1,0:T(8,128)(2,1)S(1)}, u32[]{:S(2)}, u32[]{:S(2)}) collective-permute-start(bf16[2,16,1024]{2,1,0:T(8,128)(2,1)S(1)} %add_multiply_fusion), channel_id=1, source_target_pairs={{0,16},{4,20},{8,24},{12,28},{16,0},{20,4},{24,8},{28,12},{1,17},{... | collective-permute-start | bytes 196616 | tf_op jit(solution)/shard_map/ppermute | solution.py:24
  23.1 4.1 %collective-permute-start.12 = (bf16[4,128,512]{2,1,0:T(8,128)(2,1)S(1)}, bf16[4,128,512]{2,1,0:T(8,128)(2,1)S(1)}, u32[]{:S(2)}, u32[]{:S(2)}) collective-permute-start(bf16[4,128,512]{2,1,0:T(8,128)(2,1)S(1)} %pad_maximum_fusion.3), channel_id=1, source_target_pairs={{0,2},{1,3},{2,0},{3,1},{4,6},{5,7},{6,4},{7,5},{8,10},{9,11},{10,... | collective-permute-start | bytes 1572872 | tf_op jit(solution)/shard_map/ppermute | solution.py:24
  27.2 4.1 %collective-permute-start.13 = (bf16[4,128,512]{2,1,0:T(8,128)(2,1)S(1)}, bf16[4,128,512]{2,1,0:T(8,128)(2,1)S(1)}, u32[]{:S(2)}, u32[]{:S(2)}) collective-permute-start(bf16[4,128,512]{2,1,0:T(8,128)(2,1)S(1)} %pad_maximum_fusion.4), channel_id=1, source_target_pairs={{0,3},{1,2},{2,1},{3,0},{4,7},{5,6},{6,5},{7,4},{8,11},{9,10},{10,... | collective-permute-start | bytes 1572872 | tf_op jit(solution)/shard_map/ppermute | solution.py:24
  31.3 6.7 %attention.2 = (bf16[2,128,512]{2,1,0:T(8,128)(2,1)S(1)}, bf16[2,128,512]{2,1,0:T(8,128)(2,1)S(1)}, bf16[2,128,512]{2,1,0:T(8,128)(2,1)S(1)}, bf16[2,128,512]{2,...) custom-call(bf16[4,128,512]{2,1,0:T(8,128)(2,1)S(1)} %pad_maximum_fusion.refs_0_, ...), custom_call_target="tpu_custom_call" | custom-call | flops 1761607680 | bytes 6291456 | tf_op jit(solution)/shard_map/attention/pallas_call | solution.py:90
  38.1 2.3 %collective-permute-start.20 = (bf16[2,16,512]{2,1,0:T(8,128)(2,1)S(1)}, bf16[2,16,512]{2,1,0:T(8,128)(2,1)S(1)}, u32[]{:S(2)}, u32[]{:S(2)}) collective-permute-start(bf16[2,16,512]{2,1,0:T(8,128)(2,1)S(1)} %fusion.28), channel_id=1, source_target_pairs={{0,16},{4,20},{8,24},{12,28},{16,0},{20,4},{24,8},{28,12},{1,17},{... | collective-permute-start | bytes 98312 | tf_op jit(solution)/shard_map/ppermute | solution.py:24
  41.8 1.8 %collective-permute-start.21 = (f32[2,16,512]{2,1,0:T(8,128)S(1)}, f32[2,16,512]{2,1,0:T(8,128)S(1)}, u32[]{:S(2)}, u32[]{:S(2)}) collective-permute-start(f32[2,16,512]{2,1,0:T(8,128)S(1)} %fusion.26), channel_id=1, source_target_pairs={{0,8},{4,12},{8,0},{12,4},{16,24},{20,28},{24,16},{28,20},{1,9},{5... | collective-permute-start | bytes 196616 | tf_op jit(solution)/shard_map/ppermute | solution.py:24
  43.8 2.1 %collective-permute-done.21 = f32[2,16,512]{2,1,0:T(8,128)S(1)} collective-permute-done((f32[2,16,512]{2,1,0:T(8,128)S(1)}, f32[2,16,512]{2,1,0:T(8,128)S(1)}, u32[]{:S(2)}, u32[]{:S(2)}) %collective-permute-start.21) | collective-permute-done | bytes 65568 | tf_op jit(solution)/shard_map/ppermute | solution.py:24
  49.7 1.7 %collective-permute-start.23 = (bf16[2,128,512]{2,1,0:T(8,128)(2,1)S(1)}, bf16[2,128,512]{2,1,0:T(8,128)(2,1)S(1)}, u32[]{:S(2)}, u32[]{:S(2)}) collective-permute-start(bf16[2,128,512]{2,1,0:T(8,128)(2,1)S(1)} %get-tuple-element.76), channel_id=1, source_target_pairs={{0,1},{1,0},{2,3},{3,2},{4,5},{5,4},{6,7},{7,6},{8,9},{9,8},{10,11... | collective-permute-start | bytes 786440 | tf_op jit(solution)/shard_map/ppermute | solution.py:24
  53.6 1.4 %collective-permute-start.27 = (bf16[2,128,512]{2,1,0:T(8,128)(2,1)S(1)}, bf16[2,128,512]{2,1,0:T(8,128)(2,1)S(1)}, u32[]{:S(2)}, u32[]{:S(2)}) collective-permute-start(bf16[2,128,512]{2,1,0:T(8,128)(2,1)S(1)} %get-tuple-element.74), channel_id=1, source_target_pairs={{0,3},{1,2},{2,1},{3,0},{4,7},{5,6},{6,5},{7,4},{8,11},{9,10},{10,... | collective-permute-start | bytes 786440 | tf_op jit(solution)/shard_map/ppermute | solution.py:24
  55.0 6.7 %attention.3 = (bf16[2,128,512]{2,1,0:T(8,128)(2,1)S(1)}, bf16[2,128,512]{2,1,0:T(8,128)(2,1)S(1)}, bf16[2,128,512]{2,1,0:T(8,128)(2,1)S(1)}, bf16[2,128,512]{2,...) custom-call(bf16[4,128,512]{2,1,0:T(8,128)(2,1)S(1)} %pad_maximum_fusion.6.refs_0_, ...), custom_call_target="tpu_custom_call" | custom-call | flops 1761607680 | bytes 6291456 | tf_op jit(solution)/shard_map/attention/pallas_call | solution.py:90
  61.8 3.0 %collective-permute-start.15 = (f32[2,16,512]{2,1,0:T(8,128)S(1)}, f32[2,16,512]{2,1,0:T(8,128)S(1)}, u32[]{:S(2)}, u32[]{:S(2)}) collective-permute-start(f32[2,16,512]{2,1,0:T(8,128)S(1)} %slice_bitcast_fusion.17), channel_id=1, source_target_pairs={{0,16},{4,20},{8,24},{12,28},{16,0},{20,4},{24,8},{28,12},{1,17},{... | collective-permute-start | bytes 196616 | tf_op jit(solution)/shard_map/ppermute | solution.py:24
  65.7 1.5 %collective-permute-done.15 = f32[2,16,512]{2,1,0:T(8,128)S(1)} collective-permute-done((f32[2,16,512]{2,1,0:T(8,128)S(1)}, f32[2,16,512]{2,1,0:T(8,128)S(1)}, u32[]{:S(2)}, u32[]{:S(2)}) %collective-permute-start.15) | collective-permute-done | bytes 65568 | tf_op jit(solution)/shard_map/ppermute | solution.py:24
  67.2 2.1 %collective-permute-start.24 = (f32[2,16,512]{2,1,0:T(8,128)S(1)}, f32[2,16,512]{2,1,0:T(8,128)S(1)}, u32[]{:S(2)}, u32[]{:S(2)}) collective-permute-start(f32[2,16,512]{2,1,0:T(8,128)S(1)} %fusion.27), channel_id=1, source_target_pairs={{0,8},{4,12},{8,0},{12,4},{16,24},{20,28},{24,16},{28,20},{1,9},{5... | collective-permute-start | bytes 196616 | tf_op jit(solution)/shard_map/ppermute | solution.py:24
  69.4 2.3 %collective-permute-start.19 = (bf16[2,128,512]{2,1,0:T(8,128)(2,1)S(1)}, bf16[2,128,512]{2,1,0:T(8,128)(2,1)S(1)}, u32[]{:S(2)}, u32[]{:S(2)}) collective-permute-start(bf16[2,128,512]{2,1,0:T(8,128)(2,1)S(1)} %get-tuple-element.61), channel_id=1, source_target_pairs={{0,3},{1,2},{2,1},{3,0},{4,7},{5,6},{6,5},{7,4},{8,11},{9,10},{10,... | collective-permute-start | bytes 786440 | tf_op jit(solution)/shard_map/ppermute | solution.py:24
  73.1 3.2 %collective-permute-done.27 = bf16[2,128,512]{2,1,0:T(8,128)(2,1)S(1)} collective-permute-done((bf16[2,128,512]{2,1,0:T(8,128)(2,1)S(1)}, bf16[2,128,512]{2,1,0:T(8,128)(2,1)S(1)}, u32[]{:S(2)}, u32[]{:S(2)}) %collective-permute-start.27) | collective-permute-done | bytes 262176 | tf_op jit(solution)/shard_map/ppermute | solution.py:24
  81.0 6.3 %collective-permute-done.19 = bf16[2,128,512]{2,1,0:T(8,128)(2,1)S(1)} collective-permute-done((bf16[2,128,512]{2,1,0:T(8,128)(2,1)S(1)}, bf16[2,128,512]{2,1,0:T(8,128)(2,1)S(1)}, u32[]{:S(2)}, u32[]{:S(2)}) %collective-permute-start.19) | collective-permute-done | bytes 262176 | tf_op jit(solution)/shard_map/ppermute | solution.py:24
  87.4 2.7 %collective-permute-done.31 = bf16[1,128,512]{2,1,0:T(8,128)(2,1)S(1)} collective-permute-done((bf16[1,128,512]{2,1,0:T(8,128)(2,1)S(1)}, bf16[1,128,512]{2,1,0:T(8,128)(2,1)S(1)}, u32[]{:S(2)}, u32[]{:S(2)}) %collective-permute-start.31) | collective-permute-done | bytes 131104 | tf_op jit(solution)/shard_map/ppermute | solution.py:24
  92.4 3.9 %collective-permute-done.30 = bf16[1,128,512]{2,1,0:T(8,128)(2,1)S(1)} collective-permute-done((bf16[1,128,512]{2,1,0:T(8,128)(2,1)}, bf16[1,128,512]{2,1,0:T(8,128)(2,1)S(1)}, u32[]{:S(2)}, u32[]{:S(2)}) %collective-permute-start.30) | collective-permute-done | bytes 131104 | tf_op jit(solution)/shard_map/ppermute | solution.py:24
  (121 shorter events, 25.4 us)
Async XLA Ops:
  1.8 10.1 %collective-permute-start.4 = (bf16[2,128,512]{2,1,0:T(8,128)(2,1)S(1)}, bf16[2,128,512]{2,1,0:T(8,128)(2,1)S(1)}, u32[]{:S(2)}, u32[]{:S(2)}) collective-permute-start(bf16[2,128,512]{2,1,0:T(8,128)(2,1)S(1)} %bitcast.224), channel_id=1, source_target_pairs={{0,2},{1,3},{2,0},{3,1},{4,6},{5,7},{6,4},{7,5},{8,10},{9,11},{10,... | collective-permute-start | bytes 786440 | tf_op jit(solution)/shard_map/ppermute | solution.py:24
  9.2 11.4 %collective-permute-start.9 = (bf16[4,128,512]{2,1,0:T(8,128)(2,1)S(1)}, bf16[4,128,512]{2,1,0:T(8,128)(2,1)S(1)}, u32[]{:S(2)}, u32[]{:S(2)}) collective-permute-start(bf16[4,128,512]{2,1,0:T(8,128)(2,1)S(1)} %pad_maximum_fusion.5), channel_id=1, source_target_pairs={{0,1},{1,0},{2,3},{3,2},{4,5},{5,4},{6,7},{7,6},{8,9},{9,8},{10,11... | collective-permute-start | bytes 1572872 | tf_op jit(solution)/shard_map/ppermute | solution.py:24
  9.5 21.8 %collective-permute-start.6 = (bf16[4,128,512]{2,1,0:T(8,128)(2,1)S(1)}, bf16[4,128,512]{2,1,0:T(8,128)(2,1)S(1)}, u32[]{:S(2)}, u32[]{:S(2)}) collective-permute-start(bf16[4,128,512]{2,1,0:T(8,128)(2,1)S(1)} %pad_maximum_fusion.2), channel_id=1, source_target_pairs={{0,3},{1,2},{2,1},{3,0},{4,7},{5,6},{6,5},{7,4},{8,11},{9,10},{10,... | collective-permute-start | bytes 1572872 | tf_op jit(solution)/shard_map/ppermute | solution.py:24
  10.9 20.4 %collective-permute-start.5 = (bf16[2,128,512]{2,1,0:T(8,128)(2,1)S(1)}, bf16[2,128,512]{2,1,0:T(8,128)(2,1)S(1)}, u32[]{:S(2)}, u32[]{:S(2)}) collective-permute-start(bf16[2,128,512]{2,1,0:T(8,128)(2,1)S(1)} %pad_maximum_fusion.7), channel_id=1, source_target_pairs={{0,2},{1,3},{2,0},{3,1},{4,6},{5,7},{6,4},{7,5},{8,10},{9,11},{10,... | collective-permute-start | bytes 786440 | tf_op jit(solution)/shard_map/ppermute | solution.py:24
  11.9 4.4 %collective-permute-start.7 = (f32[2,16,1024]{2,1,0:T(8,128)S(1)}, f32[2,16,1024]{2,1,0:T(8,128)S(1)}, u32[]{:S(2)}, u32[]{:S(2)}) collective-permute-start(f32[2,16,1024]{2,1,0:T(8,128)S(1)} %pad_maximum_fusion.9), channel_id=1, source_target_pairs={{0,4},{4,0},{8,12},{12,8},{16,20},{20,16},{24,28},{28,24},{1,5},{5... | collective-permute-start | bytes 393224 | tf_op jit(solution)/shard_map/ppermute | solution.py:24
  13.6 17.8 %collective-permute-start = (bf16[4,128,512]{2,1,0:T(8,128)(2,1)S(1)}, bf16[4,128,512]{2,1,0:T(8,128)(2,1)S(1)}, u32[]{:S(2)}, u32[]{:S(2)}) collective-permute-start(bf16[4,128,512]{2,1,0:T(8,128)(2,1)S(1)} %pad_maximum_fusion.1), channel_id=1, source_target_pairs={{0,1},{1,0},{2,3},{3,2},{4,5},{5,4},{6,7},{7,6},{8,9},{9,8},{10,11... | collective-permute-start | bytes 1572872 | tf_op jit(solution)/shard_map/ppermute | solution.py:24
  20.6 6.5 %collective-permute-start.10 = (bf16[2,16,1024]{2,1,0:T(8,128)(2,1)S(1)}, bf16[2,16,1024]{2,1,0:T(8,128)(2,1)S(1)}, u32[]{:S(2)}, u32[]{:S(2)}) collective-permute-start(bf16[2,16,1024]{2,1,0:T(8,128)(2,1)S(1)} %add_multiply_fusion), channel_id=1, source_target_pairs={{0,16},{4,20},{8,24},{12,28},{16,0},{20,4},{24,8},{28,12},{1,17},{... | collective-permute-start | bytes 196616 | tf_op jit(solution)/shard_map/ppermute | solution.py:24
  23.1 30.5 %collective-permute-start.12 = (bf16[4,128,512]{2,1,0:T(8,128)(2,1)S(1)}, bf16[4,128,512]{2,1,0:T(8,128)(2,1)S(1)}, u32[]{:S(2)}, u32[]{:S(2)}) collective-permute-start(bf16[4,128,512]{2,1,0:T(8,128)(2,1)S(1)} %pad_maximum_fusion.3), channel_id=1, source_target_pairs={{0,2},{1,3},{2,0},{3,1},{4,6},{5,7},{6,4},{7,5},{8,10},{9,11},{10,... | collective-permute-start | bytes 1572872 | tf_op jit(solution)/shard_map/ppermute | solution.py:24
  27.2 27.8 %collective-permute-start.13 = (bf16[4,128,512]{2,1,0:T(8,128)(2,1)S(1)}, bf16[4,128,512]{2,1,0:T(8,128)(2,1)S(1)}, u32[]{:S(2)}, u32[]{:S(2)}) collective-permute-start(bf16[4,128,512]{2,1,0:T(8,128)(2,1)S(1)} %pad_maximum_fusion.4), channel_id=1, source_target_pairs={{0,3},{1,2},{2,1},{3,0},{4,7},{5,6},{6,5},{7,4},{8,11},{9,10},{10,... | collective-permute-start | bytes 1572872 | tf_op jit(solution)/shard_map/ppermute | solution.py:24
  40.4 21.3 %collective-permute-start.14 = (bf16[2,128,512]{2,1,0:T(8,128)(2,1)S(1)}, bf16[2,128,512]{2,1,0:T(8,128)(2,1)S(1)}, u32[]{:S(2)}, u32[]{:S(2)}) collective-permute-start(bf16[2,128,512]{2,1,0:T(8,128)(2,1)S(1)} %get-tuple-element.53), channel_id=1, source_target_pairs={{0,2},{1,3},{2,0},{3,1},{4,6},{5,7},{6,4},{7,5},{8,10},{9,11},{10,... | collective-permute-start | bytes 786440 | tf_op jit(solution)/shard_map/ppermute | solution.py:24
  51.7 13.1 %collective-permute-start.16 = (bf16[2,128,512]{2,1,0:T(8,128)(2,1)S(1)}, bf16[2,128,512]{2,1,0:T(8,128)(2,1)S(1)}, u32[]{:S(2)}, u32[]{:S(2)}) collective-permute-start(bf16[2,128,512]{2,1,0:T(8,128)(2,1)S(1)} %get-tuple-element.56), channel_id=1, source_target_pairs={{0,3},{1,2},{2,1},{3,0},{4,7},{5,6},{6,5},{7,4},{8,11},{9,10},{10,... | collective-permute-start | bytes 786440 | tf_op jit(solution)/shard_map/ppermute | solution.py:24
  52.7 16.7 %collective-permute-start.25 = (bf16[2,128,512]{2,1,0:T(8,128)(2,1)S(1)}, bf16[2,128,512]{2,1,0:T(8,128)(2,1)S(1)}, u32[]{:S(2)}, u32[]{:S(2)}) collective-permute-start(bf16[2,128,512]{2,1,0:T(8,128)(2,1)S(1)} %get-tuple-element.75), channel_id=1, source_target_pairs={{0,2},{1,3},{2,0},{3,1},{4,6},{5,7},{6,4},{7,5},{8,10},{9,11},{10,... | collective-permute-start | bytes 786440 | tf_op jit(solution)/shard_map/ppermute | solution.py:24
  53.6 22.7 %collective-permute-start.27 = (bf16[2,128,512]{2,1,0:T(8,128)(2,1)S(1)}, bf16[2,128,512]{2,1,0:T(8,128)(2,1)S(1)}, u32[]{:S(2)}, u32[]{:S(2)}) collective-permute-start(bf16[2,128,512]{2,1,0:T(8,128)(2,1)S(1)} %get-tuple-element.74), channel_id=1, source_target_pairs={{0,3},{1,2},{2,1},{3,0},{4,7},{5,6},{6,5},{7,4},{8,11},{9,10},{10,... | collective-permute-start | bytes 786440 | tf_op jit(solution)/shard_map/ppermute | solution.py:24
  61.8 5.5 %collective-permute-start.15 = (f32[2,16,512]{2,1,0:T(8,128)S(1)}, f32[2,16,512]{2,1,0:T(8,128)S(1)}, u32[]{:S(2)}, u32[]{:S(2)}) collective-permute-start(f32[2,16,512]{2,1,0:T(8,128)S(1)} %slice_bitcast_fusion.17), channel_id=1, source_target_pairs={{0,16},{4,20},{8,24},{12,28},{16,0},{20,4},{24,8},{28,12},{1,17},{... | collective-permute-start | bytes 196616 | tf_op jit(solution)/shard_map/ppermute | solution.py:24
  64.7 14.6 %collective-permute-start.17 = (bf16[2,128,512]{2,1,0:T(8,128)(2,1)S(1)}, bf16[2,128,512]{2,1,0:T(8,128)(2,1)S(1)}, u32[]{:S(2)}, u32[]{:S(2)}) collective-permute-start(bf16[2,128,512]{2,1,0:T(8,128)(2,1)S(1)} %get-tuple-element.59), channel_id=1, source_target_pairs={{0,1},{1,0},{2,3},{3,2},{4,5},{5,4},{6,7},{7,6},{8,9},{9,8},{10,11... | collective-permute-start | bytes 786440 | tf_op jit(solution)/shard_map/ppermute | solution.py:24
  64.8 15.3 %collective-permute-start.18 = (bf16[2,128,512]{2,1,0:T(8,128)(2,1)S(1)}, bf16[2,128,512]{2,1,0:T(8,128)(2,1)S(1)}, u32[]{:S(2)}, u32[]{:S(2)}) collective-permute-start(bf16[2,128,512]{2,1,0:T(8,128)(2,1)S(1)} %get-tuple-element.60), channel_id=1, source_target_pairs={{0,2},{1,3},{2,0},{3,1},{4,6},{5,7},{6,4},{7,5},{8,10},{9,11},{10,... | collective-permute-start | bytes 786440 | tf_op jit(solution)/shard_map/ppermute | solution.py:24
  67.2 4.4 %collective-permute-start.24 = (f32[2,16,512]{2,1,0:T(8,128)S(1)}, f32[2,16,512]{2,1,0:T(8,128)S(1)}, u32[]{:S(2)}, u32[]{:S(2)}) collective-permute-start(f32[2,16,512]{2,1,0:T(8,128)S(1)} %fusion.27), channel_id=1, source_target_pairs={{0,8},{4,12},{8,0},{12,4},{16,24},{20,28},{24,16},{28,20},{1,9},{5... | collective-permute-start | bytes 196616 | tf_op jit(solution)/shard_map/ppermute | solution.py:24
  69.4 17.9 %collective-permute-start.19 = (bf16[2,128,512]{2,1,0:T(8,128)(2,1)S(1)}, bf16[2,128,512]{2,1,0:T(8,128)(2,1)S(1)}, u32[]{:S(2)}, u32[]{:S(2)}) collective-permute-start(bf16[2,128,512]{2,1,0:T(8,128)(2,1)S(1)} %get-tuple-element.61), channel_id=1, source_target_pairs={{0,3},{1,2},{2,1},{3,0},{4,7},{5,6},{6,5},{7,4},{8,11},{9,10},{10,... | collective-permute-start | bytes 786440 | tf_op jit(solution)/shard_map/ppermute | solution.py:24
  71.7 4.6 %collective-permute-start.26 = (f32[2,16,512]{2,1,0:T(8,128)S(1)}, f32[2,16,512]{2,1,0:T(8,128)S(1)}, u32[]{:S(2)}, u32[]{:S(2)}) collective-permute-start(f32[2,16,512]{2,1,0:T(8,128)S(1)} %bitcast_add_fusion.8), channel_id=1, source_target_pairs={{0,4},{4,0},{8,12},{12,8},{16,20},{20,16},{24,28},{28,24},{1,5},{5... | collective-permute-start | bytes 196616 | tf_op jit(solution)/shard_map/ppermute | solution.py:24
  76.7 10.7 %collective-permute-start.28 = (bf16[2,128,512]{2,1,0:T(8,128)(2,1)S(1)}, bf16[2,128,512]{2,1,0:T(8,128)(2,1)S(1)}, u32[]{:S(2)}, u32[]{:S(2)}) collective-permute-start(bf16[2,128,512]{2,1,0:T(8,128)(2,1)S(1)} %get-tuple-element.72), channel_id=1, source_target_pairs={{0,1},{1,0},{2,3},{3,2},{4,5},{5,4},{6,7},{7,6},{8,9},{9,8},{10,11... | collective-permute-start | bytes 786440 | tf_op jit(solution)/shard_map/ppermute | solution.py:24
  77.8 12.3 %collective-permute-start.31 = (bf16[1,128,512]{2,1,0:T(8,128)(2,1)S(1)}, bf16[1,128,512]{2,1,0:T(8,128)(2,1)S(1)}, u32[]{:S(2)}, u32[]{:S(2)}) collective-permute-start(bf16[1,128,512]{2,1,0:T(8,128)(2,1)S(1)} %get-tuple-element.110), channel_id=1, source_target_pairs={{0,3},{1,2},{2,1},{3,0},{4,7},{5,6},{6,5},{7,4},{8,11},{9,10},{10,... | collective-permute-start | bytes 393224 | tf_op jit(solution)/shard_map/ppermute | solution.py:24
  79.3 11.8 %collective-permute-start.32 = (bf16[1,128,512]{2,1,0:T(8,128)(2,1)}, bf16[1,128,512]{2,1,0:T(8,128)(2,1)S(1)}, u32[]{:S(2)}, u32[]{:S(2)}) collective-permute-start(bf16[1,128,512]{2,1,0:T(8,128)(2,1)} %get-tuple-element.108), channel_id=1, source_target_pairs={{0,2},{1,3},{2,0},{3,1},{4,6},{5,7},{6,4},{7,5},{8,10},{9,11},{10,... | collective-permute-start | bytes 393224 | tf_op jit(solution)/shard_map/ppermute | solution.py:24
  80.2 11.6 %collective-permute-start.29 = (bf16[1,128,512]{2,1,0:T(8,128)(2,1)}, bf16[1,128,512]{2,1,0:T(8,128)(2,1)S(1)}, u32[]{:S(2)}, u32[]{:S(2)}) collective-permute-start(bf16[1,128,512]{2,1,0:T(8,128)(2,1)} %get-tuple-element.109), channel_id=1, source_target_pairs={{0,2},{1,3},{2,0},{3,1},{4,6},{5,7},{6,4},{7,5},{8,10},{9,11},{10,... | collective-permute-start | bytes 393224 | tf_op jit(solution)/shard_map/ppermute | solution.py:24
  87.3 9.1 %collective-permute-start.30 = (bf16[1,128,512]{2,1,0:T(8,128)(2,1)}, bf16[1,128,512]{2,1,0:T(8,128)(2,1)S(1)}, u32[]{:S(2)}, u32[]{:S(2)}) collective-permute-start(bf16[1,128,512]{2,1,0:T(8,128)(2,1)} %get-tuple-element.111), channel_id=1, source_target_pairs={{0,3},{1,2},{2,1},{3,0},{4,7},{5,6},{6,5},{7,4},{8,11},{9,10},{10,... | collective-permute-start | bytes 393224 | tf_op jit(solution)/shard_map/ppermute | solution.py:24
  (17 other events, 66.0 us)

commit v8 on v6

--- a/solution.py
+++ b/solution.py
@@ -268,11 +268,11 @@
             if g < groups - 1:
                 place(2, landed["last", g, part], part, starts[g])
             else:
-                place(2, landed["last", g, part, 0], part, starts[g])
+                place(3, landed["last", g, part, 1], part, starts[g])
     for at, part in enumerate(far):
         if at == 1:
-            outs[3] = held(outs[3])
-        place(3, landed["last", groups - 1, part, 1], part, starts[-1])
+            outs[2] = held(outs[2])
+        place(2, landed["last", groups - 1, part, 0], part, starts[-1])
     return tuple(outs)
 
 

time: 97.2 us -> 97.8 us (level)
  local copies, waits for them, and re-layouts: 7.93 us -> 5.61 us
  waiting for transfers between devices: 23.9 us -> 26.1 us
    ppermute x33, waiting for transfers between devices: 23.9 us -> 26.1 us  [swapped(): return lax.ppermute(block, axis, [(i, i ^ mask) for i in range(count)])]
    dynamic_update_slice x20, local copies, waits for them, and re-layouts: 2.36 us -> 1.06 us  [place(): lax.dynamic_update_slice(outs[first + which], back[which], (0, column(par...]
    unnamed x16, local copies, waits for them, and re-layouts: 3.23 us -> 2.21 us
  transfers between devices with their start and end apart: 33 -> 33, of which waited for: 11 -> 12; matrix products, arithmetic and copies ran while one was open for 6% -> 5% of each run, Pallas kernels for 14% -> 14%
where the time goes in v8:
time: 97.8 us; the launch traced here: 97 us
  starting transfers between devices  47.6 us (49%)
  waiting for transfers between devices  26.1 us (27%)
  Pallas kernels  13.5 us (14%)
  local copies, waits for them, and re-layouts  5.61 us (6%)
  other arithmetic  3.01 us (3%)
  between operations  1.21 us (1%)
    ppermute x33, starting transfers between devices, swapped(): return lax.ppermute(block, axis, [(i, i ^ mask) for i in range(count)])  47.6 us
    ppermute x33, waiting for transfers between devices, swapped(): return lax.ppermute(block, axis, [(i, i ^ mask) for i in range(count)])  26.1 us
    pallas_call x2, Pallas kernels, attention(): pl.pallas_call(functools.partial(attention_kernel, layout, depth, pool_si...  13.5 us
    unnamed x16, local copies, waits for them, and re-layouts  2.21 us
  transfers between devices with their start and end apart: 33, of which 12 were waited for; matrix products, arithmetic and copies ran while one was open for 5% of the time, Pallas kernels for 14%

profile of v8, /device:TPU:1, one launch (start us, length us, event | category | flops | bytes accessed | tf_op | source)
XLA Modules:
  0.0 97.0 jit_solution(1817777668425168553)
XLA Ops:
  1.8 2.1 %collective-permute-start.4 = (bf16[2,128,512]{2,1,0:T(8,128)(2,1)S(1)}, bf16[2,128,512]{2,1,0:T(8,128)(2,1)S(1)}, u32[]{:S(2)}, u32[]{:S(2)}) collective-permute-start(bf16[2,128,512]{2,1,0:T(8,128)(2,1)S(1)} %bitcast.224), channel_id=1, source_target_pairs={{0,2},{1,3},{2,0},{3,1},{4,6},{5,7},{6,4},{7,5},{8,10},{9,11},{10,... | collective-permute-start | bytes 786440 | tf_op jit(solution)/shard_map/ppermute | solution.py:24
  7.6 1.5 %collective-permute-start.3 = (f32[2,4,1024]{2,1,0:T(4,128)S(1)}, f32[2,4,1024]{2,1,0:T(4,128)S(1)}, u32[]{:S(2)}, u32[]{:S(2)}) collective-permute-start(f32[2,4,1024]{2,1,0:T(4,128)S(1)} %get-tuple-element.143), channel_id=1, source_target_pairs={{0,3},{1,2},{2,1},{3,0},{4,7},{5,6},{6,5},{7,4},{8,11},{9,10},{10,... | collective-permute-start | bytes 98312 | tf_op jit(solution)/shard_map/ppermute | solution.py:24
  11.9 1.6 %collective-permute-start.7 = (f32[2,16,1024]{2,1,0:T(8,128)S(1)}, f32[2,16,1024]{2,1,0:T(8,128)S(1)}, u32[]{:S(2)}, u32[]{:S(2)}) collective-permute-start(f32[2,16,1024]{2,1,0:T(8,128)S(1)} %pad_maximum_fusion.9), channel_id=1, source_target_pairs={{0,4},{4,0},{8,12},{12,8},{16,20},{20,16},{24,28},{28,24},{1,5},{5... | collective-permute-start | bytes 393224 | tf_op jit(solution)/shard_map/ppermute | solution.py:24
  13.6 2.8 %collective-permute-start = (bf16[4,128,512]{2,1,0:T(8,128)(2,1)S(1)}, bf16[4,128,512]{2,1,0:T(8,128)(2,1)S(1)}, u32[]{:S(2)}, u32[]{:S(2)}) collective-permute-start(bf16[4,128,512]{2,1,0:T(8,128)(2,1)S(1)} %pad_maximum_fusion.1), channel_id=1, source_target_pairs={{0,1},{1,0},{2,3},{3,2},{4,5},{5,4},{6,7},{7,6},{8,9},{9,8},{10,11... | collective-permute-start | bytes 1572872 | tf_op jit(solution)/shard_map/ppermute | solution.py:24
  16.4 1.4 %collective-permute-start.8 = (f32[2,16,1024]{2,1,0:T(8,128)S(1)}, f32[2,16,1024]{2,1,0:T(8,128)S(1)}, u32[]{:S(2)}, u32[]{:S(2)}) collective-permute-start(f32[2,16,1024]{2,1,0:T(8,128)S(1)} %get-tuple-element.139), channel_id=1, source_target_pairs={{0,8},{4,12},{8,0},{12,4},{16,24},{20,28},{24,16},{28,20},{1,9},{5... | collective-permute-start | bytes 393224 | tf_op jit(solution)/shard_map/ppermute | solution.py:24
  17.9 2.7 %collective-permute-done.8 = f32[2,16,1024]{2,1,0:T(8,128)S(1)} collective-permute-done((f32[2,16,1024]{2,1,0:T(8,128)S(1)}, f32[2,16,1024]{2,1,0:T(8,128)S(1)}, u32[]{:S(2)}, u32[]{:S(2)}) %collective-permute-start.8) | collective-permute-done | bytes 131104 | tf_op jit(solution)/shard_map/ppermute | solution.py:24
  20.6 2.4 %collective-permute-start.10 = (bf16[2,16,1024]{2,1,0:T(8,128)(2,1)S(1)}, bf16[2,16,1024]{2,1,0:T(8,128)(2,1)S(1)}, u32[]{:S(2)}, u32[]{:S(2)}) collective-permute-start(bf16[2,16,1024]{2,1,0:T(8,128)(2,1)S(1)} %add_multiply_fusion), channel_id=1, source_target_pairs={{0,16},{4,20},{8,24},{12,28},{16,0},{20,4},{24,8},{28,12},{1,17},{... | collective-permute-start | bytes 196616 | tf_op jit(solution)/shard_map/ppermute | solution.py:24
  23.1 4.1 %collective-permute-start.12 = (bf16[4,128,512]{2,1,0:T(8,128)(2,1)S(1)}, bf16[4,128,512]{2,1,0:T(8,128)(2,1)S(1)}, u32[]{:S(2)}, u32[]{:S(2)}) collective-permute-start(bf16[4,128,512]{2,1,0:T(8,128)(2,1)S(1)} %pad_maximum_fusion.3), channel_id=1, source_target_pairs={{0,2},{1,3},{2,0},{3,1},{4,6},{5,7},{6,4},{7,5},{8,10},{9,11},{10,... | collective-permute-start | bytes 1572872 | tf_op jit(solution)/shard_map/ppermute | solution.py:24
  27.2 4.1 %collective-permute-start.13 = (bf16[4,128,512]{2,1,0:T(8,128)(2,1)S(1)}, bf16[4,128,512]{2,1,0:T(8,128)(2,1)S(1)}, u32[]{:S(2)}, u32[]{:S(2)}) collective-permute-start(bf16[4,128,512]{2,1,0:T(8,128)(2,1)S(1)} %pad_maximum_fusion.4), channel_id=1, source_target_pairs={{0,3},{1,2},{2,1},{3,0},{4,7},{5,6},{6,5},{7,4},{8,11},{9,10},{10,... | collective-permute-start | bytes 1572872 | tf_op jit(solution)/shard_map/ppermute | solution.py:24
  31.3 6.7 %attention.2 = (bf16[2,128,512]{2,1,0:T(8,128)(2,1)S(1)}, bf16[2,128,512]{2,1,0:T(8,128)(2,1)S(1)}, bf16[2,128,512]{2,1,0:T(8,128)(2,1)S(1)}, bf16[2,128,512]{2,...) custom-call(bf16[4,128,512]{2,1,0:T(8,128)(2,1)S(1)} %pad_maximum_fusion.refs_0_, ...), custom_call_target="tpu_custom_call" | custom-call | flops 1761607680 | bytes 6291456 | tf_op jit(solution)/shard_map/attention/pallas_call | solution.py:90
  38.1 2.3 %collective-permute-start.20 = (bf16[2,16,512]{2,1,0:T(8,128)(2,1)S(1)}, bf16[2,16,512]{2,1,0:T(8,128)(2,1)S(1)}, u32[]{:S(2)}, u32[]{:S(2)}) collective-permute-start(bf16[2,16,512]{2,1,0:T(8,128)(2,1)S(1)} %fusion.28), channel_id=1, source_target_pairs={{0,16},{4,20},{8,24},{12,28},{16,0},{20,4},{24,8},{28,12},{1,17},{... | collective-permute-start | bytes 98312 | tf_op jit(solution)/shard_map/ppermute | solution.py:24
  41.8 1.8 %collective-permute-start.21 = (f32[2,16,512]{2,1,0:T(8,128)S(1)}, f32[2,16,512]{2,1,0:T(8,128)S(1)}, u32[]{:S(2)}, u32[]{:S(2)}) collective-permute-start(f32[2,16,512]{2,1,0:T(8,128)S(1)} %fusion.26), channel_id=1, source_target_pairs={{0,8},{4,12},{8,0},{12,4},{16,24},{20,28},{24,16},{28,20},{1,9},{5... | collective-permute-start | bytes 196616 | tf_op jit(solution)/shard_map/ppermute | solution.py:24
  43.8 2.1 %collective-permute-done.21 = f32[2,16,512]{2,1,0:T(8,128)S(1)} collective-permute-done((f32[2,16,512]{2,1,0:T(8,128)S(1)}, f32[2,16,512]{2,1,0:T(8,128)S(1)}, u32[]{:S(2)}, u32[]{:S(2)}) %collective-permute-start.21) | collective-permute-done | bytes 65568 | tf_op jit(solution)/shard_map/ppermute | solution.py:24
  49.7 1.7 %collective-permute-start.23 = (bf16[2,128,512]{2,1,0:T(8,128)(2,1)S(1)}, bf16[2,128,512]{2,1,0:T(8,128)(2,1)S(1)}, u32[]{:S(2)}, u32[]{:S(2)}) collective-permute-start(bf16[2,128,512]{2,1,0:T(8,128)(2,1)S(1)} %get-tuple-element.76), channel_id=1, source_target_pairs={{0,1},{1,0},{2,3},{3,2},{4,5},{5,4},{6,7},{7,6},{8,9},{9,8},{10,11... | collective-permute-start | bytes 786440 | tf_op jit(solution)/shard_map/ppermute | solution.py:24
  53.6 1.4 %collective-permute-start.27 = (bf16[2,128,512]{2,1,0:T(8,128)(2,1)S(1)}, bf16[2,128,512]{2,1,0:T(8,128)(2,1)S(1)}, u32[]{:S(2)}, u32[]{:S(2)}) collective-permute-start(bf16[2,128,512]{2,1,0:T(8,128)(2,1)S(1)} %get-tuple-element.74), channel_id=1, source_target_pairs={{0,3},{1,2},{2,1},{3,0},{4,7},{5,6},{6,5},{7,4},{8,11},{9,10},{10,... | collective-permute-start | bytes 786440 | tf_op jit(solution)/shard_map/ppermute | solution.py:24
  55.0 6.7 %attention.3 = (bf16[2,128,512]{2,1,0:T(8,128)(2,1)S(1)}, bf16[2,128,512]{2,1,0:T(8,128)(2,1)S(1)}, bf16[2,128,512]{2,1,0:T(8,128)(2,1)S(1)}, bf16[2,128,512]{2,...) custom-call(bf16[4,128,512]{2,1,0:T(8,128)(2,1)S(1)} %pad_maximum_fusion.6.refs_0_, ...), custom_call_target="tpu_custom_call" | custom-call | flops 1761607680 | bytes 6291456 | tf_op jit(solution)/shard_map/attention/pallas_call | solution.py:90
  61.8 3.0 %collective-permute-start.15 = (f32[2,16,512]{2,1,0:T(8,128)S(1)}, f32[2,16,512]{2,1,0:T(8,128)S(1)}, u32[]{:S(2)}, u32[]{:S(2)}) collective-permute-start(f32[2,16,512]{2,1,0:T(8,128)S(1)} %slice_bitcast_fusion.17), channel_id=1, source_target_pairs={{0,16},{4,20},{8,24},{12,28},{16,0},{20,4},{24,8},{28,12},{1,17},{... | collective-permute-start | bytes 196616 | tf_op jit(solution)/shard_map/ppermute | solution.py:24
  65.7 1.5 %collective-permute-done.15 = f32[2,16,512]{2,1,0:T(8,128)S(1)} collective-permute-done((f32[2,16,512]{2,1,0:T(8,128)S(1)}, f32[2,16,512]{2,1,0:T(8,128)S(1)}, u32[]{:S(2)}, u32[]{:S(2)}) %collective-permute-start.15) | collective-permute-done | bytes 65568 | tf_op jit(solution)/shard_map/ppermute | solution.py:24
  67.3 2.1 %collective-permute-start.24 = (f32[2,16,512]{2,1,0:T(8,128)S(1)}, f32[2,16,512]{2,1,0:T(8,128)S(1)}, u32[]{:S(2)}, u32[]{:S(2)}) collective-permute-start(f32[2,16,512]{2,1,0:T(8,128)S(1)} %fusion.27), channel_id=1, source_target_pairs={{0,8},{4,12},{8,0},{12,4},{16,24},{20,28},{24,16},{28,20},{1,9},{5... | collective-permute-start | bytes 196616 | tf_op jit(solution)/shard_map/ppermute | solution.py:24
  69.4 2.3 %collective-permute-start.19 = (bf16[2,128,512]{2,1,0:T(8,128)(2,1)S(1)}, bf16[2,128,512]{2,1,0:T(8,128)(2,1)S(1)}, u32[]{:S(2)}, u32[]{:S(2)}) collective-permute-start(bf16[2,128,512]{2,1,0:T(8,128)(2,1)S(1)} %get-tuple-element.61), channel_id=1, source_target_pairs={{0,3},{1,2},{2,1},{3,0},{4,7},{5,6},{6,5},{7,4},{8,11},{9,10},{10,... | collective-permute-start | bytes 786440 | tf_op jit(solution)/shard_map/ppermute | solution.py:24
  73.1 3.2 %collective-permute-done.27 = bf16[2,128,512]{2,1,0:T(8,128)(2,1)S(1)} collective-permute-done((bf16[2,128,512]{2,1,0:T(8,128)(2,1)S(1)}, bf16[2,128,512]{2,1,0:T(8,128)(2,1)S(1)}, u32[]{:S(2)}, u32[]{:S(2)}) %collective-permute-start.27) | collective-permute-done | bytes 262176 | tf_op jit(solution)/shard_map/ppermute | solution.py:24
  81.3 6.3 %collective-permute-done.19 = bf16[2,128,512]{2,1,0:T(8,128)(2,1)S(1)} collective-permute-done((bf16[2,128,512]{2,1,0:T(8,128)(2,1)S(1)}, bf16[2,128,512]{2,1,0:T(8,128)(2,1)S(1)}, u32[]{:S(2)}, u32[]{:S(2)}) %collective-permute-start.19) | collective-permute-done | bytes 262176 | tf_op jit(solution)/shard_map/ppermute | solution.py:24
  87.7 3.6 %collective-permute-done.29 = bf16[1,128,512]{2,1,0:T(8,128)(2,1)S(1)} collective-permute-done((bf16[1,128,512]{2,1,0:T(8,128)(2,1)S(1)}, bf16[1,128,512]{2,1,0:T(8,128)(2,1)S(1)}, u32[]{:S(2)}, u32[]{:S(2)}) %collective-permute-start.29) | collective-permute-done | bytes 131104 | tf_op jit(solution)/shard_map/ppermute | solution.py:24
  93.3 3.1 %collective-permute-done.30 = bf16[1,128,512]{2,1,0:T(8,128)(2,1)S(1)} collective-permute-done((bf16[1,128,512]{2,1,0:T(8,128)(2,1)}, bf16[1,128,512]{2,1,0:T(8,128)(2,1)S(1)}, u32[]{:S(2)}, u32[]{:S(2)}) %collective-permute-start.30) | collective-permute-done | bytes 131104 | tf_op jit(solution)/shard_map/ppermute | solution.py:24
  (121 shorter events, 25.2 us)
Async XLA Ops:
  1.8 10.1 %collective-permute-start.4 = (bf16[2,128,512]{2,1,0:T(8,128)(2,1)S(1)}, bf16[2,128,512]{2,1,0:T(8,128)(2,1)S(1)}, u32[]{:S(2)}, u32[]{:S(2)}) collective-permute-start(bf16[2,128,512]{2,1,0:T(8,128)(2,1)S(1)} %bitcast.224), channel_id=1, source_target_pairs={{0,2},{1,3},{2,0},{3,1},{4,6},{5,7},{6,4},{7,5},{8,10},{9,11},{10,... | collective-permute-start | bytes 786440 | tf_op jit(solution)/shard_map/ppermute | solution.py:24
  9.2 11.4 %collective-permute-start.9 = (bf16[4,128,512]{2,1,0:T(8,128)(2,1)S(1)}, bf16[4,128,512]{2,1,0:T(8,128)(2,1)S(1)}, u32[]{:S(2)}, u32[]{:S(2)}) collective-permute-start(bf16[4,128,512]{2,1,0:T(8,128)(2,1)S(1)} %pad_maximum_fusion.5), channel_id=1, source_target_pairs={{0,1},{1,0},{2,3},{3,2},{4,5},{5,4},{6,7},{7,6},{8,9},{9,8},{10,11... | collective-permute-start | bytes 1572872 | tf_op jit(solution)/shard_map/ppermute | solution.py:24
  9.4 21.9 %collective-permute-start.6 = (bf16[4,128,512]{2,1,0:T(8,128)(2,1)S(1)}, bf16[4,128,512]{2,1,0:T(8,128)(2,1)S(1)}, u32[]{:S(2)}, u32[]{:S(2)}) collective-permute-start(bf16[4,128,512]{2,1,0:T(8,128)(2,1)S(1)} %pad_maximum_fusion.2), channel_id=1, source_target_pairs={{0,3},{1,2},{2,1},{3,0},{4,7},{5,6},{6,5},{7,4},{8,11},{9,10},{10,... | collective-permute-start | bytes 1572872 | tf_op jit(solution)/shard_map/ppermute | solution.py:24
  10.9 20.4 %collective-permute-start.5 = (bf16[2,128,512]{2,1,0:T(8,128)(2,1)S(1)}, bf16[2,128,512]{2,1,0:T(8,128)(2,1)S(1)}, u32[]{:S(2)}, u32[]{:S(2)}) collective-permute-start(bf16[2,128,512]{2,1,0:T(8,128)(2,1)S(1)} %pad_maximum_fusion.7), channel_id=1, source_target_pairs={{0,2},{1,3},{2,0},{3,1},{4,6},{5,7},{6,4},{7,5},{8,10},{9,11},{10,... | collective-permute-start | bytes 786440 | tf_op jit(solution)/shard_map/ppermute | solution.py:24
  11.9 4.5 %collective-permute-start.7 = (f32[2,16,1024]{2,1,0:T(8,128)S(1)}, f32[2,16,1024]{2,1,0:T(8,128)S(1)}, u32[]{:S(2)}, u32[]{:S(2)}) collective-permute-start(f32[2,16,1024]{2,1,0:T(8,128)S(1)} %pad_maximum_fusion.9), channel_id=1, source_target_pairs={{0,4},{4,0},{8,12},{12,8},{16,20},{20,16},{24,28},{28,24},{1,5},{5... | collective-permute-start | bytes 393224 | tf_op jit(solution)/shard_map/ppermute | solution.py:24
  13.6 17.8 %collective-permute-start = (bf16[4,128,512]{2,1,0:T(8,128)(2,1)S(1)}, bf16[4,128,512]{2,1,0:T(8,128)(2,1)S(1)}, u32[]{:S(2)}, u32[]{:S(2)}) collective-permute-start(bf16[4,128,512]{2,1,0:T(8,128)(2,1)S(1)} %pad_maximum_fusion.1), channel_id=1, source_target_pairs={{0,1},{1,0},{2,3},{3,2},{4,5},{5,4},{6,7},{7,6},{8,9},{9,8},{10,11... | collective-permute-start | bytes 1572872 | tf_op jit(solution)/shard_map/ppermute | solution.py:24
  20.6 6.5 %collective-permute-start.10 = (bf16[2,16,1024]{2,1,0:T(8,128)(2,1)S(1)}, bf16[2,16,1024]{2,1,0:T(8,128)(2,1)S(1)}, u32[]{:S(2)}, u32[]{:S(2)}) collective-permute-start(bf16[2,16,1024]{2,1,0:T(8,128)(2,1)S(1)} %add_multiply_fusion), channel_id=1, source_target_pairs={{0,16},{4,20},{8,24},{12,28},{16,0},{20,4},{24,8},{28,12},{1,17},{... | collective-permute-start | bytes 196616 | tf_op jit(solution)/shard_map/ppermute | solution.py:24
  23.1 30.5 %collective-permute-start.12 = (bf16[4,128,512]{2,1,0:T(8,128)(2,1)S(1)}, bf16[4,128,512]{2,1,0:T(8,128)(2,1)S(1)}, u32[]{:S(2)}, u32[]{:S(2)}) collective-permute-start(bf16[4,128,512]{2,1,0:T(8,128)(2,1)S(1)} %pad_maximum_fusion.3), channel_id=1, source_target_pairs={{0,2},{1,3},{2,0},{3,1},{4,6},{5,7},{6,4},{7,5},{8,10},{9,11},{10,... | collective-permute-start | bytes 1572872 | tf_op jit(solution)/shard_map/ppermute | solution.py:24
  27.2 27.8 %collective-permute-start.13 = (bf16[4,128,512]{2,1,0:T(8,128)(2,1)S(1)}, bf16[4,128,512]{2,1,0:T(8,128)(2,1)S(1)}, u32[]{:S(2)}, u32[]{:S(2)}) collective-permute-start(bf16[4,128,512]{2,1,0:T(8,128)(2,1)S(1)} %pad_maximum_fusion.4), channel_id=1, source_target_pairs={{0,3},{1,2},{2,1},{3,0},{4,7},{5,6},{6,5},{7,4},{8,11},{9,10},{10,... | collective-permute-start | bytes 1572872 | tf_op jit(solution)/shard_map/ppermute | solution.py:24
  40.4 21.3 %collective-permute-start.14 = (bf16[2,128,512]{2,1,0:T(8,128)(2,1)S(1)}, bf16[2,128,512]{2,1,0:T(8,128)(2,1)S(1)}, u32[]{:S(2)}, u32[]{:S(2)}) collective-permute-start(bf16[2,128,512]{2,1,0:T(8,128)(2,1)S(1)} %get-tuple-element.53), channel_id=1, source_target_pairs={{0,2},{1,3},{2,0},{3,1},{4,6},{5,7},{6,4},{7,5},{8,10},{9,11},{10,... | collective-permute-start | bytes 786440 | tf_op jit(solution)/shard_map/ppermute | solution.py:24
  51.7 13.1 %collective-permute-start.16 = (bf16[2,128,512]{2,1,0:T(8,128)(2,1)S(1)}, bf16[2,128,512]{2,1,0:T(8,128)(2,1)S(1)}, u32[]{:S(2)}, u32[]{:S(2)}) collective-permute-start(bf16[2,128,512]{2,1,0:T(8,128)(2,1)S(1)} %get-tuple-element.56), channel_id=1, source_target_pairs={{0,3},{1,2},{2,1},{3,0},{4,7},{5,6},{6,5},{7,4},{8,11},{9,10},{10,... | collective-permute-start | bytes 786440 | tf_op jit(solution)/shard_map/ppermute | solution.py:24
  52.7 16.7 %collective-permute-start.25 = (bf16[2,128,512]{2,1,0:T(8,128)(2,1)S(1)}, bf16[2,128,512]{2,1,0:T(8,128)(2,1)S(1)}, u32[]{:S(2)}, u32[]{:S(2)}) collective-permute-start(bf16[2,128,512]{2,1,0:T(8,128)(2,1)S(1)} %get-tuple-element.75), channel_id=1, source_target_pairs={{0,2},{1,3},{2,0},{3,1},{4,6},{5,7},{6,4},{7,5},{8,10},{9,11},{10,... | collective-permute-start | bytes 786440 | tf_op jit(solution)/shard_map/ppermute | solution.py:24
  53.6 22.7 %collective-permute-start.27 = (bf16[2,128,512]{2,1,0:T(8,128)(2,1)S(1)}, bf16[2,128,512]{2,1,0:T(8,128)(2,1)S(1)}, u32[]{:S(2)}, u32[]{:S(2)}) collective-permute-start(bf16[2,128,512]{2,1,0:T(8,128)(2,1)S(1)} %get-tuple-element.74), channel_id=1, source_target_pairs={{0,3},{1,2},{2,1},{3,0},{4,7},{5,6},{6,5},{7,4},{8,11},{9,10},{10,... | collective-permute-start | bytes 786440 | tf_op jit(solution)/shard_map/ppermute | solution.py:24
  61.8 5.5 %collective-permute-start.15 = (f32[2,16,512]{2,1,0:T(8,128)S(1)}, f32[2,16,512]{2,1,0:T(8,128)S(1)}, u32[]{:S(2)}, u32[]{:S(2)}) collective-permute-start(f32[2,16,512]{2,1,0:T(8,128)S(1)} %slice_bitcast_fusion.17), channel_id=1, source_target_pairs={{0,16},{4,20},{8,24},{12,28},{16,0},{20,4},{24,8},{28,12},{1,17},{... | collective-permute-start | bytes 196616 | tf_op jit(solution)/shard_map/ppermute | solution.py:24
  64.7 14.5 %collective-permute-start.17 = (bf16[2,128,512]{2,1,0:T(8,128)(2,1)S(1)}, bf16[2,128,512]{2,1,0:T(8,128)(2,1)S(1)}, u32[]{:S(2)}, u32[]{:S(2)}) collective-permute-start(bf16[2,128,512]{2,1,0:T(8,128)(2,1)S(1)} %get-tuple-element.59), channel_id=1, source_target_pairs={{0,1},{1,0},{2,3},{3,2},{4,5},{5,4},{6,7},{7,6},{8,9},{9,8},{10,11... | collective-permute-start | bytes 786440 | tf_op jit(solution)/shard_map/ppermute | solution.py:24
  64.8 15.6 %collective-permute-start.18 = (bf16[2,128,512]{2,1,0:T(8,128)(2,1)S(1)}, bf16[2,128,512]{2,1,0:T(8,128)(2,1)S(1)}, u32[]{:S(2)}, u32[]{:S(2)}) collective-permute-start(bf16[2,128,512]{2,1,0:T(8,128)(2,1)S(1)} %get-tuple-element.60), channel_id=1, source_target_pairs={{0,2},{1,3},{2,0},{3,1},{4,6},{5,7},{6,4},{7,5},{8,10},{9,11},{10,... | collective-permute-start | bytes 786440 | tf_op jit(solution)/shard_map/ppermute | solution.py:24
  67.3 4.4 %collective-permute-start.24 = (f32[2,16,512]{2,1,0:T(8,128)S(1)}, f32[2,16,512]{2,1,0:T(8,128)S(1)}, u32[]{:S(2)}, u32[]{:S(2)}) collective-permute-start(f32[2,16,512]{2,1,0:T(8,128)S(1)} %fusion.27), channel_id=1, source_target_pairs={{0,8},{4,12},{8,0},{12,4},{16,24},{20,28},{24,16},{28,20},{1,9},{5... | collective-permute-start | bytes 196616 | tf_op jit(solution)/shard_map/ppermute | solution.py:24
  69.4 18.2 %collective-permute-start.19 = (bf16[2,128,512]{2,1,0:T(8,128)(2,1)S(1)}, bf16[2,128,512]{2,1,0:T(8,128)(2,1)S(1)}, u32[]{:S(2)}, u32[]{:S(2)}) collective-permute-start(bf16[2,128,512]{2,1,0:T(8,128)(2,1)S(1)} %get-tuple-element.61), channel_id=1, source_target_pairs={{0,3},{1,2},{2,1},{3,0},{4,7},{5,6},{6,5},{7,4},{8,11},{9,10},{10,... | collective-permute-start | bytes 786440 | tf_op jit(solution)/shard_map/ppermute | solution.py:24
  71.7 4.6 %collective-permute-start.26 = (f32[2,16,512]{2,1,0:T(8,128)S(1)}, f32[2,16,512]{2,1,0:T(8,128)S(1)}, u32[]{:S(2)}, u32[]{:S(2)}) collective-permute-start(f32[2,16,512]{2,1,0:T(8,128)S(1)} %bitcast_add_fusion.8), channel_id=1, source_target_pairs={{0,4},{4,0},{8,12},{12,8},{16,20},{20,16},{24,28},{28,24},{1,5},{5... | collective-permute-start | bytes 196616 | tf_op jit(solution)/shard_map/ppermute | solution.py:24
  76.7 11.0 %collective-permute-start.28 = (bf16[2,128,512]{2,1,0:T(8,128)(2,1)S(1)}, bf16[2,128,512]{2,1,0:T(8,128)(2,1)S(1)}, u32[]{:S(2)}, u32[]{:S(2)}) collective-permute-start(bf16[2,128,512]{2,1,0:T(8,128)(2,1)S(1)} %get-tuple-element.72), channel_id=1, source_target_pairs={{0,1},{1,0},{2,3},{3,2},{4,5},{5,4},{6,7},{7,6},{8,9},{9,8},{10,11... | collective-permute-start | bytes 786440 | tf_op jit(solution)/shard_map/ppermute | solution.py:24
  77.8 14.6 %collective-permute-start.31 = (bf16[1,128,512]{2,1,0:T(8,128)(2,1)}, bf16[1,128,512]{2,1,0:T(8,128)(2,1)S(1)}, u32[]{:S(2)}, u32[]{:S(2)}) collective-permute-start(bf16[1,128,512]{2,1,0:T(8,128)(2,1)} %get-tuple-element.110), channel_id=1, source_target_pairs={{0,2},{1,3},{2,0},{3,1},{4,6},{5,7},{6,4},{7,5},{8,10},{9,11},{10,... | collective-permute-start | bytes 393224 | tf_op jit(solution)/shard_map/ppermute | solution.py:24
  79.3 13.9 %collective-permute-start.32 = (bf16[1,128,512]{2,1,0:T(8,128)(2,1)}, bf16[1,128,512]{2,1,0:T(8,128)(2,1)S(1)}, u32[]{:S(2)}, u32[]{:S(2)}) collective-permute-start(bf16[1,128,512]{2,1,0:T(8,128)(2,1)} %get-tuple-element.108), channel_id=1, source_target_pairs={{0,3},{1,2},{2,1},{3,0},{4,7},{5,6},{6,5},{7,4},{8,11},{9,10},{10,... | collective-permute-start | bytes 393224 | tf_op jit(solution)/shard_map/ppermute | solution.py:24
  80.5 10.9 %collective-permute-start.29 = (bf16[1,128,512]{2,1,0:T(8,128)(2,1)S(1)}, bf16[1,128,512]{2,1,0:T(8,128)(2,1)S(1)}, u32[]{:S(2)}, u32[]{:S(2)}) collective-permute-start(bf16[1,128,512]{2,1,0:T(8,128)(2,1)S(1)} %get-tuple-element.111), channel_id=1, source_target_pairs={{0,2},{1,3},{2,0},{3,1},{4,6},{5,7},{6,4},{7,5},{8,10},{9,11},{10,... | collective-permute-start | bytes 393224 | tf_op jit(solution)/shard_map/ppermute | solution.py:24
  87.6 8.7 %collective-permute-start.30 = (bf16[1,128,512]{2,1,0:T(8,128)(2,1)}, bf16[1,128,512]{2,1,0:T(8,128)(2,1)S(1)}, u32[]{:S(2)}, u32[]{:S(2)}) collective-permute-start(bf16[1,128,512]{2,1,0:T(8,128)(2,1)} %get-tuple-element.109), channel_id=1, source_target_pairs={{0,3},{1,2},{2,1},{3,0},{4,7},{5,6},{6,5},{7,4},{8,11},{9,10},{10,... | collective-permute-start | bytes 393224 | tf_op jit(solution)/shard_map/ppermute | solution.py:24
  (17 other events, 60.8 us)
